TPU v7x, 256 devices: a whole 4x4x8 slice. The times are simulated.
256 devices in a mesh: dp: 32 (over x, y, core), vocab: 8 (over z).
Axes of the slice: x: 4, y: 4, z: 8, core: 2. Of those that a mesh axis runs over, the one named last changes fastest.
Arguments:
- student_hidden: bfloat16 [512, 4096], P('dp'), may hold values from -18 to 18
- teacher_hidden: bfloat16 [512, 4096], P('dp'), may hold values from -18 to 18
- student_head: bfloat16 [4096, 98304], P('dp', 'vocab'), may hold values from -0.75 to 0.75
- teacher_head: bfloat16 [4096, 98304], P('vocab', 'dp'), may hold values from -0.75 to 0.75
- sampled_ids: int32 [512], P('dp'), may hold values from 0 to 98303
Outputs:
- grad_hidden: bfloat16 [512, 4096], P('dp')
- token_loss: float32 [512], P('dp')
All inputs are finite; a program needn't handle non-finite values.
Results may differ from a plain program's by a relative error of at most 0.0052.
Values may be sent and summed in bfloat16 or wider, within the bound.
No kernel may reach another device: no remote copies, remote signals or barrier semaphores. Data moves between devices by JAX's collectives and lax.ppermute only.
A program may use at most 64 MiB of HBM per device.

v0:
```python
import jax
import jax.numpy as jnp
from jax import lax
from jax.sharding import PartitionSpec as P

ce_weight = 0.5


def local(student_hidden, teacher_hidden, student_head, teacher_head, sampled_ids):
    dp_count = lax.axis_size("dp")
    vocab_count = lax.axis_size("vocab")
    row_part = student_head.shape[0]
    col_count = student_head.shape[1] // dp_count
    spread_in = student_head.reshape(row_part, dp_count // vocab_count, vocab_count, col_count)
    routed = lax.all_to_all(
        lax.all_to_all(spread_in, "vocab", split_axis=2, concat_axis=1, tiled=True),
        "dp",
        split_axis=1,
        concat_axis=0,
        tiled=True,
    )
    student_cols = routed.reshape(-1, col_count)
    teacher_parts = teacher_head.reshape(teacher_head.shape[0], vocab_count, col_count)
    teacher_cols = lax.all_to_all(
        teacher_parts, "vocab", split_axis=1, concat_axis=0, tiled=True
    ).reshape(-1, col_count)
    first_col = (lax.axis_index("dp") * vocab_count + lax.axis_index("vocab")) * col_count
    stacked = jnp.stack([student_hidden, teacher_hidden])
    piece = lax.all_gather(stacked, "dp", axis=1, tiled=True)
    student_part = jnp.dot(piece[0], student_cols, preferred_element_type=jnp.float32)
    teacher_part = jnp.dot(piece[1], teacher_cols, preferred_element_type=jnp.float32)
    both_logits = jnp.concatenate([student_part, teacher_part], axis=1)
    student_logits = both_logits[:, :col_count]
    teacher_logits = both_logits[:, col_count:]
    all_ids = lax.all_gather(sampled_ids, "dp", axis=0, tiled=True)
    column_ids = first_col + jnp.arange(col_count, dtype=jnp.int32)
    hit_mask = (column_ids[None, :] == all_ids[:, None]).astype(jnp.float32)
    picked_local = jnp.sum(hit_mask * student_logits, axis=1)
    student_local_top = jnp.max(student_logits, axis=1)
    teacher_local_top = jnp.max(teacher_logits, axis=1)
    logit_gap = student_logits - teacher_logits
    student_top, teacher_top = lax.pmax((student_local_top, teacher_local_top), ("dp", "vocab"))
    student_exp = jnp.exp(student_logits - student_top[:, None])
    teacher_exp = jnp.exp(teacher_logits - teacher_top[:, None])
    student_total, teacher_total, cross_total, picked = lax.psum(
        (
            jnp.sum(student_exp, axis=1),
            jnp.sum(teacher_exp, axis=1),
            jnp.sum(student_exp * logit_gap, axis=1),
            picked_local,
        ),
        ("dp", "vocab"),
    )
    student_norm = student_top + jnp.log(student_total)
    teacher_norm = teacher_top + jnp.log(teacher_total)
    divergence = cross_total / student_total - student_norm + teacher_norm
    student_logprob = student_logits - student_norm[:, None]
    teacher_logprob = teacher_logits - teacher_norm[:, None]
    student_prob = jnp.exp(student_logprob)
    logit_grad = (
        student_prob * (student_logprob - teacher_logprob - divergence[:, None])
        + ce_weight * (student_prob - hit_mask)
    ).astype(jnp.bfloat16)
    tok_count = student_hidden.shape[0]
    own_start = lax.axis_index("dp") * tok_count
    every_loss = divergence + ce_weight * (student_norm - picked)
    token_loss = lax.dynamic_slice_in_dim(every_loss, own_start, tok_count, 0)
    partial_sum = lax.psum_scatter(
        lax.dot_general(
            logit_grad, student_cols, (((1,), (1,)), ((), ())), preferred_element_type=jnp.float32
        ),
        "dp",
        scatter_dimension=0,
        tiled=True,
    )
    grad_hidden = lax.psum(partial_sum, "vocab").astype(jnp.bfloat16)
    return (grad_hidden, token_loss)


def solution(mesh):
    in_specs = (P("dp", None), P("dp", None), P("dp", "vocab"), P("vocab", "dp"), P("dp"))
    out_specs = (P("dp", None), P("dp"))
    return jax.shard_map(local, mesh=mesh, in_specs=in_specs, out_specs=out_specs, check_vma=False)
```

profile of v0, /device:TPU:8, one launch (start us, length us, event | category | flops | bytes accessed | tf_op | source)
XLA Modules:
  0.0 540.2 jit_solution(14175300822139963729)
XLA Ops:
  7.2 0.0 all-gather.2.cloned.1.call-start
  7.2 1.7 pad_maximum_fusion
  8.9 0.0 all-gather.2.cloned.1.call-update
  8.9 3.5 copy.15
  12.4 2.0 copy.16
  14.4 8.5 %all-to-all-start = ((bf16[128,4,8,384]{0,3,1,2:T(8,128)(2,1)}), bf16[128,4,8,384]{0,3,1,2:T(8,128)(2,1)S(1)}, u32[]{:S(2)}, u32[]{:S(2)}) async-start(bf16[128,4,8,384]{0,3,1,2:T(8,128)(2,1)} %copy.16), calls=%async_computation | async-start | bytes 6291456 | tf_op jit(solution)/shard_map/all_to_all | solution.py:16
  22.9 4.7 copy.21
  27.6 69.1 %all-to-all-done = bf16[128,4,8,384]{0,3,1,2:T(8,128)(2,1)S(1)} async-done(((bf16[128,4,8,384]{0,3,1,2:T(8,128)(2,1)}), bf16[128,4,8,384]{0,3,1,2:T(8,128)(2,1)S(1)}, u32[]{:S(2)}, u32[]{:S(2)}) %all-to-all-start) | async-done | bytes 3145760 | tf_op jit(solution)/shard_map/all_to_all | solution.py:16
  96.7 0.0 copy-start
  96.7 1.6 copy-done
  98.3 3.6 all-to-all-start.2
  101.9 4.7 copy.17
  106.6 69.4 %all-to-all-done.2 = bf16[512,8,384]{0,2,1:T(8,128)(2,1)S(1)} async-done(((bf16[512,8,384]{0,2,1:T(8,128)(2,1)}), bf16[512,8,384]{0,2,1:T(8,128)(2,1)S(1)}, u32[]{:S(2)}, u32[]{:S(2)}) %all-to-all-start.2) | async-done | bytes 3145760 | tf_op jit(solution)/shard_map/all_to_all | solution.py:24
  176.1 0.0 copy-start.3
  176.1 0.0 copy-start.2
  176.1 7.7 %all-to-all-start.1 = ((bf16[128,32,1,384]{3,0,2,1:T(8,128)(2,1)}), bf16[128,32,1,384]{3,0,2,1:T(8,128)(2,1)}, u32[]{:S(2)}, u32[]{:S(2)}) async-start(bf16[128,32,1,384]{3,0,2,1:T(8,128)(2,1)} %bitcast.36), calls=%async_computation.1 | async-start | bytes 6291456 | tf_op jit(solution)/shard_map/all_to_all | solution.py:15
  183.8 0.0 reduce-scatter.2.cloned.1.call-start
  183.9 0.0 copy-done.3
  183.9 0.6 dynamic-slice
  185.1 0.0 copy-done.2
  185.1 0.2 dynamic-update-slice
  185.4 45.7 %all-reduce = s32[512]{0:T(512)S(1)} all-reduce(s32[512]{0:T(512)S(1)} %dynamic-update-slice), channel_id=1, replica_groups=mesh['dp'=32,'vocab'=8] {'dp'}, use_global_device_ids=true, to_apply=%add | all-reduce | flops 512 | bytes 4096
  231.1 2.8 copy.22
  233.9 0.0 all-to-all-done.1
  233.9 3.7 copy.24
  237.6 1.1 copy.20
  238.7 0.0 all-gather.2.cloned.1.call-done
  238.8 0.0 copy-start.1
  238.8 6.1 %fusion.17 = (f32[512]{0:T(512)S(1)}, f32[512,384]{0,1:T(8,128)}) fusion(bf16[4096,384]{1,0:T(8,128)(2,1)} %bitcast.42, bf16[2,512,4096]{2,1,0:T(8,128)(2,1)} %all-gather.2.cloned.1.call-done), kind=kOutput, calls=%fused_computation.30 | convolution fusion | flops 1610808832 | bytes 8128512 | tf_op jit(solution)/shard_map/dot_general | solution.py:31
  244.8 0.0 copy-done.1
  244.8 2.8 fusion.18
  247.6 72.0 %all-reduce.2 = (f32[512]{0:T(512)S(1)}, f32[512]{0:T(512)S(1)}) all-reduce(f32[512]{0:T(512)S(1)} %get-tuple-element.16, f32[512]{0:T(512)S(1)} %get-tuple-element.18), channel_id=1, replica_groups=mesh['dp'=32,'vocab'=8] {'dp','vocab'}, use_global_device_ids=true, to_apply=%region_5.0 | all-reduce | flops 1024 | bytes 8192 | tf_op jit(solution)/shard_map/pmax | solution.py:42
  319.6 1.8 multiply_reduce_fusion
  321.4 74.5 %all-reduce.1 = (f32[512]{0:T(512)S(1)}, f32[512]{0:T(512)S(1)}, f32[512]{0:T(512)S(1)}, f32[512]{0:T(512)S(1)}) all-reduce(f32[512]{0:T(512)S(1)} %get-tuple-element.5, f32[512]{0:T(512)S(1)} %get-tuple-element.3, f32[512]{0:T(512)S(1)} %get-tuple-element.2, ...), channel_id=1, replica_groups=mesh['dp'=32,'vocab'=8] {'dp','vocab'}, use_global_device_ids=true, to_apply=%region_7.0 | all-reduce | flops 2048 | bytes 16384 | tf_op jit(solution)/shard_map/psum | solution.py:45
  395.9 7.2 %fusion.8 = f32[512,4096]{1,0:T(8,128)} fusion(bf16[4096,384]{1,0:T(8,128)(2,1)S(1)} %bitcast.41, f32[512,384]{0,1:T(8,128)} %get-tuple-element.17, f32[512,384]{0,1:T(8,128)} %get-tuple-element.19, s32[512]{0:T(512)S(1)} %all-reduce, f32[512]{0:T(512)S(1)} %get-tuple-element.13, f32[512]{0:T(512)S(1)} %get-tuple-element.15, f32[512]{0:T(512)S(1)} %get-tuple-element.14, ...), kind=kOutput, calls=%fused_computation.16 | convolution fusion | flops 1612775424 | bytes 13116928 | tf_op jit(solution)/shard_map/dot_general | solution.py:69
  403.1 0.0 reduce-scatter.2.cloned.1.call-update
  403.1 0.6 dynamic_slice.3
  403.7 95.2 %reduce-scatter.2.cloned.1.call-done = f32[16,4096]{1,0:T(8,128)} async-done(((f32[512,4096]{1,0:T(8,128)}), f32[16,4096]{1,0:T(8,128)}) %reduce-scatter.2.cloned.1.call-update) | async-done | bytes 262160 | tf_op jit(solution)/shard_map/reduce_scatter | solution.py:68
  498.9 34.5 %all-reduce.4 = bf16[16,4096]{1,0:T(8,128)(2,1)} all-reduce(f32[16,4096]{1,0:T(8,128)} %reduce-scatter.2.cloned.1.call-done), channel_id=1, replica_groups=mesh['dp'=32,'vocab'=8] {'vocab'}, use_global_device_ids=true, to_apply=%region_11.0 | all-reduce | flops 65536 | bytes 393216 | tf_op jit(solution)/shard_map/psum | solution.py:76
  (3 shorter events, 0.0 us)
Async XLA Ops:
  7.2 231.6 %all-gather.2.cloned.1.call-start = ((), (), s32[]{:S(2)}) async-start(), calls=%async_computation.4 | async-start | bytes 8650752 | tf_op jit(solution)/shard_map/all_gather | solution.py:29
  14.4 82.2 %all-to-all-start = ((bf16[128,4,8,384]{0,3,1,2:T(8,128)(2,1)}), bf16[128,4,8,384]{0,3,1,2:T(8,128)(2,1)S(1)}, u32[]{:S(2)}, u32[]{:S(2)}) async-start(bf16[128,4,8,384]{0,3,1,2:T(8,128)(2,1)} %copy.16), calls=%async_computation | async-start | bytes 6291456 | tf_op jit(solution)/shard_map/all_to_all | solution.py:16
  96.7 1.6 copy-start
  98.3 77.8 %all-to-all-start.2 = ((bf16[512,8,384]{0,2,1:T(8,128)(2,1)}), bf16[512,8,384]{0,2,1:T(8,128)(2,1)S(1)}, u32[]{:S(2)}, u32[]{:S(2)}) async-start(bf16[512,8,384]{0,2,1:T(8,128)(2,1)} %bitcast.37), calls=%async_computation.2 | async-start | bytes 6291456 | tf_op jit(solution)/shard_map/all_to_all | solution.py:24
  176.1 7.8 %copy-start.3 = (u32[256]{0:T(256)S(1)}, u32[256]{0:T(256)}, u32[]{:S(2)}) copy-start(u32[256]{0:T(256)} %constant.32) | copy-start | bytes 3076
  176.1 9.1 %copy-start.2 = (s32[16]{0:T(128)S(1)}, s32[16]{0:T(128)}, u32[]{:S(2)}) copy-start(s32[16]{0:T(128)} %param.9) | copy-start | bytes 196
  176.1 57.8 %all-to-all-start.1 = ((bf16[128,32,1,384]{3,0,2,1:T(8,128)(2,1)}), bf16[128,32,1,384]{3,0,2,1:T(8,128)(2,1)}, u32[]{:S(2)}, u32[]{:S(2)}) async-start(bf16[128,32,1,384]{3,0,2,1:T(8,128)(2,1)} %bitcast.36), calls=%async_computation.1 | async-start | bytes 6291456 | tf_op jit(solution)/shard_map/all_to_all | solution.py:15
  183.8 315.1 %reduce-scatter.2.cloned.1.call-start = ((), (), s32[]{:S(2)}) async-start(), calls=%async_computation.5 | async-start | bytes 8650752 | tf_op jit(solution)/shard_map/reduce_scatter | solution.py:68
  238.8 6.1 %copy-start.1 = (bf16[2,512,4096]{2,1,0:T(8,128)(2,1)S(1)}, bf16[2,512,4096]{2,1,0:T(8,128)(2,1)}, u32[]{:S(2)}) copy-start(bf16[2,512,4096]{2,1,0:T(8,128)(2,1)} %all-gather.2.cloned.1.call-done) | copy-start | bytes 25165828
Sparse Core Ops, SparseCore 0:
  10.7 60.5 all-gather.1
  403.2 95.5 reduce-scatter.1
where the time goes:
time: 541 us; the launch traced here: 540 us
  waiting for transfers between devices  234 us (43%)
  blocking collectives  227 us (42%)
  local copies, waits for them, and re-layouts  25.5 us (5%)
  starting transfers between devices  19.9 us (4%)
  matrix products  16.1 us (3%)
  between operations  14.8 us (3%)
    reduce_scatter x1, waiting for transfers between devices, local(): lax.psum_scatter(lax.dot_general(logit_grad, student_cols, (((1,), (1,)),...  95.2 us
    psum x1, blocking collectives, local(): lax.psum((jnp.sum(student_exp, axis=1), jnp.sum(teacher_exp, axis=1), jnp...  74.5 us
    pmax x1, blocking collectives, local(): lax.pmax((student_local_top, teacher_local_top), ('dp', 'vocab'))  72 us
    all_to_all x1, waiting for transfers between devices, local(): lax.all_to_all(teacher_parts, 'vocab', split_axis=1, concat_axis=0, tiled...  69.4 us
    all_to_all x1, waiting for transfers between devices, local(): lax.all_to_all(spread_in, 'vocab', split_axis=2, concat_axis=1, tiled=True)  69.1 us
    unnamed x1, blocking collectives  45.7 us
    psum x1, blocking collectives, local(): grad_hidden = lax.psum(partial_sum, 'vocab').astype(jnp.bfloat16)  34.5 us
  transfers between devices with their start and end apart: 5, of which 3 were waited for; matrix products, arithmetic and copies ran while one was open for 4% of the time, Pallas kernels for 0%

commit v1 on v0

v1 whole, which is shorter than its diff:
```python
import jax
import jax.numpy as jnp
from jax import lax
from jax.sharding import Mesh, PartitionSpec as P

ce_weight = 0.5
digit = 64
lanes = 128
XYH = ("x", "yh")
XY = ("x", "yh", "yl")
DP = ("x", "yh", "yl", "c")


def swap_cores(value):
    return lax.ppermute(value, "c", [(0, 1), (1, 0)])


def in_core_order(mine, other, axis):
    first = lax.axis_index("c") == 0
    return jnp.concatenate(
        [jnp.where(first, mine, other), jnp.where(first, other, mine)], axis=axis
    )


def spread(value, axes):
    count = lax.axis_size(axes)
    copies = jnp.broadcast_to(value[None], (count,) + value.shape)
    return lax.all_to_all(copies, axes, 0, 0, tiled=True)


def merge(stats):
    student_tops, teacher_tops = stats[:, 0], stats[:, 1]
    student_top = jnp.max(student_tops, axis=0)
    teacher_top = jnp.max(teacher_tops, axis=0)
    student_scale = jnp.exp(student_tops - student_top)
    teacher_scale = jnp.exp(teacher_tops - teacher_top)
    return jnp.stack(
        [
            student_top,
            teacher_top,
            jnp.sum(stats[:, 2] * student_scale, axis=0),
            jnp.sum(stats[:, 3] * teacher_scale, axis=0),
            jnp.sum(stats[:, 4] * student_scale, axis=0),
            jnp.sum(stats[:, 5], axis=0),
        ]
    )


def local(student_hidden, teacher_hidden, student_head, teacher_head, sampled_ids):
    core = lax.axis_index("c")
    tok, width = student_hidden.shape
    xy_count = lax.axis_size(XY)
    z_count = lax.axis_size("z")
    row_part = student_head.shape[0]
    unit = teacher_head.shape[1] // z_count
    teacher_rows = teacher_head.shape[0]
    half = width // 2

    teacher_parts = teacher_head.reshape(teacher_rows, z_count, unit).transpose(1, 0, 2)
    teacher_cols = lax.all_to_all(teacher_parts, XYH, 0, 0, tiled=True)

    by_core = student_hidden.reshape(tok, xy_count, 2, row_part)
    even = by_core[:, :, 0].reshape(tok, half)
    odd = by_core[:, :, 1].reshape(tok, half)
    keep = jnp.where(core == 0, even, odd)
    give = jnp.where(core == 0, odd, even)
    teacher_slice = lax.dynamic_slice_in_dim(
        teacher_hidden, lax.axis_index("z") * teacher_rows, teacher_rows, 1
    )
    digits = jnp.stack(
        [sampled_ids // (digit * digit), sampled_ids // digit % digit, sampled_ids % digit], axis=1
    ).astype(jnp.bfloat16)
    digits = jnp.pad(digits, ((0, 0), (0, lanes - 3)))
    shared = jnp.concatenate([teacher_slice, digits], axis=1)
    received = swap_cores(jnp.concatenate([give, shared], axis=1))
    pair = in_core_order(jnp.concatenate([keep, shared], axis=1), received, 0)
    rows = lax.all_gather(pair, XY, axis=0, tiled=True)
    student_rows = rows[:, :half]
    teacher_rows_all = rows[:, half : half + teacher_rows]
    id_digits = rows[:, half + teacher_rows : half + teacher_rows + 3].astype(jnp.int32)
    all_ids = (id_digits[:, 0] * digit + id_digits[:, 1]) * digit + id_digits[:, 2]
    tokens = rows.shape[0]

    teacher_part = jnp.stack(
        [
            jnp.dot(teacher_rows_all, teacher_cols[s], preferred_element_type=jnp.float32)
            for s in range(z_count)
        ]
    )
    student_head, teacher_part = lax.optimization_barrier((student_head, teacher_part))
    teacher_logits = lax.psum_scatter(teacher_part, "z", scatter_dimension=0, tiled=False)

    parts = student_head.reshape(row_part, 2, 2, z_count, unit).transpose(3, 1, 0, 2, 4)
    parts = parts.reshape(xy_count, row_part, 2 * unit)
    student_cols = lax.all_to_all(parts, XY, 0, 0, tiled=True).reshape(half, 2 * unit)
    student_part = jnp.dot(student_rows, student_cols, preferred_element_type=jnp.float32)
    left, right = student_part[:, :unit], student_part[:, unit:]
    student_logits = jnp.where(core == 0, left, right) + swap_cores(
        jnp.where(core == 0, right, left)
    )

    xyh = lax.axis_index("x") * 2 + lax.axis_index("yh")
    owner = (lax.axis_index("z") * 2 + lax.axis_index("yl")) * 2 + core
    first_col = (owner * z_count + xyh) * unit
    column_ids = first_col + jnp.arange(unit, dtype=jnp.int32)
    hit_mask = (column_ids[None, :] == all_ids[:, None]).astype(jnp.float32)

    logit_gap = student_logits - teacher_logits
    student_top = jnp.max(student_logits, axis=1)
    teacher_top = jnp.max(teacher_logits, axis=1)
    student_exp = jnp.exp(student_logits - student_top[:, None])
    teacher_exp = jnp.exp(teacher_logits - teacher_top[:, None])
    stats = jnp.stack(
        [
            student_top,
            teacher_top,
            jnp.sum(student_exp, axis=1),
            jnp.sum(teacher_exp, axis=1),
            jnp.sum(student_exp * logit_gap, axis=1),
            jnp.sum(hit_mask * student_logits, axis=1),
        ]
    )
    stats = merge(jnp.stack([stats, swap_cores(stats)]))
    stats = merge(spread(stats, XY))
    stats = merge(spread(stats, "z"))
    student_norm = stats[0] + jnp.log(stats[2])
    teacher_norm = stats[1] + jnp.log(stats[3])
    expected_gap = stats[4] / stats[2]
    divergence = expected_gap - student_norm + teacher_norm
    every_loss = divergence + ce_weight * (student_norm - stats[5])
    own_start = lax.axis_index(DP) * tok
    token_loss = lax.dynamic_slice_in_dim(every_loss, own_start, tok, 0)

    student_prob = jnp.exp(student_logits - student_norm[:, None])
    logit_grad = (
        student_prob * (logit_gap - expected_gap[:, None])
        + ce_weight * (student_prob - hit_mask)
    ).astype(jnp.bfloat16)
    pair_grad = in_core_order(logit_grad, swap_cores(logit_grad), 1)
    grad_part = lax.dot_general(
        pair_grad, student_cols, (((1,), (1,)), ((), ())), preferred_element_type=jnp.float32
    ).astype(jnp.bfloat16)
    grad_part = grad_part.reshape(xy_count, tokens // xy_count, half)
    plane_sum = jnp.sum(
        lax.all_to_all(grad_part, XY, 0, 0, tiled=True).astype(jnp.float32), axis=0
    )
    plane_part = plane_sum.astype(jnp.bfloat16).reshape(z_count, -1, half)
    total = jnp.sum(
        lax.all_to_all(plane_part, "z", 0, 0, tiled=True).astype(jnp.float32), axis=0
    ).astype(jnp.bfloat16)
    grads = spread(total, "z").reshape(2, tok, half)
    mine = jnp.where(core == 0, grads[0], grads[1])
    other = swap_cores(jnp.where(core == 0, grads[1], grads[0]))
    grad_hidden = in_core_order(
        mine.reshape(tok, xy_count, 1, row_part), other.reshape(tok, xy_count, 1, row_part), 2
    ).reshape(tok, width)
    return (grad_hidden, token_loss)


def solution(mesh):
    fine = Mesh(mesh.devices.reshape(4, 2, 2, 2, 8), ("x", "yh", "yl", "c", "z"))
    in_specs = (P(DP, None), P(DP, None), P(DP, "z"), P("z", DP), P(DP))
    out_specs = (P(DP, None), P(DP))
    return jax.shard_map(local, mesh=fine, in_specs=in_specs, out_specs=out_specs, check_vma=False)
```

time: 541 us -> 280 us (0.52)
  waiting for transfers between devices: 234 us -> 45 us
  blocking collectives: 227 us -> 174 us
  starting transfers between devices: 19.9 us -> 0.72 us
  local copies, waits for them, and re-layouts: 25.5 us -> 12.7 us
  matrix products: 16.1 us -> 21.6 us
  other arithmetic: 3.48 us -> 8.95 us
    all_to_all x0 -> x7, blocking collectives: none -> 174 us  [the longest x1 48.3 us: local(): teacher_cols = lax.all_to_all(teacher_parts, XYH, 0, 0, tiled=True)]
    all_to_all x3 -> x0, waiting for transfers between devices: 139 us -> none  [the longest x1 69.4 us: local(): lax.all_to_all(teacher_parts, 'vocab', split_axis=1, concat_axis=0, tiled...]
    psum x2 -> x0, blocking collectives: 109 us -> none  [the longest x1 74.5 us: local(): lax.psum((jnp.sum(student_exp, axis=1), jnp.sum(teacher_exp, axis=1), jnp...]
    reduce_scatter x1, waiting for transfers between devices: 95.2 us -> 18.5 us  [local(): lax.psum_scatter(teacher_part, 'z', scatter_dimension=0, tiled=False)]
    pmax x1 -> x0, blocking collectives: 72 us -> none  [local(): lax.pmax((student_local_top, teacher_local_top), ('dp', 'vocab'))]
    unnamed x1 -> x0, blocking collectives: 45.7 us -> none
    all_gather x1, waiting for transfers between devices: 0.02 us -> 20.8 us  [local(): rows = lax.all_gather(pair, XY, axis=0, tiled=True)]
    all_to_all x3 -> x0, starting transfers between devices: 19.8 us -> none  [the longest x1 8.47 us: local(): lax.all_to_all(spread_in, 'vocab', split_axis=2, concat_axis=1, tiled=True)]
  transfers between devices with their start and end apart: 5 -> 7, of which waited for: 3 -> 7; matrix products, arithmetic and copies ran while one was open for 4% -> 6% of each run, Pallas kernels for 0% -> 0%
where the time goes in v1:
time: 280 us; the launch traced here: 278 us
  blocking collectives  174 us (62%)
  waiting for transfers between devices  45 us (16%)
  matrix products  21.6 us (8%)
  between operations  14.4 us (5%)
  local copies, waits for them, and re-layouts  12.7 us (5%)
  other arithmetic  8.95 us (3%)
    all_to_all x1, blocking collectives, local(): teacher_cols = lax.all_to_all(teacher_parts, XYH, 0, 0, tiled=True)  48.3 us
    all_to_all x1, blocking collectives, local(): lax.all_to_all(parts, XY, 0, 0, tiled=True).reshape(half, 2 * unit)  42.9 us
    all_to_all x3, blocking collectives, spread(): return lax.all_to_all(copies, axes, 0, 0, tiled=True)  39.3 us
    all_to_all x1, blocking collectives, local(): lax.all_to_all(grad_part, XY, 0, 0, tiled=True).astype(jnp.float32)  32.2 us
    all_gather x1, waiting for transfers between devices, local(): rows = lax.all_gather(pair, XY, axis=0, tiled=True)  20.8 us
    reduce_scatter x1, waiting for transfers between devices, local(): lax.psum_scatter(teacher_part, 'z', scatter_dimension=0, tiled=False)  18.5 us
    dot_general x8, matrix products, local(): jnp.dot(teacher_rows_all, teacher_cols[s], preferred_element_type=jnp.flo...  15.4 us
    all_to_all x1, blocking collectives, local(): lax.all_to_all(plane_part, 'z', 0, 0, tiled=True).astype(jnp.float32)  11.5 us
  transfers between devices with their start and end apart: 7, of which 7 were waited for; matrix products, arithmetic and copies ran while one was open for 6% of the time, Pallas kernels for 0%

profile of v1, /device:TPU:8, one launch (start us, length us, event | category | flops | bytes accessed | tf_op | source)
XLA Modules:
  0.0 277.5 jit_solution(5778274449150762316)
XLA Ops:
  7.2 0.0 copy-start
  7.2 0.0 all-gather.2.cloned.1.call-start
  7.2 1.0 reshape.126
  8.2 0.8 fusion.24
  9.0 0.7 convert_bitcast_fusion
  9.7 0.1 copy.121
  9.8 0.1 collective-permute-start
  10.0 1.2 collective-permute-done
  11.2 0.7 pad_maximum_fusion
  11.9 0.0 all-gather.2.cloned.1.call-update
  11.9 0.0 reduce-scatter.2.cloned.1.call-start
  12.0 3.2 %copy.122 = bf16[512,3072]{0,1:T(8,128)(2,1)S(1)} copy(bf16[512,3072]{1,0:T(8,128)(2,1)} %param.8) | data formatting | bytes 6291456 | tf_op args[3]
  15.2 48.3 %all_to_all.35 = bf16[8,512,384]{1,2,0:T(8,128)(2,1)} all-to-all(bf16[8,512,384]{1,2,0:T(8,128)(2,1)S(1)} %bitcast.210), channel_id=1, replica_groups=mesh['x'=4,'yh'=2,'yl'=2,'c'=2,'z'=8] {'x','yh'}, dimensions={0} | all-to-all | bytes 6291456 | tf_op jit(solution)/shard_map/all_to_all | solution.py:60
  63.5 20.8 %all-gather.2.cloned.1.call-done = bf16[512,2688]{1,0:T(8,128)(2,1)} async-done(((bf16[32,2688]{1,0:T(8,128)(2,1)}), bf16[512,2688]{1,0:T(8,128)(2,1)}) %all-gather.2.cloned.1.call-update) | async-done | bytes 2752528 | tf_op jit(solution)/shard_map/all_gather | solution.py:77
  84.3 2.6 fusion.9
  87.0 2.5 fusion.8
  89.5 2.4 fusion.7
  91.9 2.4 fusion.6
  94.3 1.3 fusion.5
  95.6 1.3 fusion.4
  97.0 1.4 fusion.3
  98.3 1.4 fusion.2
  99.7 0.0 reduce-scatter.2.cloned.1.call-update
  99.8 3.5 %copy.131 = bf16[128,12288]{0,1:T(8,128)(2,1)S(1)} copy(bf16[128,12288]{1,0:T(8,128)(2,1)} %param.7) | data formatting | bytes 6291456 | tf_op jit(solution)/shard_map/optimization_barrier | solution.py:90
  103.3 0.2 copy.132
  103.5 42.9 %all_to_all.36 = bf16[16,128,768]{1,2,0:T(8,128)(2,1)S(1)} all-to-all(bf16[16,128,768]{1,2,0:T(8,128)(2,1)S(1)} %bitcast.209), channel_id=1, replica_groups=mesh['x'=4,'yh'=2,'yl'=2,'c'=2,'z'=8] {'x','yh','yl'}, dimensions={0} | all-to-all | bytes 6291456 | tf_op jit(solution)/shard_map/all_to_all | solution.py:95
  146.4 2.9 %copy.133 = bf16[16,128,768]{2,1,0:T(8,128)(2,1)} copy(bf16[16,128,768]{1,2,0:T(8,128)(2,1)S(1)} %all_to_all.36) | data formatting | bytes 6291456 | tf_op jit(solution)/shard_map/all_to_all | solution.py:95
  149.3 4.3 %fusion = f32[512,768]{1,0:T(8,128)S(1)} fusion(bf16[2048,768]{1,0:T(8,128)(2,1)} %bitcast.212, bf16[512,2688]{1,0:T(8,128)(2,1)} %all-gather.2.cloned.1.call-done), kind=kOutput, calls=%fused_computation.1 | convolution fusion | flops 1610612736 | bytes 6815744 | tf_op jit(solution)/shard_map/dot_general | solution.py:96
  153.6 0.1 slice_select_fusion
  153.7 0.1 collective-permute-start.1
  153.9 0.9 slice_convert_fusion
  154.8 0.3 fusion.21
  155.1 1.0 collective-permute-done.1
  156.1 0.2 fusion.76
  156.3 18.5 %reduce-scatter.2.cloned.1.call-done = f32[1,512,384]{2,1,0:T(8,128)} async-done(((f32[8,512,384]{2,1,0:T(8,128)}), f32[1,512,384]{2,1,0:T(8,128)}) %reduce-scatter.2.cloned.1.call-update) | async-done | bytes 786448 | tf_op jit(solution)/shard_map/reduce_scatter | solution.py:91
  174.8 1.4 reduce_max.73
  176.1 1.9 multiply_reduce_fusion
  178.1 0.1 collective-permute-start.2
  178.2 1.1 collective-permute-done.2
  179.5 14.4 %all_to_all.37 = f32[16,6,512]{2,1,0:T(8,128)S(1)} all-to-all(f32[16,6,512]{2,1,0:T(8,128)S(1)} %broadcast_in_dim.6), channel_id=1, replica_groups=mesh['x'=4,'yh'=2,'yl'=2,'c'=2,'z'=8] {'x','yh','yl'}, dimensions={0} | all-to-all | bytes 393216 | tf_op jit(solution)/shard_map/all_to_all | solution.py:28
  193.9 0.2 fusion.77
  194.1 0.0 copy-start.2
  194.1 13.5 %all_to_all.38 = f32[8,6,512]{2,1,0:T(8,128)S(1)} all-to-all(f32[8,6,512]{2,1,0:T(8,128)S(1)} %broadcast_in_dim.7), channel_id=1, replica_groups=mesh['x'=4,'yh'=2,'yl'=2,'c'=2,'z'=8] {'z'}, dimensions={0} | all-to-all | bytes 196608 | tf_op jit(solution)/shard_map/all_to_all | solution.py:28
  207.6 0.1 fusion.78
  207.8 0.4 fusion.14
  208.2 0.3 collective-permute-start.3
  208.5 1.7 collective-permute-done.3
  210.2 0.1 broadcast_select_fusion.1
  210.3 1.8 convolution_convert_fusion
  212.1 32.2 %all_to_all.39 = bf16[16,32,2048]{2,1,0:T(8,128)(2,1)S(1)} all-to-all(bf16[16,32,2048]{2,1,0:T(8,128)(2,1)S(1)} %bitcast.214), channel_id=1, replica_groups=mesh['x'=4,'yh'=2,'yl'=2,'c'=2,'z'=8] {'x','yh','yl'}, dimensions={0} | all-to-all | bytes 4194304 | tf_op jit(solution)/shard_map/all_to_all | solution.py:145
  244.3 0.4 reduce_sum.182
  244.7 0.1 reshape.132
  244.8 11.5 %all_to_all.40 = bf16[8,4,2048]{2,1,0:T(4,128)(2,1)S(1)} all-to-all(bf16[8,4,2048]{2,1,0:T(4,128)(2,1)S(1)} %reshape.132), channel_id=1, replica_groups=mesh['x'=4,'yh'=2,'yl'=2,'c'=2,'z'=8] {'z'}, dimensions={0} | all-to-all | bytes 262144 | tf_op jit(solution)/shard_map/all_to_all | solution.py:149
  256.2 0.1 reduce_sum.183
  256.4 11.5 %all_to_all.41 = bf16[8,4,2048]{2,1,0:T(4,128)(2,1)S(1)} all-to-all(bf16[8,4,2048]{2,1,0:T(4,128)(2,1)S(1)} %broadcast_in_dim.8), channel_id=1, replica_groups=mesh['x'=4,'yh'=2,'yl'=2,'c'=2,'z'=8] {'z'}, dimensions={0} | all-to-all | bytes 262144 | tf_op jit(solution)/shard_map/all_to_all | solution.py:28
  267.8 0.1 broadcast_select_fusion.9
  267.9 0.1 collective-permute-start.4
  268.0 0.6 dynamic_slice.7
  268.6 0.1 select_n.158
  268.7 0.5 collective-permute-done.4
  269.2 0.1 reshape.135
  269.3 0.3 broadcast_select_fusion.3
  269.6 0.3 pad_maximum_fusion.1
  269.9 0.7 reshape.134
  (30 shorter events, 0.5 us)
Async XLA Ops:
  7.2 2.7 copy-start
  7.2 77.2 %all-gather.2.cloned.1.call-start = ((), (), s32[]{:S(2)}) async-start(), calls=%async_computation.8 | async-start | bytes 2924544 | tf_op jit(solution)/shard_map/all_gather | solution.py:77
  9.8 1.4 collective-permute-start
  11.9 162.8 %reduce-scatter.2.cloned.1.call-start = ((), (), s32[]{:S(2)}) async-start(), calls=%async_computation.9 | async-start | bytes 7077888 | tf_op jit(solution)/shard_map/reduce_scatter | solution.py:91
  63.5 26.0 %copy-start.3 = (bf16[8,512,384]{1,2,0:T(8,128)(2,1)S(1)}, bf16[8,512,384]{1,2,0:T(8,128)(2,1)}, u32[]{:S(2)}) copy-start(bf16[8,512,384]{1,2,0:T(8,128)(2,1)} %all_to_all.35) | copy-start | bytes 9437188
  84.3 10.0 %copy-start.4 = (bf16[512,2688]{1,0:T(8,128)(2,1)S(1)}, bf16[512,2688]{1,0:T(8,128)(2,1)}, u32[]{:S(2)}) copy-start(bf16[512,2688]{1,0:T(8,128)(2,1)} %all-gather.2.cloned.1.call-done) | copy-start | bytes 8257540
  153.7 2.4 collective-permute-start.1
  174.8 33.0 %copy-start.1 = (f32[1,512,384]{2,1,0:T(8,128)S(1)}, f32[1,512,384]{2,1,0:T(8,128)}, u32[]{:S(2)}) copy-start(f32[1,512,384]{2,1,0:T(8,128)} %reduce-scatter.2.cloned.1.call-done) | copy-start | bytes 2359300
  178.1 1.3 collective-permute-start.2
  194.1 16.2 %copy-start.2 = (bf16[16,128,768]{2,1,0:T(8,128)(2,1)S(1)}, bf16[16,128,768]{2,1,0:T(8,128)(2,1)}, u32[]{:S(2)}) copy-start(bf16[16,128,768]{2,1,0:T(8,128)(2,1)} %copy.133) | copy-start | bytes 9437188
  208.2 2.0 collective-permute-start.3
  267.9 1.3 collective-permute-start.4
Sparse Core Ops, SparseCore 0:
  12.1 72.2 all-gather.1
  99.9 74.8 reduce-scatter.1

commit v2 on v1

v2 whole, which is shorter than its diff:
```python
import jax
import jax.numpy as jnp
from jax import lax
from jax.experimental import pallas as pl
from jax.experimental.pallas import tpu as pltpu
from jax.sharding import Mesh, PartitionSpec as P

ce_weight = 0.5
digit = 64
lanes = 128
XYH = ("x", "yh")
XY = ("x", "yh", "yl")
DP = ("x", "yh", "yl", "c")


def swap_cores(value):
    return lax.ppermute(value, "c", [(0, 1), (1, 0)])


def in_core_order(mine, other, axis):
    first = lax.axis_index("c") == 0
    return jnp.concatenate(
        [jnp.where(first, mine, other), jnp.where(first, other, mine)], axis=axis
    )


def exchange(value, axes):
    return lax.all_to_all(value, axes, 0, 0, tiled=True)


def spread(value, axes):
    count = lax.axis_size(axes)
    return exchange(jnp.broadcast_to(value[None], (count,) + value.shape), axes)


def merge(stats):
    student_tops, teacher_tops = stats[:, 0], stats[:, 1]
    student_top = jnp.max(student_tops, axis=0)
    teacher_top = jnp.max(teacher_tops, axis=0)
    student_scale = jnp.exp(student_tops - student_top)
    teacher_scale = jnp.exp(teacher_tops - teacher_top)
    return jnp.stack(
        [
            student_top,
            teacher_top,
            jnp.sum(stats[:, 2] * student_scale, axis=0),
            jnp.sum(stats[:, 3] * teacher_scale, axis=0),
            jnp.sum(stats[:, 4] * student_scale, axis=0),
            jnp.sum(stats[:, 5], axis=0),
        ]
    )


def teacher_kernel(rows_ref, cols_ref, out_ref):
    part = jnp.dot(rows_ref[...], cols_ref[...], preferred_element_type=jnp.float32)
    out_ref[:, 0] = part.reshape(out_ref.shape[0], out_ref.shape[2], out_ref.shape[3])


def teacher_partial(rows, head, planes, unit):
    depth, width = head.shape
    tokens = rows.shape[0]
    units = width // unit
    return pl.pallas_call(
        teacher_kernel,
        grid=(units,),
        in_specs=[
            pl.BlockSpec((tokens, depth), lambda j: (0, 0)),
            pl.BlockSpec((depth, unit), lambda j: (0, j)),
        ],
        out_specs=pl.BlockSpec((planes, 1, tokens // planes, unit), lambda j: (0, j, 0, 0)),
        out_shape=jax.ShapeDtypeStruct((planes, units, tokens // planes, unit), jnp.float32),
        compiler_params=pltpu.CompilerParams(vmem_limit_bytes=32 * 2**20),
    )(rows, head)


def regroup_kernel(head_ref, out_ref):
    unit = out_ref.shape[4]
    for j in range(out_ref.shape[0]):
        out_ref[j, 0, 0] = head_ref[:, j * unit : (j + 1) * unit]


def regroup(head, units, unit):
    rows, width = head.shape
    return pl.pallas_call(
        regroup_kernel,
        grid=(2, 2),
        in_specs=[pl.BlockSpec((rows, width // 4), lambda yl, core: (0, yl * 2 + core))],
        out_specs=pl.BlockSpec(
            (units, 1, 1, rows, unit), lambda yl, core: (0, yl, core, 0, 0)
        ),
        out_shape=jax.ShapeDtypeStruct((units, 2, 2, rows, unit), head.dtype),
        compiler_params=pltpu.CompilerParams(vmem_limit_bytes=32 * 2**20),
    )(head)


def student_kernel(core_ref, rows_ref, own_ref, pair_ref, mine_ref, other_ref):
    depth, unit = rows_ref.shape[1], mine_ref.shape[1]
    for cols_ref, out_ref in ((own_ref, mine_ref), (pair_ref, other_ref)):
        cols = cols_ref[:, 0].reshape(depth, unit)
        out_ref[...] = jnp.dot(rows_ref[...], cols, preferred_element_type=jnp.float32)


def student_partial(core, rows, cols):
    tokens, depth = rows.shape
    groups, _, part, unit = cols.shape
    block = 128
    half = jax.ShapeDtypeStruct((tokens, unit), jnp.float32)
    return pl.pallas_call(
        student_kernel,
        grid_spec=pltpu.PrefetchScalarGridSpec(
            num_scalar_prefetch=1,
            grid=(tokens // block,),
            in_specs=[
                pl.BlockSpec((block, depth), lambda i, core: (i, 0)),
                pl.BlockSpec((groups, 1, part, unit), lambda i, core: (0, core[0], 0, 0)),
                pl.BlockSpec((groups, 1, part, unit), lambda i, core: (0, 1 - core[0], 0, 0)),
            ],
            out_specs=[pl.BlockSpec((block, unit), lambda i, core: (i, 0))] * 2,
        ),
        out_shape=[half, half],
        compiler_params=pltpu.CompilerParams(vmem_limit_bytes=32 * 2**20),
    )(core, rows, cols, cols)


def grad_kernel(core_ref, own_grad_ref, pair_grad_ref, own_ref, pair_ref, out_ref):
    total = None
    for grad_ref, cols_ref in ((own_grad_ref, own_ref), (pair_grad_ref, pair_ref)):
        cols = cols_ref[:, 0].reshape(out_ref.shape[1], grad_ref.shape[1])
        term = lax.dot_general(
            grad_ref[...], cols, (((1,), (1,)), ((), ())), preferred_element_type=jnp.float32
        )
        total = term if total is None else total + term
    out_ref[...] = total.astype(out_ref.dtype)


def grad_partial(core, own_grad, pair_grad, cols):
    tokens, unit = own_grad.shape
    groups, _, part, _ = cols.shape
    block = 4
    return pl.pallas_call(
        grad_kernel,
        grid_spec=pltpu.PrefetchScalarGridSpec(
            num_scalar_prefetch=1,
            grid=(groups // block,),
            in_specs=[
                pl.BlockSpec((tokens, unit), lambda i, core: (0, 0)),
                pl.BlockSpec((tokens, unit), lambda i, core: (0, 0)),
                pl.BlockSpec((block, 1, part, unit), lambda i, core: (i, core[0], 0, 0)),
                pl.BlockSpec((block, 1, part, unit), lambda i, core: (i, 1 - core[0], 0, 0)),
            ],
            out_specs=pl.BlockSpec((tokens, block * part), lambda i, core: (0, i)),
        ),
        out_shape=jax.ShapeDtypeStruct((tokens, groups * part), jnp.bfloat16),
        compiler_params=pltpu.CompilerParams(vmem_limit_bytes=32 * 2**20),
    )(core, own_grad, pair_grad, cols, cols)


def local(student_hidden, teacher_hidden, student_head, teacher_head, sampled_ids):
    core = lax.axis_index("c")
    core_id = core.reshape(1).astype(jnp.int32)
    plane = lax.axis_index("z")
    tok, width = student_hidden.shape
    xy_count = lax.axis_size(XY)
    z_count = lax.axis_size("z")
    row_part = student_head.shape[0]
    unit = teacher_head.shape[1] // z_count
    depth = teacher_head.shape[0]
    half = width // 2

    teacher_slice = lax.dynamic_slice_in_dim(teacher_hidden, plane * depth, depth, 1)
    digits = jnp.stack(
        [sampled_ids // (digit * digit), sampled_ids // digit % digit, sampled_ids % digit], axis=1
    ).astype(jnp.bfloat16)
    digits = jnp.pad(digits, ((0, 0), (0, lanes - 3)))
    shared = jnp.concatenate([teacher_slice, digits], axis=1)
    shared = in_core_order(shared, swap_cores(shared), 0)
    shared = spread(shared, XY).reshape(-1, depth + lanes)
    tokens = shared.shape[0]
    some = tokens // z_count

    teacher_part = teacher_partial(shared, teacher_head, z_count, unit)

    parts = regroup(student_head, z_count, unit).reshape(xy_count, 2, row_part, unit)
    by_core = student_hidden.reshape(tok, xy_count, 2, row_part)
    even = by_core[:, :, 0].reshape(tok, half)
    odd = by_core[:, :, 1].reshape(tok, half)
    received = swap_cores(jnp.where(core == 0, odd, even))
    student_pair = in_core_order(jnp.where(core == 0, even, odd), received, 0)

    parts, student_pair, teacher_part = lax.optimization_barrier(
        (parts, student_pair, teacher_part)
    )
    teacher_own = lax.psum_scatter(teacher_part, "z", scatter_dimension=0, tiled=False)

    student_cols = exchange(parts, XY)
    student_rows = spread(student_pair, XY).reshape(tokens, half)
    teacher_own, _ = lax.optimization_barrier((teacher_own, (student_rows, student_cols)))
    teacher_logits = exchange(teacher_own, XYH)

    mine, other = student_partial(core_id, student_rows, student_cols)
    student_logits = exchange((mine + swap_cores(other)).reshape(z_count, some, unit), "z")

    xyh = lax.axis_index("x") * 2 + lax.axis_index("yh")
    planes = jnp.arange(z_count, dtype=jnp.int32)
    owner = (planes * 2 + lax.axis_index("yl")) * 2 + core
    column_ids = ((owner * z_count + xyh) * unit)[:, None] + jnp.arange(unit, dtype=jnp.int32)
    id_digits = lax.dynamic_slice_in_dim(shared, plane * some, some, 0)[:, depth : depth + 3]
    id_digits = id_digits.astype(jnp.int32)
    ids = (id_digits[:, 0] * digit + id_digits[:, 1]) * digit + id_digits[:, 2]
    hit_mask = (column_ids[:, None, :] == ids[None, :, None]).astype(jnp.float32)

    logit_gap = student_logits - teacher_logits
    student_top = jnp.max(student_logits, axis=(0, 2))
    teacher_top = jnp.max(teacher_logits, axis=(0, 2))
    student_exp = jnp.exp(student_logits - student_top[:, None])
    teacher_exp = jnp.exp(teacher_logits - teacher_top[:, None])
    stats = jnp.stack(
        [
            student_top,
            teacher_top,
            jnp.sum(student_exp, axis=(0, 2)),
            jnp.sum(teacher_exp, axis=(0, 2)),
            jnp.sum(student_exp * logit_gap, axis=(0, 2)),
            jnp.sum(hit_mask * student_logits, axis=(0, 2)),
        ]
    )
    stats = merge(jnp.stack([stats, swap_cores(stats)]))
    stats = merge(spread(stats, XY))
    student_norm = stats[0] + jnp.log(stats[2])
    teacher_norm = stats[1] + jnp.log(stats[3])
    expected_gap = stats[4] / stats[2]
    divergence = expected_gap - student_norm + teacher_norm
    losses = divergence + ce_weight * (student_norm - stats[5])

    student_prob = jnp.exp(student_logits - student_norm[:, None])
    logit_grad = (
        student_prob * (logit_gap - expected_gap[:, None])
        + ce_weight * (student_prob - hit_mask)
    ).astype(jnp.bfloat16)
    logit_grad = exchange(logit_grad, "z").reshape(tokens, unit)
    grad_part = grad_partial(core_id, logit_grad, swap_cores(logit_grad), student_cols)
    grad_part = grad_part.reshape(xy_count, 2 * tok, half)
    plane_sum = jnp.sum(exchange(grad_part, XY).astype(jnp.float32), axis=0)
    plane_part = plane_sum.astype(jnp.bfloat16).reshape(z_count, -1, half)
    total = jnp.sum(exchange(plane_part, "z").astype(jnp.float32), axis=0).astype(jnp.bfloat16)

    high = losses.astype(jnp.bfloat16)
    rest = losses - high.astype(jnp.float32)
    middle = rest.astype(jnp.bfloat16)
    low = (rest - middle.astype(jnp.float32)).astype(jnp.bfloat16)
    terms = jnp.pad(
        jnp.stack([high, middle, low]), ((0, total.shape[0] - 3), (0, lanes - some))
    )
    final = spread(jnp.concatenate([total, terms], axis=1), "z")
    term = final[:, :3, half : half + some].astype(jnp.float32)
    every_loss = ((term[:, 2] + term[:, 1]) + term[:, 0]).reshape(tokens)
    token_loss = lax.dynamic_slice_in_dim(every_loss, lax.axis_index(DP) * tok, tok, 0)
    grads = final[:, :, :half].reshape(2, tok, half)
    mine = jnp.where(core == 0, grads[0], grads[1])
    other = swap_cores(jnp.where(core == 0, grads[1], grads[0]))
    grad_hidden = in_core_order(
        mine.reshape(tok, xy_count, 1, row_part), other.reshape(tok, xy_count, 1, row_part), 2
    ).reshape(tok, width)
    return (grad_hidden, token_loss)


def solution(mesh):
    fine = Mesh(mesh.devices.reshape(4, 2, 2, 2, 8), ("x", "yh", "yl", "c", "z"))
    in_specs = (P(DP, None), P(DP, None), P(DP, "z"), P("z", DP), P(DP))
    out_specs = (P(DP, None), P(DP))
    return jax.shard_map(local, mesh=fine, in_specs=in_specs, out_specs=out_specs, check_vma=False)
```

time: 280 us -> 284 us (1.014)
  blocking collectives: 174 us -> 131 us
  starting transfers between devices: 0.72 us -> 27.8 us
  waiting for transfers between devices: 45 us -> 70.1 us
  matrix products: 21.6 us -> 0 us
  Pallas kernels: 0 us -> 12.8 us
  other arithmetic: 8.95 us -> 12.6 us
    all_to_all x0 -> x5, waiting for transfers between devices: none -> 64.4 us  [exchange(): return lax.all_to_all(value, axes, 0, 0, tiled=True)]
    all_to_all x7 -> x5, blocking collectives: 174 us -> 131 us  [exchange(): return lax.all_to_all(value, axes, 0, 0, tiled=True)]
    all_to_all x0 -> x5, starting transfers between devices: none -> 26.8 us  [exchange(): return lax.all_to_all(value, axes, 0, 0, tiled=True)]
    dot_general x10 -> x0, matrix products: 21.6 us -> none  [the longest x8 15.4 us: local(): jnp.dot(teacher_rows_all, teacher_cols[s], preferred_element_type=jnp.flo...]
    all_gather x1 -> x0, waiting for transfers between devices: 20.8 us -> none  [local(): rows = lax.all_gather(pair, XY, axis=0, tiled=True)]
    reduce_scatter x1, waiting for transfers between devices: 18.5 us -> 0.01 us  [local(): lax.psum_scatter(teacher_part, 'z', scatter_dimension=0, tiled=False)]
    pallas_call x0 -> x4, Pallas kernels: none -> 12.8 us  [the longest x1 5.19 us: teacher_partial(): pl.pallas_call(teacher_kernel, grid=(units,), in_specs=[pl.BlockSpec((tok...]
    unnamed x13 -> x16, local copies, waits for them, and re-layouts: 3.25 us -> 6.91 us
  transfers between devices with their start and end apart: 7 -> 12, of which waited for: 7 -> 9; matrix products, arithmetic and copies ran while one was open for 6% -> 2% of each run, Pallas kernels for 0% -> 1%
where the time goes in v2:
time: 284 us; the launch traced here: 281 us
  blocking collectives  131 us (46%)
  waiting for transfers between devices  70.1 us (25%)
  starting transfers between devices  27.8 us (10%)
  between operations  14.4 us (5%)
  Pallas kernels  12.8 us (5%)
  local copies, waits for them, and re-layouts  12.6 us (4%)
  other arithmetic  12.6 us (4%)
    all_to_all x5, blocking collectives, exchange(): return lax.all_to_all(value, axes, 0, 0, tiled=True)  131 us
    all_to_all x5, waiting for transfers between devices, exchange(): return lax.all_to_all(value, axes, 0, 0, tiled=True)  64.4 us
    all_to_all x5, starting transfers between devices, exchange(): return lax.all_to_all(value, axes, 0, 0, tiled=True)  26.8 us
    unnamed x16, local copies, waits for them, and re-layouts  6.91 us
  transfers between devices with their start and end apart: 12, of which 9 were waited for; matrix products, arithmetic and copies ran while one was open for 2% of the time, Pallas kernels for 1%

profile of v2, /device:TPU:8, one launch (start us, length us, event | category | flops | bytes accessed | tf_op | source)
XLA Modules:
  0.0 281.3 jit_solution(6791727710769343401)
XLA Ops:
  7.2 0.7 convert_bitcast_fusion
  7.9 0.1 copy.48
  8.0 0.1 copy-done
  8.1 0.1 collective-permute-start.1
  8.2 1.0 reshape.317
  9.2 0.8 fusion.6
  10.0 0.6 collective-permute-start
  10.6 2.2 copy-done.5
  12.8 0.9 shard_map.68
  13.7 1.7 copy-done.2
  15.4 0.9 broadcast_in_dim.8
  16.3 7.4 %all-to-all-start = ((bf16[16,32,640]{2,1,0:T(8,128)(2,1)}), bf16[16,32,640]{2,1,0:T(8,128)(2,1)}, u32[]{:S(2)}, u32[]{:S(2)}) async-start(bf16[16,32,640]{2,1,0:T(8,128)(2,1)} %broadcast_in_dim.8), calls=%async_computation | async-start | bytes 1310720 | tf_op jit(solution)/shard_map/all_to_all | solution.py:28
  23.7 0.0 reduce-scatter.2.cloned.1.call-start
  23.8 11.6 %all-to-all-done = bf16[16,32,640]{2,1,0:T(8,128)(2,1)} async-done(((bf16[16,32,640]{2,1,0:T(8,128)(2,1)}), bf16[16,32,640]{2,1,0:T(8,128)(2,1)}, u32[]{:S(2)}, u32[]{:S(2)}) %all-to-all-start) | async-done | bytes 655392 | tf_op jit(solution)/shard_map/all_to_all | solution.py:28
  35.4 5.2 %shard_map.69 = f32[8,8,64,384]{3,2,1,0:T(8,128)S(1)} custom-call(bf16[512,640]{1,0:T(8,128)(2,1)} %bitcast.5.rows_ref, bf16[512,3072]{1,0:T(8,128)(2,1)S(1)} %copy-done.4), custom_call_target="tpu_custom_call" | custom-call | tf_op jit(solution)/shard_map/pallas_call | solution.py:63
  40.6 2.7 copy-done.1
  43.2 0.0 reduce-scatter.2.cloned.1.call-update
  43.3 0.2 broadcast_in_dim.9
  43.5 30.6 %all_to_all.50 = bf16[16,32,2048]{2,1,0:T(8,128)(2,1)S(1)} all-to-all(bf16[16,32,2048]{2,1,0:T(8,128)(2,1)S(1)} %broadcast_in_dim.9), channel_id=1, replica_groups=mesh['x'=4,'yh'=2,'yl'=2,'c'=2,'z'=8] {'x','yh','yl'}, dimensions={0} | all-to-all | bytes 4194304 | tf_op jit(solution)/shard_map/all_to_all | solution.py:28
  74.1 40.7 %all_to_all.51.own_ref.pair_ref = bf16[16,2,128,384]{3,2,1,0:T(8,128)(2,1)S(1)} all-to-all(bf16[16,2,128,384]{3,2,1,0:T(8,128)(2,1)S(1)} %bitcast.66), channel_id=1, replica_groups=mesh['x'=4,'yh'=2,'yl'=2,'c'=2,'z'=8] {'x','yh','yl'}, dimensions={0} | all-to-all | bytes 6291456 | tf_op jit(solution)/shard_map/all_to_all | solution.py:28
  114.8 3.2 %shard_map.70 = (f32[512,384]{1,0:T(8,128)S(1)}, f32[512,384]{1,0:T(8,128)S(1)}) custom-call(s32[1]{0:T(128)} %bitcast.core_ref, bf16[512,2048]{1,0:T(8,128)(2,1)S(1)} %bitcast.67, bf16[16,2,128,384]{3,2,1,0:T(8,128)(2,1)S(1)} %all_to_all.51.own_ref.pair_ref, bf16[16,2,128,384]{3,2,1,0:T(8,128)(2,1)S(1)} %all_to_all.51.own_ref.pair_ref), custom_call_target="tpu_custom_call" | custom-call | tf_op jit(solution)/shard_map/pallas_call | solution.py:108
  118.0 0.1 collective-permute-start.2
  118.1 2.3 collective-permute-done.2
  120.4 1.0 add.206
  121.4 8.5 %all-to-all-start.3 = ((f32[8,64,384]{2,1,0:T(8,128)}), f32[8,64,384]{2,1,0:T(8,128)}, u32[]{:S(2)}, u32[]{:S(2)}) async-start(f32[8,64,384]{2,1,0:T(8,128)} %bitcast.71), calls=%async_computation.3 | async-start | bytes 1572864 | tf_op jit(solution)/shard_map/all_to_all | solution.py:28
  129.9 23.5 %all-to-all-done.3 = f32[8,64,384]{2,1,0:T(8,128)} async-done(((f32[8,64,384]{2,1,0:T(8,128)}), f32[8,64,384]{2,1,0:T(8,128)}, u32[]{:S(2)}, u32[]{:S(2)}) %all-to-all-start.3) | async-done | bytes 786464 | tf_op jit(solution)/shard_map/all_to_all | solution.py:28
  153.4 4.2 %all-to-all-start.4 = ((f32[8,64,384]{2,1,0:T(8,128)}), f32[8,64,384]{2,1,0:T(8,128)}, u32[]{:S(2)}, u32[]{:S(2)}) async-start(f32[8,64,384]{2,1,0:T(8,128)} %bitcast.72), calls=%async_computation.5 | async-start | bytes 1572864 | tf_op jit(solution)/shard_map/all_to_all | solution.py:28
  157.6 0.1 iota_add_fusion
  157.7 0.7 dynamic-slice_convert_fusion
  158.4 0.2 fusion.9
  158.6 1.3 reduce_max.54
  159.9 11.3 %all-to-all-done.4 = f32[8,64,384]{2,1,0:T(8,128)} async-done(((f32[8,64,384]{2,1,0:T(8,128)}), f32[8,64,384]{2,1,0:T(8,128)}, u32[]{:S(2)}, u32[]{:S(2)}) %all-to-all-start.4) | async-done | bytes 786464 | tf_op jit(solution)/shard_map/all_to_all | solution.py:28
  171.2 1.3 reduce_max.55
  172.5 2.8 multiply_reduce_fusion
  175.3 0.1 collective-permute-start.3
  175.4 1.2 collective-permute-done.3
  176.7 0.1 reshape.338
  176.8 11.5 %all_to_all.52 = f32[16,1,384]{2,1,0:T(1,128)S(1)} all-to-all(f32[16,1,384]{2,1,0:T(1,128)S(1)} %reshape.338), channel_id=1, replica_groups=mesh['x'=4,'yh'=2,'yl'=2,'c'=2,'z'=8] {'x','yh','yl'}, dimensions={0} | all-to-all | bytes 49152 | tf_op jit(solution)/shard_map/all_to_all | solution.py:28
  188.3 0.5 broadcast.222
  188.8 0.7 reduce.18
  189.5 0.1 reshape.339
  189.7 1.7 fusion.4
  191.5 16.3 %all_to_all.53 = bf16[8,64,384]{2,1,0:T(8,128)(2,1)S(1)} all-to-all(bf16[8,64,384]{2,1,0:T(8,128)(2,1)S(1)} %fusion.4), channel_id=1, replica_groups=mesh['x'=4,'yh'=2,'yl'=2,'c'=2,'z'=8] {'z'}, dimensions={0} | all-to-all | bytes 786432 | tf_op jit(solution)/shard_map/all_to_all | solution.py:28
  207.7 1.7 collective-permute-done.4.pair_grad_ref
  209.4 3.5 %shard_map.71 = bf16[512,2048]{1,0:T(8,128)(2,1)S(1)} custom-call(s32[1]{0:T(128)} %bitcast.core_ref, bf16[512,384]{1,0:T(8,128)(2,1)S(1)} %bitcast.70, bf16[512,384]{1,0:T(8,128)(2,1)S(1)} %collective-permute-done.4.pair_grad_ref, bf16[16,2,128,384]{3,2,1,0:T(8,128)(2,1)S(1)} %all_to_all.51.own_ref.pair_ref, ...), custom_call_target="tpu_custom_call" | custom-call | tf_op jit(solution)/shard_map/pallas_call | solution.py:140
  212.9 32.0 %all_to_all.54 = bf16[16,32,2048]{2,1,0:T(8,128)(2,1)S(1)} all-to-all(bf16[16,32,2048]{2,1,0:T(8,128)(2,1)S(1)} %bitcast.68), channel_id=1, replica_groups=mesh['x'=4,'yh'=2,'yl'=2,'c'=2,'z'=8] {'x','yh','yl'}, dimensions={0} | all-to-all | bytes 4194304 | tf_op jit(solution)/shard_map/all_to_all | solution.py:28
  244.9 0.4 reduce_sum.142
  245.3 0.7 reshape.323
  246.0 3.4 %all-to-all-start.8 = ((bf16[8,4,2048]{2,1,0:T(4,128)(2,1)}), bf16[8,4,2048]{2,1,0:T(4,128)(2,1)S(1)}, u32[]{:S(2)}, u32[]{:S(2)}) async-start(bf16[8,4,2048]{2,1,0:T(4,128)(2,1)} %reshape.323), calls=%async_computation.9 | async-start | bytes 262144 | tf_op jit(solution)/shard_map/all_to_all | solution.py:28
  249.4 9.0 %all-to-all-done.8 = bf16[8,4,2048]{2,1,0:T(4,128)(2,1)S(1)} async-done(((bf16[8,4,2048]{2,1,0:T(4,128)(2,1)}), bf16[8,4,2048]{2,1,0:T(4,128)(2,1)S(1)}, u32[]{:S(2)}, u32[]{:S(2)}) %all-to-all-start.8) | async-done | bytes 131104 | tf_op jit(solution)/shard_map/all_to_all | solution.py:28
  258.4 0.1 reduce_sum.143
  258.5 0.7 broadcast_in_dim.11
  259.2 3.4 %all-to-all-start.9 = ((bf16[8,4,2176]{2,1,0:T(4,128)(2,1)}), bf16[8,4,2176]{2,1,0:T(4,128)(2,1)S(1)}, u32[]{:S(2)}, u32[]{:S(2)}) async-start(bf16[8,4,2176]{2,1,0:T(4,128)(2,1)} %broadcast_in_dim.11), calls=%async_computation.10 | async-start | bytes 278528 | tf_op jit(solution)/shard_map/all_to_all | solution.py:28
  262.6 9.1 %all-to-all-done.9 = bf16[8,4,2176]{2,1,0:T(4,128)(2,1)S(1)} async-done(((bf16[8,4,2176]{2,1,0:T(4,128)(2,1)}), bf16[8,4,2176]{2,1,0:T(4,128)(2,1)S(1)}, u32[]{:S(2)}, u32[]{:S(2)}) %all-to-all-start.9) | async-done | bytes 139296 | tf_op jit(solution)/shard_map/all_to_all | solution.py:28
  271.6 0.1 broadcast_select_fusion.5
  271.7 0.1 collective-permute-start.5
  271.9 0.1 add.229
  271.9 0.1 select_n.148
  272.0 0.6 dynamic_slice.11
  272.6 0.4 collective-permute-done.5
  273.0 0.1 reshape.327
  273.2 0.3 broadcast_select_fusion.1
  273.4 0.3 pad_maximum_fusion.1
  273.7 0.7 reshape.325
  (39 shorter events, 0.5 us)
Async XLA Ops:
  7.2 0.9 copy-start
  8.1 7.3 %collective-permute-start.1 = (bf16[16,640]{1,0:T(8,128)(2,1)S(1)}, bf16[16,640]{1,0:T(8,128)(2,1)S(1)}, u32[]{:S(2)}, u32[]{:S(2)}) collective-permute-start(bf16[16,640]{1,0:T(8,128)(2,1)S(1)} %fusion.11), channel_id=1, source_target_pairs={{0,8},{8,0},{1,9},{9,1},{2,10},{10,2},{3,11},{11,3},{4,12},{12,4},... | collective-permute-start | bytes 61448 | tf_op jit(solution)/shard_map/ppermute | solution.py:17
  10.0 25.4 %copy-start.4 = (bf16[512,3072]{1,0:T(8,128)(2,1)S(1)}, bf16[512,3072]{1,0:T(8,128)(2,1)}, u32[]{:S(2)}) copy-start(bf16[512,3072]{1,0:T(8,128)(2,1)} %cols_ref.1) | copy-start | bytes 9437188
  10.0 13.7 %collective-permute-start = (bf16[16,2048]{1,0:T(8,128)(2,1)S(1)}, bf16[16,2048]{1,0:T(8,128)(2,1)S(1)}, u32[]{:S(2)}, u32[]{:S(2)}) collective-permute-start(bf16[16,2048]{1,0:T(8,128)(2,1)S(1)} %bitcast.79), channel_id=1, source_target_pairs={{0,8},{8,0},{1,9},{9,1},{2,10},{10,2},{3,11},{11,3},{4,12},{12,4},... | collective-permute-start | bytes 196616 | tf_op jit(solution)/shard_map/ppermute | solution.py:17
  10.6 2.2 copy-start.5
  13.7 1.7 copy-start.2
  16.3 19.1 %all-to-all-start = ((bf16[16,32,640]{2,1,0:T(8,128)(2,1)}), bf16[16,32,640]{2,1,0:T(8,128)(2,1)}, u32[]{:S(2)}, u32[]{:S(2)}) async-start(bf16[16,32,640]{2,1,0:T(8,128)(2,1)} %broadcast_in_dim.8), calls=%async_computation | async-start | bytes 1310720 | tf_op jit(solution)/shard_map/all_to_all | solution.py:28
  23.7 106.2 %reduce-scatter.2.cloned.1.call-start = ((), (), s32[]{:S(2)}) async-start(), calls=%async_computation.11 | async-start | bytes 7077888 | tf_op jit(solution)/shard_map/reduce_scatter | solution.py:193
  40.6 2.7 copy-start.1
  43.3 30.9 %copy-start.3 = (bf16[8,2,2,128,384]{4,3,2,1,0:T(8,128)(2,1)S(1)}, bf16[8,2,2,128,384]{4,3,2,1,0:T(8,128)(2,1)}, u32[]{:S(2)}) copy-start(bf16[8,2,2,128,384]{4,3,2,1,0:T(8,128)(2,1)} %copy-done.2) | copy-start | bytes 9437188
  118.0 2.4 collective-permute-start.2
  121.4 32.0 %all-to-all-start.3 = ((f32[8,64,384]{2,1,0:T(8,128)}), f32[8,64,384]{2,1,0:T(8,128)}, u32[]{:S(2)}, u32[]{:S(2)}) async-start(f32[8,64,384]{2,1,0:T(8,128)} %bitcast.71), calls=%async_computation.3 | async-start | bytes 1572864 | tf_op jit(solution)/shard_map/all_to_all | solution.py:28
  153.4 17.8 %all-to-all-start.4 = ((f32[8,64,384]{2,1,0:T(8,128)}), f32[8,64,384]{2,1,0:T(8,128)}, u32[]{:S(2)}, u32[]{:S(2)}) async-start(f32[8,64,384]{2,1,0:T(8,128)} %bitcast.72), calls=%async_computation.5 | async-start | bytes 1572864 | tf_op jit(solution)/shard_map/all_to_all | solution.py:28
  175.3 1.3 collective-permute-start.3
  207.7 1.7 collective-permute-start.4
  246.0 12.4 %all-to-all-start.8 = ((bf16[8,4,2048]{2,1,0:T(4,128)(2,1)}), bf16[8,4,2048]{2,1,0:T(4,128)(2,1)S(1)}, u32[]{:S(2)}, u32[]{:S(2)}) async-start(bf16[8,4,2048]{2,1,0:T(4,128)(2,1)} %reshape.323), calls=%async_computation.9 | async-start | bytes 262144 | tf_op jit(solution)/shard_map/all_to_all | solution.py:28
  259.2 12.5 %all-to-all-start.9 = ((bf16[8,4,2176]{2,1,0:T(4,128)(2,1)}), bf16[8,4,2176]{2,1,0:T(4,128)(2,1)S(1)}, u32[]{:S(2)}, u32[]{:S(2)}) async-start(bf16[8,4,2176]{2,1,0:T(4,128)(2,1)} %broadcast_in_dim.11), calls=%async_computation.10 | async-start | bytes 278528 | tf_op jit(solution)/shard_map/all_to_all | solution.py:28
  271.7 1.3 collective-permute-start.5
Sparse Core Ops, SparseCore 0:
  43.4 75.3 reduce-scatter.1

commit v3 on v2

--- a/solution.py
+++ b/solution.py
@@ -8,6 +8,8 @@
 ce_weight = 0.5
 digit = 64
 lanes = 128
+big_vmem = 56 * 2**20
+early_groups = 4
 XYH = ("x", "yh")
 XY = ("x", "yh", "yl")
 DP = ("x", "yh", "yl", "c")
@@ -51,26 +53,41 @@
     )
 
 
+def teacher_regroup_kernel(head_ref, out_ref):
+    out_ref[0] = head_ref[...]
+
+
+def teacher_regroup(head, unit):
+    depth, width = head.shape
+    units = width // unit
+    return pl.pallas_call(
+        teacher_regroup_kernel,
+        grid=(units,),
+        in_specs=[pl.BlockSpec((depth, unit), lambda j: (0, j))],
+        out_specs=pl.BlockSpec((1, depth, unit), lambda j: (j, 0, 0)),
+        out_shape=jax.ShapeDtypeStruct((units, depth, unit), head.dtype),
+        compiler_params=pltpu.CompilerParams(vmem_limit_bytes=big_vmem),
+    )(head)
+
+
 def teacher_kernel(rows_ref, cols_ref, out_ref):
-    part = jnp.dot(rows_ref[...], cols_ref[...], preferred_element_type=jnp.float32)
-    out_ref[:, 0] = part.reshape(out_ref.shape[0], out_ref.shape[2], out_ref.shape[3])
-
-
-def teacher_partial(rows, head, planes, unit):
-    depth, width = head.shape
+    out_ref[0] = jnp.dot(rows_ref[...], cols_ref[0], preferred_element_type=jnp.float32)
+
+
+def teacher_partial(rows, cols):
+    units, depth, unit = cols.shape
     tokens = rows.shape[0]
-    units = width // unit
     return pl.pallas_call(
         teacher_kernel,
         grid=(units,),
         in_specs=[
             pl.BlockSpec((tokens, depth), lambda j: (0, 0)),
-            pl.BlockSpec((depth, unit), lambda j: (0, j)),
+            pl.BlockSpec((1, depth, unit), lambda j: (j, 0, 0)),
         ],
-        out_specs=pl.BlockSpec((planes, 1, tokens // planes, unit), lambda j: (0, j, 0, 0)),
-        out_shape=jax.ShapeDtypeStruct((planes, units, tokens // planes, unit), jnp.float32),
-        compiler_params=pltpu.CompilerParams(vmem_limit_bytes=32 * 2**20),
-    )(rows, head)
+        out_specs=pl.BlockSpec((1, tokens, unit), lambda j: (j, 0, 0)),
+        out_shape=jax.ShapeDtypeStruct((units, tokens, unit), jnp.float32),
+        compiler_params=pltpu.CompilerParams(vmem_limit_bytes=big_vmem),
+    )(rows, cols)
 
 
 def regroup_kernel(head_ref, out_ref):
@@ -93,17 +110,22 @@
     )(head)
 
 
-def student_kernel(core_ref, rows_ref, own_ref, pair_ref, mine_ref, other_ref):
-    depth, unit = rows_ref.shape[1], mine_ref.shape[1]
+def student_kernel(core_ref, early_ref, late_ref, own_ref, pair_ref, mine_ref, other_ref):
+    unit = mine_ref.shape[1]
+    split = early_groups
     for cols_ref, out_ref in ((own_ref, mine_ref), (pair_ref, other_ref)):
-        cols = cols_ref[:, 0].reshape(depth, unit)
-        out_ref[...] = jnp.dot(rows_ref[...], cols, preferred_element_type=jnp.float32)
-
-
-def student_partial(core, rows, cols):
-    tokens, depth = rows.shape
+        first = cols_ref[:split, 0].reshape(-1, unit)
+        second = cols_ref[split:, 0].reshape(-1, unit)
+        out_ref[...] = jnp.dot(
+            early_ref[...], first, preferred_element_type=jnp.float32
+        ) + jnp.dot(late_ref[...], second, preferred_element_type=jnp.float32)
+
+
+def student_partial(core, early, late, cols):
+    tokens = early.shape[0]
     groups, _, part, unit = cols.shape
     block = 128
+    first = early_groups * part
     half = jax.ShapeDtypeStruct((tokens, unit), jnp.float32)
     return pl.pallas_call(
         student_kernel,
@@ -111,7 +133,8 @@
             num_scalar_prefetch=1,
             grid=(tokens // block,),
             in_specs=[
-                pl.BlockSpec((block, depth), lambda i, core: (i, 0)),
+                pl.BlockSpec((block, first), lambda i, core: (i, 0)),
+                pl.BlockSpec((block, groups * part - first), lambda i, core: (i, 0)),
                 pl.BlockSpec((groups, 1, part, unit), lambda i, core: (0, core[0], 0, 0)),
                 pl.BlockSpec((groups, 1, part, unit), lambda i, core: (0, 1 - core[0], 0, 0)),
             ],
@@ -119,7 +142,7 @@
         ),
         out_shape=[half, half],
         compiler_params=pltpu.CompilerParams(vmem_limit_bytes=32 * 2**20),
-    )(core, rows, cols, cols)
+    )(core, early, late, cols, cols)
 
 
 def grad_kernel(core_ref, own_grad_ref, pair_grad_ref, own_ref, pair_ref, out_ref):
@@ -167,95 +190,83 @@
     depth = teacher_head.shape[0]
     half = width // 2
 
+    by_core = student_hidden.reshape(tok, xy_count, 2, row_part)
+    even = by_core[:, :, 0].reshape(tok, half)
+    odd = by_core[:, :, 1].reshape(tok, half)
+    keep = jnp.where(core == 0, even, odd)
+    give = jnp.where(core == 0, odd, even)
     teacher_slice = lax.dynamic_slice_in_dim(teacher_hidden, plane * depth, depth, 1)
     digits = jnp.stack(
         [sampled_ids // (digit * digit), sampled_ids // digit % digit, sampled_ids % digit], axis=1
     ).astype(jnp.bfloat16)
     digits = jnp.pad(digits, ((0, 0), (0, lanes - 3)))
     shared = jnp.concatenate([teacher_slice, digits], axis=1)
-    shared = in_core_order(shared, swap_cores(shared), 0)
-    shared = spread(shared, XY).reshape(-1, depth + lanes)
-    tokens = shared.shape[0]
-    some = tokens // z_count
-
-    teacher_part = teacher_partial(shared, teacher_head, z_count, unit)
+    received = swap_cores(jnp.concatenate([shared, give], axis=1))
+    pair = in_core_order(jnp.concatenate([shared, keep], axis=1), received, 0)
+    early = early_groups * row_part
+    cut = depth + lanes + early
+    gathered = lax.all_gather(pair[:, :cut], XY, axis=0, tiled=True)
+    late_pair = pair[:, cut:]
+    tokens = gathered.shape[0]
+    early_rows = gathered[:, depth + lanes :]
+    id_digits = gathered[:, depth : depth + 3].astype(jnp.int32)
+    all_ids = (id_digits[:, 0] * digit + id_digits[:, 1]) * digit + id_digits[:, 2]
+
+    teacher_cols = exchange(teacher_regroup(teacher_head, unit), XYH)
+    teacher_part = teacher_partial(gathered[:, :depth], teacher_cols)
+    student_head, late_pair, teacher_part = lax.optimization_barrier(
+        (student_head, late_pair, teacher_part)
+    )
+    teacher_logits = lax.psum_scatter(teacher_part, "z", scatter_dimension=0, tiled=False)
 
     parts = regroup(student_head, z_count, unit).reshape(xy_count, 2, row_part, unit)
-    by_core = student_hidden.reshape(tok, xy_count, 2, row_part)
-    even = by_core[:, :, 0].reshape(tok, half)
-    odd = by_core[:, :, 1].reshape(tok, half)
-    received = swap_cores(jnp.where(core == 0, odd, even))
-    student_pair = in_core_order(jnp.where(core == 0, even, odd), received, 0)
-
-    parts, student_pair, teacher_part = lax.optimization_barrier(
-        (parts, student_pair, teacher_part)
-    )
-    teacher_own = lax.psum_scatter(teacher_part, "z", scatter_dimension=0, tiled=False)
-
     student_cols = exchange(parts, XY)
-    student_rows = spread(student_pair, XY).reshape(tokens, half)
-    teacher_own, _ = lax.optimization_barrier((teacher_own, (student_rows, student_cols)))
-    teacher_logits = exchange(teacher_own, XYH)
-
-    mine, other = student_partial(core_id, student_rows, student_cols)
-    student_logits = exchange((mine + swap_cores(other)).reshape(z_count, some, unit), "z")
+    late_rows = spread(late_pair, XY).reshape(tokens, half - early)
+    mine, other = student_partial(core_id, early_rows, late_rows, student_cols)
+    student_logits = mine + swap_cores(other)
 
     xyh = lax.axis_index("x") * 2 + lax.axis_index("yh")
-    planes = jnp.arange(z_count, dtype=jnp.int32)
-    owner = (planes * 2 + lax.axis_index("yl")) * 2 + core
-    column_ids = ((owner * z_count + xyh) * unit)[:, None] + jnp.arange(unit, dtype=jnp.int32)
-    id_digits = lax.dynamic_slice_in_dim(shared, plane * some, some, 0)[:, depth : depth + 3]
-    id_digits = id_digits.astype(jnp.int32)
-    ids = (id_digits[:, 0] * digit + id_digits[:, 1]) * digit + id_digits[:, 2]
-    hit_mask = (column_ids[:, None, :] == ids[None, :, None]).astype(jnp.float32)
+    owner = (plane * 2 + lax.axis_index("yl")) * 2 + core
+    column_ids = (owner * z_count + xyh) * unit + jnp.arange(unit, dtype=jnp.int32)
+    hit_mask = (column_ids[None, :] == all_ids[:, None]).astype(jnp.float32)
 
     logit_gap = student_logits - teacher_logits
-    student_top = jnp.max(student_logits, axis=(0, 2))
-    teacher_top = jnp.max(teacher_logits, axis=(0, 2))
+    student_top = jnp.max(student_logits, axis=1)
+    teacher_top = jnp.max(teacher_logits, axis=1)
     student_exp = jnp.exp(student_logits - student_top[:, None])
     teacher_exp = jnp.exp(teacher_logits - teacher_top[:, None])
     stats = jnp.stack(
         [
             student_top,
             teacher_top,
-            jnp.sum(student_exp, axis=(0, 2)),
-            jnp.sum(teacher_exp, axis=(0, 2)),
-            jnp.sum(student_exp * logit_gap, axis=(0, 2)),
-            jnp.sum(hit_mask * student_logits, axis=(0, 2)),
+            jnp.sum(student_exp, axis=1),
+            jnp.sum(teacher_exp, axis=1),
+            jnp.sum(student_exp * logit_gap, axis=1),
+            jnp.sum(hit_mask * student_logits, axis=1),
         ]
     )
     stats = merge(jnp.stack([stats, swap_cores(stats)]))
     stats = merge(spread(stats, XY))
+    stats = merge(spread(stats, "z"))
     student_norm = stats[0] + jnp.log(stats[2])
     teacher_norm = stats[1] + jnp.log(stats[3])
     expected_gap = stats[4] / stats[2]
     divergence = expected_gap - student_norm + teacher_norm
-    losses = divergence + ce_weight * (student_norm - stats[5])
+    every_loss = divergence + ce_weight * (student_norm - stats[5])
+    token_loss = lax.dynamic_slice_in_dim(every_loss, lax.axis_index(DP) * tok, tok, 0)
 
     student_prob = jnp.exp(student_logits - student_norm[:, None])
     logit_grad = (
         student_prob * (logit_gap - expected_gap[:, None])
         + ce_weight * (student_prob - hit_mask)
     ).astype(jnp.bfloat16)
-    logit_grad = exchange(logit_grad, "z").reshape(tokens, unit)
     grad_part = grad_partial(core_id, logit_grad, swap_cores(logit_grad), student_cols)
     grad_part = grad_part.reshape(xy_count, 2 * tok, half)
     plane_sum = jnp.sum(exchange(grad_part, XY).astype(jnp.float32), axis=0)
     plane_part = plane_sum.astype(jnp.bfloat16).reshape(z_count, -1, half)
     total = jnp.sum(exchange(plane_part, "z").astype(jnp.float32), axis=0).astype(jnp.bfloat16)
 
-    high = losses.astype(jnp.bfloat16)
-    rest = losses - high.astype(jnp.float32)
-    middle = rest.astype(jnp.bfloat16)
-    low = (rest - middle.astype(jnp.float32)).astype(jnp.bfloat16)
-    terms = jnp.pad(
-        jnp.stack([high, middle, low]), ((0, total.shape[0] - 3), (0, lanes - some))
-    )
-    final = spread(jnp.concatenate([total, terms], axis=1), "z")
-    term = final[:, :3, half : half + some].astype(jnp.float32)
-    every_loss = ((term[:, 2] + term[:, 1]) + term[:, 0]).reshape(tokens)
-    token_loss = lax.dynamic_slice_in_dim(every_loss, lax.axis_index(DP) * tok, tok, 0)
-    grads = final[:, :, :half].reshape(2, tok, half)
+    grads = spread(total, "z").reshape(2, tok, half)
     mine = jnp.where(core == 0, grads[0], grads[1])
     other = swap_cores(jnp.where(core == 0, grads[1], grads[0]))
     grad_hidden = in_core_order(

time: 284 us -> 296 us (1.042)
  waiting for transfers between devices: 70.1 us -> 93.9 us
  starting transfers between devices: 27.8 us -> 12.3 us
  Pallas kernels: 12.8 us -> 22.7 us
  blocking collectives: 131 us -> 124 us
    all_gather x0 -> x1, waiting for transfers between devices: none -> 72.1 us  [local(): gathered = lax.all_gather(pair[:, :cut], XY, axis=0, tiled=True)]
    all_to_all x5 -> x2, waiting for transfers between devices: 64.4 us -> 17.1 us  [exchange(): return lax.all_to_all(value, axes, 0, 0, tiled=True)]
    all_to_all x5 -> x2, starting transfers between devices: 26.8 us -> 11.7 us  [exchange(): return lax.all_to_all(value, axes, 0, 0, tiled=True)]
    all_to_all x5 -> x6, blocking collectives: 131 us -> 124 us  [exchange(): return lax.all_to_all(value, axes, 0, 0, tiled=True)]
    pallas_call x0 -> x1, Pallas kernels: none -> 6.15 us  [teacher_regroup(): pl.pallas_call(teacher_regroup_kernel, grid=(units,), in_specs=[pl.BlockS...]
    pallas_call x1, Pallas kernels: 5.19 us -> 8.36 us  [teacher_partial(): pl.pallas_call(teacher_kernel, grid=(units,), in_specs=[pl.BlockSpec((tok...]
    unnamed x16 -> x19, local copies, waits for them, and re-layouts: 6.91 us -> 7.4 us
  transfers between devices with their start and end apart: 12 -> 9, of which waited for: 9 -> 6; matrix products, arithmetic and copies ran while one was open for 2% -> 3% of each run, Pallas kernels for 1% -> 4%
where the time goes in v3:
time: 296 us; the launch traced here: 293 us
  blocking collectives  124 us (42%)
  waiting for transfers between devices  93.9 us (32%)
  Pallas kernels  22.7 us (8%)
  between operations  14.3 us (5%)
  local copies, waits for them, and re-layouts  14.1 us (5%)
  starting transfers between devices  12.3 us (4%)
  other arithmetic  11.2 us (4%)
    all_to_all x6, blocking collectives, exchange(): return lax.all_to_all(value, axes, 0, 0, tiled=True)  124 us
    all_gather x1, waiting for transfers between devices, local(): gathered = lax.all_gather(pair[:, :cut], XY, axis=0, tiled=True)  72.1 us
    all_to_all x2, waiting for transfers between devices, exchange(): return lax.all_to_all(value, axes, 0, 0, tiled=True)  17.1 us
    all_to_all x2, starting transfers between devices, exchange(): return lax.all_to_all(value, axes, 0, 0, tiled=True)  11.7 us
    pallas_call x1, Pallas kernels, teacher_partial(): pl.pallas_call(teacher_kernel, grid=(units,), in_specs=[pl.BlockSpec((tok...  8.36 us
    unnamed x19, local copies, waits for them, and re-layouts  7.4 us
    pallas_call x1, Pallas kernels, teacher_regroup(): pl.pallas_call(teacher_regroup_kernel, grid=(units,), in_specs=[pl.BlockS...  6.15 us
  transfers between devices with their start and end apart: 9, of which 6 were waited for; matrix products, arithmetic and copies ran while one was open for 3% of the time, Pallas kernels for 4%

profile of v3, /device:TPU:8, one launch (start us, length us, event | category | flops | bytes accessed | tf_op | source)
XLA Modules:
  0.0 292.8 jit_solution(13526035340495210785)
XLA Ops:
  7.2 0.0 copy-start
  7.2 0.7 convert_bitcast_fusion
  7.9 0.1 copy.61
  8.0 1.0 reshape.125
  9.0 0.2 fusion.56
  9.2 0.0 copy-done
  9.3 0.1 collective-permute-start
  9.4 6.1 %shard_map.68 = bf16[8,512,384]{2,1,0:T(8,128)(2,1)} custom-call(bf16[512,3072]{1,0:T(8,128)(2,1)} %head_ref.1), custom_call_target="tpu_custom_call" | custom-call | tf_op jit(solution)/shard_map/pallas_call | solution.py:63
  15.5 6.0 %all-to-all-start = ((bf16[8,512,384]{2,1,0:T(8,128)(2,1)}), bf16[8,512,384]{2,1,0:T(8,128)(2,1)S(1)}, u32[]{:S(2)}, u32[]{:S(2)}) async-start(bf16[8,512,384]{2,1,0:T(8,128)(2,1)} %shard_map.68), calls=%async_computation | async-start | bytes 6291456 | tf_op jit(solution)/shard_map/all_to_all | solution.py:30
  21.6 0.0 all-gather.2.cloned.1.call-start
  21.6 0.0 collective-permute-done
  21.7 0.6 pad_maximum_fusion.4
  22.3 0.0 all-gather.2.cloned.1.call-update
  22.4 0.0 reduce-scatter.2.cloned.1.call-start
  22.4 72.1 %all-gather.2.cloned.1.call-done = bf16[512,1152]{1,0:T(8,128)(2,1)} async-done(((bf16[32,1152]{1,0:T(8,128)(2,1)}), bf16[512,1152]{1,0:T(8,128)(2,1)}) %all-gather.2.cloned.1.call-update) | async-done | bytes 1179664 | tf_op jit(solution)/shard_map/all_gather | solution.py:208
  94.5 2.3 fusion.53
  96.8 0.0 all-to-all-done.cols_ref
  96.8 0.0 copy-start.7
  96.8 1.7 copy-done.7
  98.5 8.4 %shard_map.69 = f32[8,512,384]{2,1,0:T(8,128)} custom-call(bf16[512,512]{1,0:T(8,128)(2,1)} %get-tuple-element.38.rows_ref, bf16[8,512,384]{2,1,0:T(8,128)(2,1)} %copy-done.7), custom_call_target="tpu_custom_call" | custom-call | tf_op jit(solution)/shard_map/pallas_call | solution.py:80
  106.9 0.0 reduce-scatter.2.cloned.1.call-update
  106.9 1.3 broadcast_in_dim.8
  108.3 5.7 %all-to-all-start.1 = ((bf16[16,32,1536]{2,1,0:T(8,128)(2,1)}), bf16[16,32,1536]{2,1,0:T(8,128)(2,1)S(1)}, u32[]{:S(2)}, u32[]{:S(2)}) async-start(bf16[16,32,1536]{2,1,0:T(8,128)(2,1)} %broadcast_in_dim.8), calls=%async_computation.1 | async-start | bytes 3145728 | tf_op jit(solution)/shard_map/all_to_all | solution.py:30
  114.0 0.0 copy-start.4
  114.0 1.9 copy-done.4
  115.8 0.9 shard_map.70
  116.8 0.0 copy-start.1
  116.8 1.7 copy-done.1
  118.5 17.1 %all-to-all-done.1 = bf16[16,32,1536]{2,1,0:T(8,128)(2,1)S(1)} async-done(((bf16[16,32,1536]{2,1,0:T(8,128)(2,1)}), bf16[16,32,1536]{2,1,0:T(8,128)(2,1)S(1)}, u32[]{:S(2)}, u32[]{:S(2)}) %all-to-all-start.1) | async-done | bytes 1572896 | tf_op jit(solution)/shard_map/all_to_all | solution.py:30
  135.5 1.2 copy-done.2
  136.7 40.9 %all_to_all.40.own_ref.pair_ref = bf16[16,2,128,384]{3,2,1,0:T(8,128)(2,1)S(1)} all-to-all(bf16[16,2,128,384]{3,2,1,0:T(8,128)(2,1)} %bitcast.148), channel_id=1, replica_groups=mesh['x'=4,'yh'=2,'yl'=2,'c'=2,'z'=8] {'x','yh','yl'}, dimensions={0} | all-to-all | bytes 6291456 | tf_op jit(solution)/shard_map/all_to_all | solution.py:30
  177.6 0.0 copy-done.3
  177.6 0.0 copy-done.5
  177.6 3.9 %shard_map.71 = (f32[512,384]{1,0:T(8,128)S(1)}, f32[512,384]{1,0:T(8,128)}) custom-call(s32[1]{0:T(128)} %bitcast.core_ref, bf16[512,512]{1,0:T(8,128)(2,1)S(1)} %copy-done.5, bf16[512,1536]{1,0:T(8,128)(2,1)S(1)} %bitcast.150, bf16[16,2,128,384]{3,2,1,0:T(8,128)(2,1)S(1)} %all_to_all.40.own_ref.pair_ref, ...), custom_call_target="tpu_custom_call" | custom-call | tf_op jit(solution)/shard_map/pallas_call | solution.py:130
  181.4 0.9 copy-done.6
  182.3 0.0 collective-permute-start.1
  182.3 0.9 slice_convert_fusion
  183.3 0.3 fusion.8
  183.6 1.4 collective-permute-done.1
  184.9 2.4 fusion.52
  187.3 1.3 reduce_max.73
  188.6 2.1 multiply_reduce_fusion
  190.8 0.2 collective-permute-start.2
  191.0 1.0 collective-permute-done.2
  192.2 12.3 %all_to_all.41 = f32[16,6,512]{2,1,0:T(8,128)S(1)} all-to-all(f32[16,6,512]{2,1,0:T(8,128)S(1)} %broadcast_in_dim.9), channel_id=1, replica_groups=mesh['x'=4,'yh'=2,'yl'=2,'c'=2,'z'=8] {'x','yh','yl'}, dimensions={0} | all-to-all | bytes 393216 | tf_op jit(solution)/shard_map/all_to_all | solution.py:30
  204.5 0.2 fusion.54
  204.8 15.9 %all_to_all.42 = f32[8,6,512]{2,1,0:T(8,128)S(1)} all-to-all(f32[8,6,512]{2,1,0:T(8,128)S(1)} %broadcast_in_dim.10), channel_id=1, replica_groups=mesh['x'=4,'yh'=2,'yl'=2,'c'=2,'z'=8] {'z'}, dimensions={0} | all-to-all | bytes 196608 | tf_op jit(solution)/shard_map/all_to_all | solution.py:30
  220.7 0.1 fusion.55
  220.9 1.7 fusion.4.own_grad_ref
  222.6 0.1 collective-permute-start.3
  222.7 1.7 collective-permute-done.3.pair_grad_ref
  224.4 3.5 %shard_map.72 = bf16[512,2048]{1,0:T(8,128)(2,1)S(1)} custom-call(s32[1]{0:T(128)} %bitcast.core_ref, bf16[512,384]{1,0:T(8,128)(2,1)S(1)} %fusion.4.own_grad_ref, bf16[512,384]{1,0:T(8,128)(2,1)S(1)} %collective-permute-done.3.pair_grad_ref, bf16[16,2,128,384]{3,2,1,0:T(8,128)(2,1)S(1)} %all_to_all.40.own_ref.pair_ref, ...), custom_call_target="tpu_custom_call" | custom-call | tf_op jit(solution)/shard_map/pallas_call | solution.py:163
  227.9 32.2 %all_to_all.43 = bf16[16,32,2048]{2,1,0:T(8,128)(2,1)S(1)} all-to-all(bf16[16,32,2048]{2,1,0:T(8,128)(2,1)S(1)} %bitcast.149), channel_id=1, replica_groups=mesh['x'=4,'yh'=2,'yl'=2,'c'=2,'z'=8] {'x','yh','yl'}, dimensions={0} | all-to-all | bytes 4194304 | tf_op jit(solution)/shard_map/all_to_all | solution.py:30
  260.1 0.4 reduce_sum.182
  260.5 0.1 reshape.129
  260.6 11.5 %all_to_all.44 = bf16[8,4,2048]{2,1,0:T(4,128)(2,1)S(1)} all-to-all(bf16[8,4,2048]{2,1,0:T(4,128)(2,1)S(1)} %reshape.129), channel_id=1, replica_groups=mesh['x'=4,'yh'=2,'yl'=2,'c'=2,'z'=8] {'z'}, dimensions={0} | all-to-all | bytes 262144 | tf_op jit(solution)/shard_map/all_to_all | solution.py:30
  272.0 0.1 reduce_sum.183
  272.1 11.5 %all_to_all.45 = bf16[8,4,2048]{2,1,0:T(4,128)(2,1)S(1)} all-to-all(bf16[8,4,2048]{2,1,0:T(4,128)(2,1)S(1)} %broadcast_in_dim.11), channel_id=1, replica_groups=mesh['x'=4,'yh'=2,'yl'=2,'c'=2,'z'=8] {'z'}, dimensions={0} | all-to-all | bytes 262144 | tf_op jit(solution)/shard_map/all_to_all | solution.py:30
  283.6 0.1 broadcast_select_fusion.2
  283.7 0.1 collective-permute-start.4
  283.8 0.6 dynamic_slice.7
  284.4 0.6 collective-permute-done.4
  285.1 0.1 copy.72
  285.2 0.7 reshape.131
  (33 shorter events, 0.6 us)
Async XLA Ops:
  7.2 2.1 copy-start
  9.3 12.4 %collective-permute-start = (bf16[16,2688]{1,0:T(8,128)(2,1)S(1)}, bf16[16,2688]{1,0:T(8,128)(2,1)S(1)}, u32[]{:S(2)}, u32[]{:S(2)}) collective-permute-start(bf16[16,2688]{1,0:T(8,128)(2,1)S(1)} %pad_maximum_fusion.3), channel_id=1, source_target_pairs={{0,8},{8,0},{1,9},{9,1},{2,10},{10,2},{3,11},{11,3},{4,12},{12,4},... | collective-permute-start | bytes 258056 | tf_op jit(solution)/shard_map/ppermute | solution.py:19
  15.5 81.3 %all-to-all-start = ((bf16[8,512,384]{2,1,0:T(8,128)(2,1)}), bf16[8,512,384]{2,1,0:T(8,128)(2,1)S(1)}, u32[]{:S(2)}, u32[]{:S(2)}) async-start(bf16[8,512,384]{2,1,0:T(8,128)(2,1)} %shard_map.68), calls=%async_computation | async-start | bytes 6291456 | tf_op jit(solution)/shard_map/all_to_all | solution.py:30
  21.6 73.0 %all-gather.2.cloned.1.call-start = ((), (), s32[]{:S(2)}) async-start(), calls=%async_computation.9 | async-start | bytes 1253376 | tf_op jit(solution)/shard_map/all_gather | solution.py:208
  22.4 165.0 %reduce-scatter.2.cloned.1.call-start = ((), (), s32[]{:S(2)}) async-start(), calls=%async_computation.10 | async-start | bytes 7077888 | tf_op jit(solution)/shard_map/reduce_scatter | solution.py:220
  96.8 1.7 copy-start.7
  108.3 27.3 %all-to-all-start.1 = ((bf16[16,32,1536]{2,1,0:T(8,128)(2,1)}), bf16[16,32,1536]{2,1,0:T(8,128)(2,1)S(1)}, u32[]{:S(2)}, u32[]{:S(2)}) async-start(bf16[16,32,1536]{2,1,0:T(8,128)(2,1)} %broadcast_in_dim.8), calls=%async_computation.1 | async-start | bytes 3145728 | tf_op jit(solution)/shard_map/all_to_all | solution.py:30
  114.0 1.9 copy-start.4
  116.8 1.7 copy-start.1
  135.5 1.2 copy-start.2
  136.7 40.9 %copy-start.3 = (bf16[16,32,1536]{2,1,0:T(8,128)(2,1)S(1)}, bf16[16,32,1536]{2,1,0:T(8,128)(2,1)}, u32[]{:S(2)}) copy-start(bf16[16,32,1536]{2,1,0:T(8,128)(2,1)} %copy-done.2) | copy-start | bytes 4718596
  136.7 40.9 %copy-start.5 = (bf16[512,512]{1,0:T(8,128)(2,1)S(1)}, bf16[512,512]{1,0:T(8,128)(2,1)}, u32[]{:S(2)}) copy-start(bf16[512,512]{1,0:T(8,128)(2,1)} %get-tuple-element.39.early_ref) | copy-start | bytes 1572868
  181.4 0.9 copy-start.6
  182.3 2.6 collective-permute-start.1
  190.8 1.3 collective-permute-start.2
  222.6 1.8 collective-permute-start.3
  283.7 1.3 collective-permute-start.4
Sparse Core Ops, SparseCore 0:
  25.4 69.0 all-gather.1
  107.1 74.8 reduce-scatter.1

commit v4 on v2

--- a/solution.py
+++ b/solution.py
@@ -8,6 +8,7 @@
 ce_weight = 0.5
 digit = 64
 lanes = 128
+big_vmem = 56 * 2**20
 XYH = ("x", "yh")
 XY = ("x", "yh", "yl")
 DP = ("x", "yh", "yl", "c")
@@ -52,8 +53,10 @@
 
 
 def teacher_kernel(rows_ref, cols_ref, out_ref):
+    planes, pair, some, unit = out_ref.shape
     part = jnp.dot(rows_ref[...], cols_ref[...], preferred_element_type=jnp.float32)
-    out_ref[:, 0] = part.reshape(out_ref.shape[0], out_ref.shape[2], out_ref.shape[3])
+    for j in range(pair):
+        out_ref[:, j] = part[:, j * unit : (j + 1) * unit].reshape(planes, some, unit)
 
 
 def teacher_partial(rows, head, planes, unit):
@@ -62,14 +65,14 @@
     units = width // unit
     return pl.pallas_call(
         teacher_kernel,
-        grid=(units,),
+        grid=(units // 2,),
         in_specs=[
             pl.BlockSpec((tokens, depth), lambda j: (0, 0)),
-            pl.BlockSpec((depth, unit), lambda j: (0, j)),
+            pl.BlockSpec((depth, 2 * unit), lambda j: (0, j)),
         ],
-        out_specs=pl.BlockSpec((planes, 1, tokens // planes, unit), lambda j: (0, j, 0, 0)),
+        out_specs=pl.BlockSpec((planes, 2, tokens // planes, unit), lambda j: (0, j, 0, 0)),
         out_shape=jax.ShapeDtypeStruct((planes, units, tokens // planes, unit), jnp.float32),
-        compiler_params=pltpu.CompilerParams(vmem_limit_bytes=32 * 2**20),
+        compiler_params=pltpu.CompilerParams(vmem_limit_bytes=big_vmem),
     )(rows, head)
 
 
@@ -173,12 +176,15 @@
     ).astype(jnp.bfloat16)
     digits = jnp.pad(digits, ((0, 0), (0, lanes - 3)))
     shared = jnp.concatenate([teacher_slice, digits], axis=1)
-    shared = in_core_order(shared, swap_cores(shared), 0)
-    shared = spread(shared, XY).reshape(-1, depth + lanes)
-    tokens = shared.shape[0]
+    pair = in_core_order(shared, swap_cores(shared), 0)
+    student_hidden, student_head, pair = lax.optimization_barrier(
+        (student_hidden, student_head, pair)
+    )
+    gathered = spread(pair, XY).reshape(-1, depth + lanes)
+    tokens = gathered.shape[0]
     some = tokens // z_count
-
-    teacher_part = teacher_partial(shared, teacher_head, z_count, unit)
+    id_digits = gathered[:, depth : depth + 3].astype(jnp.int32)
+    all_ids = (id_digits[:, 0] * digit + id_digits[:, 1]) * digit + id_digits[:, 2]
 
     parts = regroup(student_head, z_count, unit).reshape(xy_count, 2, row_part, unit)
     by_core = student_hidden.reshape(tok, xy_count, 2, row_part)
@@ -186,76 +192,63 @@
     odd = by_core[:, :, 1].reshape(tok, half)
     received = swap_cores(jnp.where(core == 0, odd, even))
     student_pair = in_core_order(jnp.where(core == 0, even, odd), received, 0)
-
-    parts, student_pair, teacher_part = lax.optimization_barrier(
-        (parts, student_pair, teacher_part)
-    )
+    copies = jnp.broadcast_to(student_pair[None], (xy_count,) + student_pair.shape)
+
+    gathered, parts, copies = lax.optimization_barrier((gathered, parts, copies))
+    teacher_part = teacher_partial(gathered, teacher_head, z_count, unit)
+    parts, copies, teacher_part = lax.optimization_barrier((parts, copies, teacher_part))
     teacher_own = lax.psum_scatter(teacher_part, "z", scatter_dimension=0, tiled=False)
 
+    student_rows = exchange(copies, XY).reshape(tokens, half)
     student_cols = exchange(parts, XY)
-    student_rows = spread(student_pair, XY).reshape(tokens, half)
-    teacher_own, _ = lax.optimization_barrier((teacher_own, (student_rows, student_cols)))
-    teacher_logits = exchange(teacher_own, XYH)
-
     mine, other = student_partial(core_id, student_rows, student_cols)
-    student_logits = exchange((mine + swap_cores(other)).reshape(z_count, some, unit), "z")
+    student_logits = mine + swap_cores(other)
+
+    teacher_own, _ = lax.optimization_barrier((teacher_own, student_cols))
+    teacher_logits = exchange(exchange(teacher_own, XYH), "z").reshape(tokens, unit)
 
     xyh = lax.axis_index("x") * 2 + lax.axis_index("yh")
-    planes = jnp.arange(z_count, dtype=jnp.int32)
-    owner = (planes * 2 + lax.axis_index("yl")) * 2 + core
-    column_ids = ((owner * z_count + xyh) * unit)[:, None] + jnp.arange(unit, dtype=jnp.int32)
-    id_digits = lax.dynamic_slice_in_dim(shared, plane * some, some, 0)[:, depth : depth + 3]
-    id_digits = id_digits.astype(jnp.int32)
-    ids = (id_digits[:, 0] * digit + id_digits[:, 1]) * digit + id_digits[:, 2]
-    hit_mask = (column_ids[:, None, :] == ids[None, :, None]).astype(jnp.float32)
+    owner = (plane * 2 + lax.axis_index("yl")) * 2 + core
+    column_ids = (owner * z_count + xyh) * unit + jnp.arange(unit, dtype=jnp.int32)
+    hit_mask = (column_ids[None, :] == all_ids[:, None]).astype(jnp.float32)
 
     logit_gap = student_logits - teacher_logits
-    student_top = jnp.max(student_logits, axis=(0, 2))
-    teacher_top = jnp.max(teacher_logits, axis=(0, 2))
+    student_top = jnp.max(student_logits, axis=1)
+    teacher_top = jnp.max(teacher_logits, axis=1)
     student_exp = jnp.exp(student_logits - student_top[:, None])
     teacher_exp = jnp.exp(teacher_logits - teacher_top[:, None])
     stats = jnp.stack(
         [
             student_top,
             teacher_top,
-            jnp.sum(student_exp, axis=(0, 2)),
-            jnp.sum(teacher_exp, axis=(0, 2)),
-            jnp.sum(student_exp * logit_gap, axis=(0, 2)),
-            jnp.sum(hit_mask * student_logits, axis=(0, 2)),
+            jnp.sum(student_exp, axis=1),
+            jnp.sum(teacher_exp, axis=1),
+            jnp.sum(student_exp * logit_gap, axis=1),
+            jnp.sum(hit_mask * student_logits, axis=1),
         ]
     )
     stats = merge(jnp.stack([stats, swap_cores(stats)]))
     stats = merge(spread(stats, XY))
+    stats = merge(spread(stats, "z"))
     student_norm = stats[0] + jnp.log(stats[2])
     teacher_norm = stats[1] + jnp.log(stats[3])
     expected_gap = stats[4] / stats[2]
     divergence = expected_gap - student_norm + teacher_norm
-    losses = divergence + ce_weight * (student_norm - stats[5])
+    every_loss = divergence + ce_weight * (student_norm - stats[5])
+    token_loss = lax.dynamic_slice_in_dim(every_loss, lax.axis_index(DP) * tok, tok, 0)
 
     student_prob = jnp.exp(student_logits - student_norm[:, None])
     logit_grad = (
         student_prob * (logit_gap - expected_gap[:, None])
         + ce_weight * (student_prob - hit_mask)
     ).astype(jnp.bfloat16)
-    logit_grad = exchange(logit_grad, "z").reshape(tokens, unit)
     grad_part = grad_partial(core_id, logit_grad, swap_cores(logit_grad), student_cols)
     grad_part = grad_part.reshape(xy_count, 2 * tok, half)
     plane_sum = jnp.sum(exchange(grad_part, XY).astype(jnp.float32), axis=0)
     plane_part = plane_sum.astype(jnp.bfloat16).reshape(z_count, -1, half)
     total = jnp.sum(exchange(plane_part, "z").astype(jnp.float32), axis=0).astype(jnp.bfloat16)
 
-    high = losses.astype(jnp.bfloat16)
-    rest = losses - high.astype(jnp.float32)
-    middle = rest.astype(jnp.bfloat16)
-    low = (rest - middle.astype(jnp.float32)).astype(jnp.bfloat16)
-    terms = jnp.pad(
-        jnp.stack([high, middle, low]), ((0, total.shape[0] - 3), (0, lanes - some))
-    )
-    final = spread(jnp.concatenate([total, terms], axis=1), "z")
-    term = final[:, :3, half : half + some].astype(jnp.float32)
-    every_loss = ((term[:, 2] + term[:, 1]) + term[:, 0]).reshape(tokens)
-    token_loss = lax.dynamic_slice_in_dim(every_loss, lax.axis_index(DP) * tok, tok, 0)
-    grads = final[:, :, :half].reshape(2, tok, half)
+    grads = spread(total, "z").reshape(2, tok, half)
     mine = jnp.where(core == 0, grads[0], grads[1])
     other = swap_cores(jnp.where(core == 0, grads[1], grads[0]))
     grad_hidden = in_core_order(

time: 284 us -> 267 us (0.940)
  waiting for transfers between devices: 70.1 us -> 51.8 us
  blocking collectives: 131 us -> 141 us
  starting transfers between devices: 27.8 us -> 18 us
    all_to_all x5 -> x3, waiting for transfers between devices: 64.4 us -> 18.2 us  [exchange(): return lax.all_to_all(value, axes, 0, 0, tiled=True)]
    reduce_scatter x1, waiting for transfers between devices: 0.01 us -> 27.6 us  [local(): lax.psum_scatter(teacher_part, 'z', scatter_dimension=0, tiled=False)]
    all_to_all x5 -> x7, blocking collectives: 131 us -> 141 us  [exchange(): return lax.all_to_all(value, axes, 0, 0, tiled=True)]
    all_to_all x5 -> x3, starting transfers between devices: 26.8 us -> 17.4 us  [exchange(): return lax.all_to_all(value, axes, 0, 0, tiled=True)]
    unnamed x16 -> x10, local copies, waits for them, and re-layouts: 6.91 us -> 4.68 us
  transfers between devices with their start and end apart: 12 -> 10, of which waited for: 9 -> 8; matrix products, arithmetic and copies ran while one was open for 2% -> 2% of each run, Pallas kernels for 1% -> 2%
where the time goes in v4:
time: 267 us; the launch traced here: 264 us
  blocking collectives  141 us (53%)
  waiting for transfers between devices  51.8 us (19%)
  starting transfers between devices  18 us (7%)
  Pallas kernels  15.6 us (6%)
  between operations  14.3 us (5%)
  other arithmetic  13.1 us (5%)
  local copies, waits for them, and re-layouts  10 us (4%)
    all_to_all x7, blocking collectives, exchange(): return lax.all_to_all(value, axes, 0, 0, tiled=True)  141 us
    reduce_scatter x1, waiting for transfers between devices, local(): lax.psum_scatter(teacher_part, 'z', scatter_dimension=0, tiled=False)  27.6 us
    all_to_all x3, waiting for transfers between devices, exchange(): return lax.all_to_all(value, axes, 0, 0, tiled=True)  18.2 us
    all_to_all x3, starting transfers between devices, exchange(): return lax.all_to_all(value, axes, 0, 0, tiled=True)  17.4 us
    pallas_call x1, Pallas kernels, teacher_partial(): pl.pallas_call(teacher_kernel, grid=(units // 2,), in_specs=[pl.BlockSpec...  6.16 us
    ppermute x6, waiting for transfers between devices, swap_cores(): return lax.ppermute(value, 'c', [(0, 1), (1, 0)])  5.98 us
  transfers between devices with their start and end apart: 10, of which 8 were waited for; matrix products, arithmetic and copies ran while one was open for 2% of the time, Pallas kernels for 2%

profile of v4, /device:TPU:8, one launch (start us, length us, event | category | flops | bytes accessed | tf_op | source)
XLA Modules:
  0.0 264.1 jit_solution(15553581771977232907)
XLA Ops:
  7.2 0.0 copy-start
  7.2 0.7 convert_bitcast_fusion
  7.9 0.1 copy.93
  8.0 0.1 copy-done
  8.1 0.1 collective-permute-start
  8.2 1.2 collective-permute-done
  9.4 1.0 reshape.144
  10.4 0.8 fusion.8
  11.2 0.3 collective-permute-start.1
  11.5 0.9 broadcast_in_dim.10
  12.3 7.4 %all-to-all-start = ((bf16[16,32,640]{2,1,0:T(8,128)(2,1)}), bf16[16,32,640]{2,1,0:T(8,128)(2,1)}, u32[]{:S(2)}, u32[]{:S(2)}) async-start(bf16[16,32,640]{2,1,0:T(8,128)(2,1)} %broadcast_in_dim.10), calls=%async_computation | async-start | bytes 1310720 | tf_op jit(solution)/shard_map/all_to_all | solution.py:29
  19.7 0.0 reduce-scatter.2.cloned.1.call-start
  19.8 0.0 copy-start.2
  19.8 1.9 copy-done.2
  21.7 0.9 shard_map.68
  22.6 1.7 copy-done.1
  24.3 0.0 collective-permute-done.1
  24.3 7.6 %all-to-all-done = bf16[16,32,640]{2,1,0:T(8,128)(2,1)} async-done(((bf16[16,32,640]{2,1,0:T(8,128)(2,1)}), bf16[16,32,640]{2,1,0:T(8,128)(2,1)}, u32[]{:S(2)}, u32[]{:S(2)}) %all-to-all-start) | async-done | bytes 655392 | tf_op jit(solution)/shard_map/all_to_all | solution.py:29
  32.0 1.6 broadcast_in_dim.11
  33.5 6.2 %shard_map.69 = f32[8,8,64,384]{3,2,1,0:T(8,128)} custom-call(bf16[512,640]{1,0:T(8,128)(2,1)} %bitcast.4.rows_ref, bf16[512,3072]{1,0:T(8,128)(2,1)} %cols_ref.1), custom_call_target="tpu_custom_call" | custom-call | tf_op jit(solution)/shard_map/pallas_call | solution.py:66
  39.7 0.0 reduce-scatter.2.cloned.1.call-update
  39.7 42.4 %all_to_all.50.own_ref.pair_ref = bf16[16,2,128,384]{3,2,1,0:T(8,128)(2,1)S(1)} all-to-all(bf16[16,2,128,384]{3,2,1,0:T(8,128)(2,1)} %bitcast.142), channel_id=1, replica_groups=mesh['x'=4,'yh'=2,'yl'=2,'c'=2,'z'=8] {'x','yh','yl'}, dimensions={0} | all-to-all | bytes 6291456 | tf_op jit(solution)/shard_map/all_to_all | solution.py:29
  82.1 5.6 %all-to-all-start.1 = ((bf16[16,32,2048]{2,1,0:T(8,128)(2,1)}), bf16[16,32,2048]{2,1,0:T(8,128)(2,1)}, u32[]{:S(2)}, u32[]{:S(2)}) async-start(bf16[16,32,2048]{2,1,0:T(8,128)(2,1)} %broadcast_in_dim.11), calls=%async_computation.1 | async-start | bytes 4194304 | tf_op jit(solution)/shard_map/all_to_all | solution.py:29
  87.7 27.6 %reduce-scatter.2.cloned.1.call-done = f32[1,8,64,384]{3,2,1,0:T(8,128)} async-done(((f32[8,8,64,384]{3,2,1,0:T(8,128)}), f32[1,8,64,384]{3,2,1,0:T(8,128)}) %reduce-scatter.2.cloned.1.call-update) | async-done | bytes 786448 | tf_op jit(solution)/shard_map/reduce_scatter | solution.py:200
  115.3 0.0 all-to-all-done.1
  115.3 20.0 %all_to_all.51 = f32[8,64,384]{2,1,0:T(8,128)} all-to-all(f32[8,64,384]{2,1,0:T(8,128)} %bitcast.144), channel_id=1, replica_groups=mesh['x'=4,'yh'=2,'yl'=2,'c'=2,'z'=8] {'x','yh'}, dimensions={0} | all-to-all | bytes 1572864 | tf_op jit(solution)/shard_map/all_to_all | solution.py:29
  135.3 4.4 %all-to-all-start.4 = ((f32[8,64,384]{2,1,0:T(8,128)}), f32[8,64,384]{2,1,0:T(8,128)}, u32[]{:S(2)}, u32[]{:S(2)}) async-start(f32[8,64,384]{2,1,0:T(8,128)} %all_to_all.51), calls=%async_computation.5 | async-start | bytes 1572864 | tf_op jit(solution)/shard_map/all_to_all | solution.py:29
  139.7 5.1 %shard_map.70 = (f32[512,384]{1,0:T(8,128)S(1)}, f32[512,384]{1,0:T(8,128)}) custom-call(s32[1]{0:T(128)} %bitcast.core_ref, bf16[512,2048]{1,0:T(8,128)(2,1)} %bitcast.6.rows_ref, bf16[16,2,128,384]{3,2,1,0:T(8,128)(2,1)S(1)} %all_to_all.50.own_ref.pair_ref, bf16[16,2,128,384]{3,2,1,0:T(8,128)(2,1)S(1)} %all_to_all.50.own_ref.pair_ref), custom_call_target="tpu_custom_call" | custom-call | tf_op jit(solution)/shard_map/pallas_call | solution.py:111
  144.7 0.9 copy-done.3
  145.6 0.9 slice_convert_fusion
  146.6 0.3 fusion.6
  146.9 1.4 collective-permute-done.2
  148.3 2.3 fusion.47
  150.6 10.5 %all-to-all-done.4 = f32[8,64,384]{2,1,0:T(8,128)} async-done(((f32[8,64,384]{2,1,0:T(8,128)}), f32[8,64,384]{2,1,0:T(8,128)}, u32[]{:S(2)}, u32[]{:S(2)}) %all-to-all-start.4) | async-done | bytes 786464 | tf_op jit(solution)/shard_map/all_to_all | solution.py:29
  161.2 1.3 reduce_max.73
  162.4 0.1 stack.93
  162.5 1.4 exponential_reduce_fusion
  163.9 0.1 stack.95
  164.0 2.0 multiply_reduce_fusion
  166.0 0.1 collective-permute-start.3
  166.1 1.2 collective-permute-done.3
  167.4 12.3 %all_to_all.52 = f32[16,6,512]{2,1,0:T(8,128)S(1)} all-to-all(f32[16,6,512]{2,1,0:T(8,128)S(1)} %broadcast_in_dim.12), channel_id=1, replica_groups=mesh['x'=4,'yh'=2,'yl'=2,'c'=2,'z'=8] {'x','yh','yl'}, dimensions={0} | all-to-all | bytes 393216 | tf_op jit(solution)/shard_map/all_to_all | solution.py:29
  179.8 0.2 fusion.48
  180.1 11.5 %all_to_all.53 = f32[8,6,512]{2,1,0:T(8,128)S(1)} all-to-all(f32[8,6,512]{2,1,0:T(8,128)S(1)} %broadcast_in_dim.13), channel_id=1, replica_groups=mesh['x'=4,'yh'=2,'yl'=2,'c'=2,'z'=8] {'z'}, dimensions={0} | all-to-all | bytes 196608 | tf_op jit(solution)/shard_map/all_to_all | solution.py:29
  191.5 0.1 fusion.49
  191.7 1.7 fusion.4.own_grad_ref
  193.4 0.1 collective-permute-start.4
  193.5 1.7 collective-permute-done.4.pair_grad_ref
  195.3 3.5 %shard_map.71 = bf16[512,2048]{1,0:T(8,128)(2,1)S(1)} custom-call(s32[1]{0:T(128)} %bitcast.core_ref, bf16[512,384]{1,0:T(8,128)(2,1)S(1)} %fusion.4.own_grad_ref, bf16[512,384]{1,0:T(8,128)(2,1)S(1)} %collective-permute-done.4.pair_grad_ref, bf16[16,2,128,384]{3,2,1,0:T(8,128)(2,1)S(1)} %all_to_all.50.own_ref.pair_ref, ...), custom_call_target="tpu_custom_call" | custom-call | tf_op jit(solution)/shard_map/pallas_call | solution.py:143
  198.7 32.2 %all_to_all.54 = bf16[16,32,2048]{2,1,0:T(8,128)(2,1)S(1)} all-to-all(bf16[16,32,2048]{2,1,0:T(8,128)(2,1)S(1)} %bitcast.143), channel_id=1, replica_groups=mesh['x'=4,'yh'=2,'yl'=2,'c'=2,'z'=8] {'x','yh','yl'}, dimensions={0} | all-to-all | bytes 4194304 | tf_op jit(solution)/shard_map/all_to_all | solution.py:29
  230.9 0.4 reduce_sum.182
  231.3 0.1 reshape.148
  231.4 11.5 %all_to_all.55 = bf16[8,4,2048]{2,1,0:T(4,128)(2,1)S(1)} all-to-all(bf16[8,4,2048]{2,1,0:T(4,128)(2,1)S(1)} %reshape.148), channel_id=1, replica_groups=mesh['x'=4,'yh'=2,'yl'=2,'c'=2,'z'=8] {'z'}, dimensions={0} | all-to-all | bytes 262144 | tf_op jit(solution)/shard_map/all_to_all | solution.py:29
  242.9 0.1 reduce_sum.183
  243.0 11.5 %all_to_all.56 = bf16[8,4,2048]{2,1,0:T(4,128)(2,1)S(1)} all-to-all(bf16[8,4,2048]{2,1,0:T(4,128)(2,1)S(1)} %broadcast_in_dim.14), channel_id=1, replica_groups=mesh['x'=4,'yh'=2,'yl'=2,'c'=2,'z'=8] {'z'}, dimensions={0} | all-to-all | bytes 262144 | tf_op jit(solution)/shard_map/all_to_all | solution.py:29
  254.4 0.1 broadcast_select_fusion.5
  254.5 0.1 collective-permute-start.5
  254.6 0.6 dynamic_slice.7
  255.2 0.1 select_n.144
  255.3 0.5 collective-permute-done.5
  255.9 0.1 reshape.151
  256.0 0.3 broadcast_select_fusion.1
  256.2 0.3 pad_maximum_fusion.1
  256.6 0.7 reshape.150
  (26 shorter events, 0.5 us)
Async XLA Ops:
  7.2 0.9 copy-start
  8.1 1.3 collective-permute-start
  11.2 13.1 %collective-permute-start.1 = (bf16[16,2048]{1,0:T(8,128)(2,1)S(1)}, bf16[16,2048]{1,0:T(8,128)(2,1)S(1)}, u32[]{:S(2)}, u32[]{:S(2)}) collective-permute-start(bf16[16,2048]{1,0:T(8,128)(2,1)S(1)} %bitcast.147), channel_id=1, source_target_pairs={{0,8},{8,0},{1,9},{9,1},{2,10},{10,2},{3,11},{11,3},{4,12},{12,4},... | collective-permute-start | bytes 196616 | tf_op jit(solution)/shard_map/ppermute | solution.py:18
  12.3 19.6 %all-to-all-start = ((bf16[16,32,640]{2,1,0:T(8,128)(2,1)}), bf16[16,32,640]{2,1,0:T(8,128)(2,1)}, u32[]{:S(2)}, u32[]{:S(2)}) async-start(bf16[16,32,640]{2,1,0:T(8,128)(2,1)} %broadcast_in_dim.10), calls=%async_computation | async-start | bytes 1310720 | tf_op jit(solution)/shard_map/all_to_all | solution.py:29
  19.7 95.6 %reduce-scatter.2.cloned.1.call-start = ((), (), s32[]{:S(2)}) async-start(), calls=%async_computation.11 | async-start | bytes 7077888 | tf_op jit(solution)/shard_map/reduce_scatter | solution.py:200
  19.8 1.9 copy-start.2
  22.6 1.7 copy-start.1
  82.1 33.3 %all-to-all-start.1 = ((bf16[16,32,2048]{2,1,0:T(8,128)(2,1)}), bf16[16,32,2048]{2,1,0:T(8,128)(2,1)}, u32[]{:S(2)}, u32[]{:S(2)}) async-start(bf16[16,32,2048]{2,1,0:T(8,128)(2,1)} %broadcast_in_dim.11), calls=%async_computation.1 | async-start | bytes 4194304 | tf_op jit(solution)/shard_map/all_to_all | solution.py:29
  135.3 25.8 %all-to-all-start.4 = ((f32[8,64,384]{2,1,0:T(8,128)}), f32[8,64,384]{2,1,0:T(8,128)}, u32[]{:S(2)}, u32[]{:S(2)}) async-start(f32[8,64,384]{2,1,0:T(8,128)} %all_to_all.51), calls=%async_computation.5 | async-start | bytes 1572864 | tf_op jit(solution)/shard_map/all_to_all | solution.py:29
  144.7 0.9 copy-start.3
  145.6 2.6 collective-permute-start.2
  166.0 1.3 collective-permute-start.3
  193.4 1.8 collective-permute-start.4
  254.5 1.3 collective-permute-start.5
Sparse Core Ops, SparseCore 0:
  39.8 75.4 reduce-scatter.1

commit v5 on v3

--- a/solution.py
+++ b/solution.py
@@ -9,10 +9,11 @@
 digit = 64
 lanes = 128
 big_vmem = 56 * 2**20
-early_groups = 4
-XYH = ("x", "yh")
-XY = ("x", "yh", "yl")
-DP = ("x", "yh", "yl", "c")
+XY = "xy"
+DP = ("xy", "c")
+near_groups = [
+    [4 * x + y for x in range(4) for y in pair] for pair in ((0, 3), (1, 2))
+]
 
 
 def swap_cores(value):
@@ -54,78 +55,92 @@
 
 
 def teacher_regroup_kernel(head_ref, out_ref):
-    out_ref[0] = head_ref[...]
+    unit = out_ref.shape[2]
+    for j in range(out_ref.shape[0]):
+        out_ref[j] = head_ref[:, j * unit : (j + 1) * unit]
 
 
 def teacher_regroup(head, unit):
     depth, width = head.shape
     units = width // unit
+    block = units // 2
     return pl.pallas_call(
         teacher_regroup_kernel,
-        grid=(units,),
-        in_specs=[pl.BlockSpec((depth, unit), lambda j: (0, j))],
-        out_specs=pl.BlockSpec((1, depth, unit), lambda j: (j, 0, 0)),
+        grid=(units // block,),
+        in_specs=[pl.BlockSpec((depth, block * unit), lambda j: (0, j))],
+        out_specs=pl.BlockSpec((block, depth, unit), lambda j: (j, 0, 0)),
         out_shape=jax.ShapeDtypeStruct((units, depth, unit), head.dtype),
         compiler_params=pltpu.CompilerParams(vmem_limit_bytes=big_vmem),
     )(head)
 
 
 def teacher_kernel(rows_ref, cols_ref, out_ref):
-    out_ref[0] = jnp.dot(rows_ref[...], cols_ref[0], preferred_element_type=jnp.float32)
-
-
-def teacher_partial(rows, cols):
-    units, depth, unit = cols.shape
+    unit = out_ref.shape[2]
+    for j in range(0, out_ref.shape[0], 2):
+        cols = jnp.concatenate([cols_ref[j], cols_ref[j + 1]], axis=1)
+        part = jnp.dot(rows_ref[...], cols, preferred_element_type=jnp.float32)
+        out_ref[j] = part[:, :unit]
+        out_ref[j + 1] = part[:, unit:]
+
+
+def teacher_partial(rows, cols, depth):
+    units, _, unit = cols.shape
     tokens = rows.shape[0]
+    block = units // 2
     return pl.pallas_call(
         teacher_kernel,
-        grid=(units,),
+        grid=(units // block,),
         in_specs=[
             pl.BlockSpec((tokens, depth), lambda j: (0, 0)),
-            pl.BlockSpec((1, depth, unit), lambda j: (j, 0, 0)),
+            pl.BlockSpec((block, depth, unit), lambda j: (j, 0, 0)),
         ],
-        out_specs=pl.BlockSpec((1, tokens, unit), lambda j: (j, 0, 0)),
+        out_specs=pl.BlockSpec((block, tokens, unit), lambda j: (j, 0, 0)),
         out_shape=jax.ShapeDtypeStruct((units, tokens, unit), jnp.float32),
         compiler_params=pltpu.CompilerParams(vmem_limit_bytes=big_vmem),
     )(rows, cols)
 
 
-def regroup_kernel(head_ref, out_ref):
+def regroup_kernel(odd_ref, low_ref, high_ref, out_ref):
     unit = out_ref.shape[4]
-    for j in range(out_ref.shape[0]):
-        out_ref[j, 0, 0] = head_ref[:, j * unit : (j + 1) * unit]
-
-
-def regroup(head, units, unit):
+    odd = odd_ref[0]
+    for half, head_ref in enumerate((low_ref, high_ref)):
+        for j in range(out_ref.shape[0]):
+            row = 1 - odd if half != j % 2 else odd
+            out_ref[j, row, 0] = head_ref[:, j * unit : (j + 1) * unit]
+
+
+def regroup(odd, head, units, unit):
     rows, width = head.shape
     return pl.pallas_call(
         regroup_kernel,
-        grid=(2, 2),
-        in_specs=[pl.BlockSpec((rows, width // 4), lambda yl, core: (0, yl * 2 + core))],
-        out_specs=pl.BlockSpec(
-            (units, 1, 1, rows, unit), lambda yl, core: (0, yl, core, 0, 0)
+        grid_spec=pltpu.PrefetchScalarGridSpec(
+            num_scalar_prefetch=1,
+            grid=(2,),
+            in_specs=[
+                pl.BlockSpec((rows, width // 4), lambda core, odd: (0, core)),
+                pl.BlockSpec((rows, width // 4), lambda core, odd: (0, 2 + core)),
+            ],
+            out_specs=pl.BlockSpec(
+                (units, 2, 1, rows, unit), lambda core, odd: (0, 0, core, 0, 0)
+            ),
         ),
         out_shape=jax.ShapeDtypeStruct((units, 2, 2, rows, unit), head.dtype),
         compiler_params=pltpu.CompilerParams(vmem_limit_bytes=32 * 2**20),
-    )(head)
-
-
-def student_kernel(core_ref, early_ref, late_ref, own_ref, pair_ref, mine_ref, other_ref):
+    )(odd, head, head)
+
+
+def student_kernel(core_ref, rows_ref, own_ref, pair_ref, mine_ref, other_ref):
     unit = mine_ref.shape[1]
-    split = early_groups
+    rows = jnp.concatenate([rows_ref[k] for k in range(rows_ref.shape[0])], axis=1)
     for cols_ref, out_ref in ((own_ref, mine_ref), (pair_ref, other_ref)):
-        first = cols_ref[:split, 0].reshape(-1, unit)
-        second = cols_ref[split:, 0].reshape(-1, unit)
-        out_ref[...] = jnp.dot(
-            early_ref[...], first, preferred_element_type=jnp.float32
-        ) + jnp.dot(late_ref[...], second, preferred_element_type=jnp.float32)
-
-
-def student_partial(core, early, late, cols):
-    tokens = early.shape[0]
+        cols = cols_ref[:, 0].reshape(rows.shape[1], unit)
+        out_ref[...] = jnp.dot(rows, cols, preferred_element_type=jnp.float32)
+
+
+def student_partial(core, rows, cols):
+    slices, tokens, depth = rows.shape
     groups, _, part, unit = cols.shape
     block = 128
-    first = early_groups * part
     half = jax.ShapeDtypeStruct((tokens, unit), jnp.float32)
     return pl.pallas_call(
         student_kernel,
@@ -133,8 +148,7 @@
             num_scalar_prefetch=1,
             grid=(tokens // block,),
             in_specs=[
-                pl.BlockSpec((block, first), lambda i, core: (i, 0)),
-                pl.BlockSpec((block, groups * part - first), lambda i, core: (i, 0)),
+                pl.BlockSpec((slices, block, depth), lambda i, core: (0, i, 0)),
                 pl.BlockSpec((groups, 1, part, unit), lambda i, core: (0, core[0], 0, 0)),
                 pl.BlockSpec((groups, 1, part, unit), lambda i, core: (0, 1 - core[0], 0, 0)),
             ],
@@ -142,7 +156,7 @@
         ),
         out_shape=[half, half],
         compiler_params=pltpu.CompilerParams(vmem_limit_bytes=32 * 2**20),
-    )(core, early, late, cols, cols)
+    )(core, rows, cols, cols)
 
 
 def grad_kernel(core_ref, own_grad_ref, pair_grad_ref, own_ref, pair_ref, out_ref):
@@ -190,43 +204,57 @@
     depth = teacher_head.shape[0]
     half = width // 2
 
-    by_core = student_hidden.reshape(tok, xy_count, 2, row_part)
-    even = by_core[:, :, 0].reshape(tok, half)
-    odd = by_core[:, :, 1].reshape(tok, half)
+    share = half // z_count
+    student_slice = lax.dynamic_slice_in_dim(student_hidden, plane * 2 * share, 2 * share, 1)
+    by_core = student_slice.reshape(tok, -1, 2, row_part)
+    even = by_core[:, :, 0].reshape(tok, share)
+    odd = by_core[:, :, 1].reshape(tok, share)
     keep = jnp.where(core == 0, even, odd)
     give = jnp.where(core == 0, odd, even)
     teacher_slice = lax.dynamic_slice_in_dim(teacher_hidden, plane * depth, depth, 1)
+    received = swap_cores(jnp.concatenate([teacher_slice, give], axis=1))
+    pair = in_core_order(jnp.concatenate([teacher_slice, keep], axis=1), received, 0)
+    teacher_head, student_head, sampled_ids, pair = lax.optimization_barrier(
+        (teacher_head, student_head, sampled_ids, pair)
+    )
+    gathered = spread(pair, XY).reshape(-1, depth + share)
+    tokens = gathered.shape[0]
+
+    teacher_parts = teacher_regroup(teacher_head, unit)
+    odd_plane = lax.rem(plane, 2)
+    parts = regroup(odd_plane.reshape(1).astype(jnp.int32), student_head, z_count, unit)
+    parts = parts.reshape(xy_count, 2, row_part, unit)
     digits = jnp.stack(
         [sampled_ids // (digit * digit), sampled_ids // digit % digit, sampled_ids % digit], axis=1
     ).astype(jnp.bfloat16)
     digits = jnp.pad(digits, ((0, 0), (0, lanes - 3)))
-    shared = jnp.concatenate([teacher_slice, digits], axis=1)
-    received = swap_cores(jnp.concatenate([shared, give], axis=1))
-    pair = in_core_order(jnp.concatenate([shared, keep], axis=1), received, 0)
-    early = early_groups * row_part
-    cut = depth + lanes + early
-    gathered = lax.all_gather(pair[:, :cut], XY, axis=0, tiled=True)
-    late_pair = pair[:, cut:]
-    tokens = gathered.shape[0]
-    early_rows = gathered[:, depth + lanes :]
-    id_digits = gathered[:, depth : depth + 3].astype(jnp.int32)
+    digits = in_core_order(digits, swap_cores(digits), 0)
+    share_rows = gathered[:, depth:]
+    teacher_parts, gathered, share_rows, parts, digits = lax.optimization_barrier(
+        (teacher_parts, gathered, share_rows, parts, digits)
+    )
+
+    student_rows = lax.all_gather(share_rows, "z", axis=0, tiled=False)
+    teacher_cols = lax.all_to_all(
+        teacher_parts, XY, 0, 0, axis_index_groups=near_groups, tiled=True
+    )
+    teacher_part = teacher_partial(gathered, teacher_cols, depth)
+
+    parts, teacher_part = lax.optimization_barrier((parts, teacher_part))
+    teacher_logits = lax.psum_scatter(teacher_part, "z", scatter_dimension=0, tiled=False)
+    student_cols = exchange(parts, XY)
+    digits, core_id, place, student_cols = lax.optimization_barrier(
+        (digits, core_id, lax.axis_index(XY), student_cols)
+    )
+    id_digits = spread(digits, XY).reshape(tokens, lanes)[:, :3].astype(jnp.int32)
     all_ids = (id_digits[:, 0] * digit + id_digits[:, 1]) * digit + id_digits[:, 2]
-
-    teacher_cols = exchange(teacher_regroup(teacher_head, unit), XYH)
-    teacher_part = teacher_partial(gathered[:, :depth], teacher_cols)
-    student_head, late_pair, teacher_part = lax.optimization_barrier(
-        (student_head, late_pair, teacher_part)
-    )
-    teacher_logits = lax.psum_scatter(teacher_part, "z", scatter_dimension=0, tiled=False)
-
-    parts = regroup(student_head, z_count, unit).reshape(xy_count, 2, row_part, unit)
-    student_cols = exchange(parts, XY)
-    late_rows = spread(late_pair, XY).reshape(tokens, half - early)
-    mine, other = student_partial(core_id, early_rows, late_rows, student_cols)
+    mine, other = student_partial(core_id, student_rows, student_cols)
     student_logits = mine + swap_cores(other)
 
-    xyh = lax.axis_index("x") * 2 + lax.axis_index("yh")
-    owner = (plane * 2 + lax.axis_index("yl")) * 2 + core
+    row = lax.rem(place, 4)
+    xyh = place // 2
+    near = lax.rem(row // 2 + row, 2)
+    owner = (plane * 2 + lax.rem(near + plane, 2)) * 2 + core
     column_ids = (owner * z_count + xyh) * unit + jnp.arange(unit, dtype=jnp.int32)
     hit_mask = (column_ids[None, :] == all_ids[:, None]).astype(jnp.float32)
 
@@ -276,7 +304,7 @@
 
 
 def solution(mesh):
-    fine = Mesh(mesh.devices.reshape(4, 2, 2, 2, 8), ("x", "yh", "yl", "c", "z"))
+    fine = Mesh(mesh.devices.reshape(16, 2, 8), ("xy", "c", "z"))
     in_specs = (P(DP, None), P(DP, None), P(DP, "z"), P("z", DP), P(DP))
     out_specs = (P(DP, None), P(DP))
     return jax.shard_map(local, mesh=fine, in_specs=in_specs, out_specs=out_specs, check_vma=False)

time: 296 us -> 263 us (0.89)
  waiting for transfers between devices: 93.9 us -> 64.8 us
  starting transfers between devices: 12.3 us -> 21 us
  Pallas kernels: 22.7 us -> 17 us
  local copies, waits for them, and re-layouts: 14.1 us -> 10.2 us
    all_gather x1, waiting for transfers between devices: 72.1 us -> 0.01 us  [local(): student_rows = lax.all_gather(share_rows, 'z', axis=0, tiled=False)]
    all_to_all x6 -> x5, blocking collectives: 124 us -> 82.8 us  [exchange(): return lax.all_to_all(value, axes, 0, 0, tiled=True)]
    all_to_all x0 -> x1, blocking collectives: none -> 40.4 us  [local(): lax.all_to_all(teacher_parts, XY, 0, 0, axis_index_groups=near_groups, ti...]
    all_to_all x2 -> x3, waiting for transfers between devices: 17.1 us -> 49.8 us  [exchange(): return lax.all_to_all(value, axes, 0, 0, tiled=True)]
    reduce_scatter x1, waiting for transfers between devices: 0.01 us -> 10.3 us  [local(): lax.psum_scatter(teacher_part, 'z', scatter_dimension=0, tiled=False)]
    all_to_all x2 -> x3, starting transfers between devices: 11.7 us -> 20.4 us  [exchange(): return lax.all_to_all(value, axes, 0, 0, tiled=True)]
    pallas_call x3, Pallas kernels: 15.4 us -> 9.44 us  [the longest x1 5.2 us: teacher_partial(): pl.pallas_call(teacher_kernel, grid=(units // block,), in_specs=[pl.Block...]
    unnamed x19 -> x11, local copies, waits for them, and re-layouts: 7.4 us -> 4.21 us
  transfers between devices with their start and end apart: 9 -> 11, of which waited for: 6 -> 8; matrix products, arithmetic and copies ran while one was open for 3% -> 2% of each run, Pallas kernels for 4% -> 5%
where the time goes in v5:
time: 263 us; the launch traced here: 260 us
  blocking collectives  123 us (47%)
  waiting for transfers between devices  64.8 us (25%)
  starting transfers between devices  21 us (8%)
  Pallas kernels  17 us (6%)
  between operations  14.3 us (5%)
  local copies, waits for them, and re-layouts  10.2 us (4%)
  other arithmetic  9.71 us (4%)
    all_to_all x5, blocking collectives, exchange(): return lax.all_to_all(value, axes, 0, 0, tiled=True)  82.8 us
    all_to_all x3, waiting for transfers between devices, exchange(): return lax.all_to_all(value, axes, 0, 0, tiled=True)  49.8 us
    all_to_all x1, blocking collectives, local(): lax.all_to_all(teacher_parts, XY, 0, 0, axis_index_groups=near_groups, ti...  40.4 us
    all_to_all x3, starting transfers between devices, exchange(): return lax.all_to_all(value, axes, 0, 0, tiled=True)  20.4 us
    reduce_scatter x1, waiting for transfers between devices, local(): lax.psum_scatter(teacher_part, 'z', scatter_dimension=0, tiled=False)  10.3 us
  transfers between devices with their start and end apart: 11, of which 8 were waited for; matrix products, arithmetic and copies ran while one was open for 2% of the time, Pallas kernels for 5%

profile of v5, /device:TPU:8, one launch (start us, length us, event | category | flops | bytes accessed | tf_op | source)
XLA Modules:
  0.0 260.2 jit_solution(9894038124312747235)
XLA Ops:
  7.2 0.8 constant_dynamic-slice_fusion
  8.0 0.1 fusion.24
  8.1 0.1 collective-permute-start
  8.2 1.2 collective-permute-done
  9.4 1.0 broadcast_in_dim.10
  10.4 7.4 %all-to-all-start = ((bf16[16,32,768]{2,1,0:T(8,128)(2,1)}), bf16[16,32,768]{2,1,0:T(8,128)(2,1)}, u32[]{:S(2)}, u32[]{:S(2)}) async-start(bf16[16,32,768]{2,1,0:T(8,128)(2,1)} %broadcast_in_dim.10), calls=%async_computation | async-start | bytes 1572864 | tf_op jit(solution)/shard_map/all_to_all | solution.py:31
  17.8 0.0 all-gather.3.cloned.1.call-start
  17.8 0.7 convert_bitcast_fusion
  18.5 0.1 collective-permute-start.1
  18.6 0.0 copy-start.1
  18.6 3.4 %shard_map.68 = bf16[8,512,384]{2,1,0:T(8,128)(2,1)} custom-call(bf16[512,3072]{1,0:T(8,128)(2,1)} %head_ref), custom_call_target="tpu_custom_call" | custom-call | tf_op jit(solution)/shard_map/pallas_call | solution.py:67
  22.0 0.0 copy-done.1
  22.0 0.9 shard_map.69
  22.8 0.0 copy-start
  22.9 1.7 copy-done
  24.5 0.0 collective-permute-done.1
  24.6 0.1 copy.58
  24.6 0.1 copy.59
  24.7 6.7 %all-to-all-done = bf16[16,32,768]{2,1,0:T(8,128)(2,1)} async-done(((bf16[16,32,768]{2,1,0:T(8,128)(2,1)}), bf16[16,32,768]{2,1,0:T(8,128)(2,1)}, u32[]{:S(2)}, u32[]{:S(2)}) %all-to-all-start) | async-done | bytes 786464 | tf_op jit(solution)/shard_map/all_to_all | solution.py:31
  31.4 1.7 slice.114
  33.1 0.0 all-gather.3.cloned.1.call-update
  33.1 0.0 reduce-scatter.2.cloned.1.call-start
  33.1 40.4 %all_to_all.45.cols_ref = bf16[8,512,384]{2,1,0:T(8,128)(2,1)} all-to-all(bf16[8,512,384]{2,1,0:T(8,128)(2,1)} %shard_map.68), channel_id=1, replica_groups={{0,48,64,112,128,176,192,240},{16,32,80,96,144,160,208,224},{1,49,65,11..., dimensions={0} | all-to-all | bytes 6291456 | tf_op jit(solution)/shard_map/all_to_all | solution.py:238
  73.6 5.2 %shard_map.70 = f32[8,512,384]{2,1,0:T(8,128)} custom-call(bf16[512,768]{1,0:T(8,128)(2,1)} %bitcast.rows_ref, bf16[8,512,384]{2,1,0:T(8,128)(2,1)} %all_to_all.45.cols_ref), custom_call_target="tpu_custom_call" | custom-call | tf_op jit(solution)/shard_map/pallas_call | solution.py:90
  78.8 0.0 reduce-scatter.2.cloned.1.call-update
  78.8 6.2 %all-to-all-start.2 = ((bf16[16,2,128,384]{3,2,1,0:T(8,128)(2,1)}), bf16[16,2,128,384]{3,2,1,0:T(8,128)(2,1)S(1)}, u32[]{:S(2)}, u32[]{:S(2)}) async-start(bf16[16,2,128,384]{3,2,1,0:T(8,128)(2,1)} %bitcast.147), calls=%async_computation.2 | async-start | bytes 6291456 | tf_op jit(solution)/shard_map/all_to_all | solution.py:31
  85.0 36.5 %all-to-all-done.2.own_ref.pair_ref = bf16[16,2,128,384]{3,2,1,0:T(8,128)(2,1)S(1)} async-done(((bf16[16,2,128,384]{3,2,1,0:T(8,128)(2,1)}), bf16[16,2,128,384]{3,2,1,0:T(8,128)(2,1)S(1)}, u32[]{:S(2)}, u32[]{:S(2)}) %all-to-all-start.2) | async-done | bytes 3145760 | tf_op jit(solution)/shard_map/all_to_all | solution.py:31
  121.5 0.0 all-gather.3.cloned.1.call-done
  121.5 0.0 copy-start.2
  121.5 1.6 copy-done.2
  123.2 4.1 %shard_map.71 = (f32[512,384]{1,0:T(8,128)S(1)}, f32[512,384]{1,0:T(8,128)}) custom-call(s32[1]{0:T(128)} %bitcast.6.core_ref, bf16[8,512,256]{2,1,0:T(8,128)(2,1)S(1)} %bitcast.149, bf16[16,2,128,384]{3,2,1,0:T(8,128)(2,1)S(1)} %all-to-all-done.2.own_ref.pair_ref, bf16[16,2,128,384]{3,2,1,0:T(8,128)(2,1)S(1)} %all-to-all-done.2.own_ref.pair_ref), custom_call_target="tpu_custom_call" | custom-call | tf_op jit(solution)/shard_map/pallas_call | solution.py:145
  127.2 0.9 copy-done.3
  128.1 0.0 collective-permute-start.2
  128.1 0.7 broadcast_in_dim.11
  128.8 6.8 %all-to-all-start.3 = ((bf16[16,32,128]{2,1,0:T(8,128)(2,1)}), bf16[16,32,128]{2,1,0:T(8,128)(2,1)S(1)}, u32[]{:S(2)}, u32[]{:S(2)}) async-start(bf16[16,32,128]{2,1,0:T(8,128)(2,1)} %broadcast_in_dim.11), calls=%async_computation.4 | async-start | bytes 262144 | tf_op jit(solution)/shard_map/all_to_all | solution.py:31
  135.6 6.6 %all-to-all-done.3 = bf16[16,32,128]{2,1,0:T(8,128)(2,1)S(1)} async-done(((bf16[16,32,128]{2,1,0:T(8,128)(2,1)}), bf16[16,32,128]{2,1,0:T(8,128)(2,1)S(1)}, u32[]{:S(2)}, u32[]{:S(2)}) %all-to-all-start.3) | async-done | bytes 131104 | tf_op jit(solution)/shard_map/all_to_all | solution.py:31
  142.3 0.3 fusion.8
  142.6 0.0 collective-permute-done.2
  142.6 2.4 fusion.56
  145.0 10.3 %reduce-scatter.2.cloned.1.call-done = f32[1,512,384]{2,1,0:T(8,128)} async-done(((f32[8,512,384]{2,1,0:T(8,128)}), f32[1,512,384]{2,1,0:T(8,128)}) %reduce-scatter.2.cloned.1.call-update) | async-done | bytes 786448 | tf_op jit(solution)/shard_map/reduce_scatter | solution.py:244
  155.3 1.3 reduce_max.73
  156.5 2.1 multiply_reduce_fusion
  158.7 0.1 collective-permute-start.3
  158.8 1.1 collective-permute-done.3
  160.1 14.4 %all_to_all.46 = f32[16,6,512]{2,1,0:T(8,128)S(1)} all-to-all(f32[16,6,512]{2,1,0:T(8,128)S(1)} %broadcast_in_dim.12), channel_id=1, replica_groups=mesh['xy'=16,'c'=2,'z'=8] {'xy'}, dimensions={0} | all-to-all | bytes 393216 | tf_op jit(solution)/shard_map/all_to_all | solution.py:31
  174.5 0.2 fusion.57
  174.8 13.2 %all_to_all.47 = f32[8,6,512]{2,1,0:T(8,128)S(1)} all-to-all(f32[8,6,512]{2,1,0:T(8,128)S(1)} %broadcast_in_dim.13), channel_id=1, replica_groups=mesh['xy'=16,'c'=2,'z'=8] {'z'}, dimensions={0} | all-to-all | bytes 196608 | tf_op jit(solution)/shard_map/all_to_all | solution.py:31
  188.1 0.1 fusion.58
  188.2 1.7 fusion.4.own_grad_ref
  190.0 0.1 collective-permute-start.4
  190.1 1.7 collective-permute-done.4.pair_grad_ref
  191.8 3.5 %shard_map.72 = bf16[512,2048]{1,0:T(8,128)(2,1)S(1)} custom-call(s32[1]{0:T(128)} %bitcast.6.core_ref, bf16[512,384]{1,0:T(8,128)(2,1)S(1)} %fusion.4.own_grad_ref, bf16[512,384]{1,0:T(8,128)(2,1)S(1)} %collective-permute-done.4.pair_grad_ref, bf16[16,2,128,384]{3,2,1,0:T(8,128)(2,1)S(1)} %all-to-all-done.2.own_ref.pair_ref, ...), custom_call_target="tpu_custom_call" | custom-call | tf_op jit(solution)/shard_map/pallas_call | solution.py:177
  195.3 32.2 %all_to_all.48 = bf16[16,32,2048]{2,1,0:T(8,128)(2,1)S(1)} all-to-all(bf16[16,32,2048]{2,1,0:T(8,128)(2,1)S(1)} %bitcast.148), channel_id=1, replica_groups=mesh['xy'=16,'c'=2,'z'=8] {'xy'}, dimensions={0} | all-to-all | bytes 4194304 | tf_op jit(solution)/shard_map/all_to_all | solution.py:31
  227.5 0.4 reduce_sum.182
  227.9 0.1 reshape.138
  227.9 11.5 %all_to_all.49 = bf16[8,4,2048]{2,1,0:T(4,128)(2,1)S(1)} all-to-all(bf16[8,4,2048]{2,1,0:T(4,128)(2,1)S(1)} %reshape.138), channel_id=1, replica_groups=mesh['xy'=16,'c'=2,'z'=8] {'z'}, dimensions={0} | all-to-all | bytes 262144 | tf_op jit(solution)/shard_map/all_to_all | solution.py:31
  239.4 0.1 reduce_sum.183
  239.5 11.5 %all_to_all.50 = bf16[8,4,2048]{2,1,0:T(4,128)(2,1)S(1)} all-to-all(bf16[8,4,2048]{2,1,0:T(4,128)(2,1)S(1)} %broadcast_in_dim.14), channel_id=1, replica_groups=mesh['xy'=16,'c'=2,'z'=8] {'z'}, dimensions={0} | all-to-all | bytes 262144 | tf_op jit(solution)/shard_map/all_to_all | solution.py:31
  251.0 0.1 broadcast_select_fusion
  251.0 0.1 collective-permute-start.5
  251.2 0.6 dynamic_slice.11
  251.8 0.6 collective-permute-done.5
  252.5 0.1 copy.68
  252.6 0.7 reshape.140
  (32 shorter events, 0.6 us)
Async XLA Ops:
  8.1 1.3 collective-permute-start
  10.4 21.0 %all-to-all-start = ((bf16[16,32,768]{2,1,0:T(8,128)(2,1)}), bf16[16,32,768]{2,1,0:T(8,128)(2,1)}, u32[]{:S(2)}, u32[]{:S(2)}) async-start(bf16[16,32,768]{2,1,0:T(8,128)(2,1)} %broadcast_in_dim.10), calls=%async_computation | async-start | bytes 1572864 | tf_op jit(solution)/shard_map/all_to_all | solution.py:31
  17.8 103.8 %all-gather.3.cloned.1.call-start = ((), (), s32[]{:S(2)}) async-start(), calls=%async_computation.11 | async-start | bytes 2359296 | tf_op jit(solution)/shard_map/all_gather | solution.py:237
  18.5 6.1 %collective-permute-start.1 = (bf16[16,128]{0,1:T(8,128)(2,1)S(1)}, bf16[16,128]{0,1:T(8,128)(2,1)S(1)}, u32[]{:S(2)}, u32[]{:S(2)}) collective-permute-start(bf16[16,128]{0,1:T(8,128)(2,1)S(1)} %fusion.14), channel_id=1, source_target_pairs={{0,8},{8,0},{1,9},{9,1},{2,10},{10,2},{3,11},{11,3},{4,12},{12,4},... | collective-permute-start | bytes 12296 | tf_op jit(solution)/shard_map/ppermute | solution.py:20
  18.6 3.4 %copy-start.1 = (bf16[128,12288]{1,0:T(8,128)(2,1)S(1)}, bf16[128,12288]{1,0:T(8,128)(2,1)}, u32[]{:S(2)}) copy-start(bf16[128,12288]{1,0:T(8,128)(2,1)} %high_ref) | copy-start | bytes 9437188
  22.8 1.7 copy-start
  33.1 122.2 %reduce-scatter.2.cloned.1.call-start = ((), (), s32[]{:S(2)}) async-start(), calls=%async_computation.10 | async-start | bytes 7077888 | tf_op jit(solution)/shard_map/reduce_scatter | solution.py:244
  78.8 42.8 %all-to-all-start.2 = ((bf16[16,2,128,384]{3,2,1,0:T(8,128)(2,1)}), bf16[16,2,128,384]{3,2,1,0:T(8,128)(2,1)S(1)}, u32[]{:S(2)}, u32[]{:S(2)}) async-start(bf16[16,2,128,384]{3,2,1,0:T(8,128)(2,1)} %bitcast.147), calls=%async_computation.2 | async-start | bytes 6291456 | tf_op jit(solution)/shard_map/all_to_all | solution.py:31
  121.5 1.6 copy-start.2
  127.2 0.9 copy-start.3
  128.1 14.5 %collective-permute-start.2 = (f32[512,384]{1,0:T(8,128)}, f32[512,384]{1,0:T(8,128)}, u32[]{:S(2)}, u32[]{:S(2)}) collective-permute-start(f32[512,384]{1,0:T(8,128)} %get-tuple-element.32), channel_id=1, source_target_pairs={{0,8},{8,0},{1,9},{9,1},{2,10},{10,2},{3,11},{11,3},{4,12},{12,4},... | collective-permute-start | bytes 2359304 | tf_op jit(solution)/shard_map/ppermute | solution.py:20
  128.8 13.4 %all-to-all-start.3 = ((bf16[16,32,128]{2,1,0:T(8,128)(2,1)}), bf16[16,32,128]{2,1,0:T(8,128)(2,1)S(1)}, u32[]{:S(2)}, u32[]{:S(2)}) async-start(bf16[16,32,128]{2,1,0:T(8,128)(2,1)} %broadcast_in_dim.11), calls=%async_computation.4 | async-start | bytes 262144 | tf_op jit(solution)/shard_map/all_to_all | solution.py:31
  158.7 1.3 collective-permute-start.3
  190.0 1.8 collective-permute-start.4
  251.0 1.3 collective-permute-start.5
Sparse Core Ops, SparseCore 0:
  33.2 41.4 all-gather.2
  78.9 76.3 reduce-scatter.1

commit v6 on v5

v6 whole, which is shorter than its diff:
```python
import jax
import jax.numpy as jnp
from jax import lax
from jax.experimental import pallas as pl
from jax.experimental.pallas import tpu as pltpu
from jax.sharding import Mesh, PartitionSpec as P

ce_weight = 0.5
digit = 64
lanes = 128
stat_rows = 8
big_vmem = 56 * 2**20
XY = "xy"
DP = ("xy", "c")
near_groups = [
    [4 * x + y for x in range(4) for y in pair] for pair in ((0, 3), (1, 2))
]


def swap_cores(value):
    return lax.ppermute(value, "c", [(0, 1), (1, 0)])


def exchange(value, axes):
    return lax.all_to_all(value, axes, 0, 0, tiled=True)


def spread(value, axes):
    count = lax.axis_size(axes)
    return exchange(jnp.broadcast_to(value[None], (count,) + value.shape), axes)


def hits(info_ref, h, digits_ref, shape):
    digits = digits_ref[...].astype(jnp.float32)
    ids = (digits[:, 0:1] * digit + digits[:, 1:2]) * digit + digits[:, 2:3]
    columns = info_ref[1 + h] + lax.broadcasted_iota(jnp.int32, shape, 1)
    return columns == ids.astype(jnp.int32)


def stats_kernel(info_ref, digits_ref, student_ref, own_ref, pair_ref, out_ref):
    teacher = (own_ref, pair_ref)
    tokens, unit = own_ref.shape
    tops = [jnp.full((tokens, 1), -jnp.inf, jnp.float32)] * 2
    for h in range(2):
        tops[0] = jnp.maximum(tops[0], jnp.max(student_ref[h], axis=1, keepdims=True))
        tops[1] = jnp.maximum(tops[1], jnp.max(teacher[h][...], axis=1, keepdims=True))
    sums = [jnp.zeros((tokens, 1), jnp.float32)] * 4
    for h in range(2):
        student, other = student_ref[h], teacher[h][...]
        weight = jnp.exp(student - tops[0])
        found = jnp.where(hits(info_ref, h, digits_ref, (tokens, unit)), student, 0.0)
        terms = (weight, jnp.exp(other - tops[1]), weight * (student - other), found)
        sums = [a + jnp.sum(b, axis=1, keepdims=True) for a, b in zip(sums, terms)]
    lane = lax.broadcasted_iota(jnp.int32, (tokens, lanes), 1)
    table = jnp.zeros((tokens, lanes), jnp.float32)
    for k, column in enumerate(tops + sums):
        table = jnp.where(lane == k, column, table)
    out_ref[...] = jnp.broadcast_to(table.T[: out_ref.shape[1]], out_ref.shape)


def merged(stats):
    tops = jnp.max(stats, axis=0)
    scale = jnp.exp(stats - tops[None])
    row = lax.broadcasted_iota(jnp.int32, stats.shape, 1)
    weight = jnp.where((row == 2) | (row == 4), scale[:, 0:1], 0.0)
    weight = jnp.where(row == 3, scale[:, 1:2], weight)
    weight = jnp.where(row == 5, 1.0, weight)
    total = jnp.sum(stats * weight, axis=0)
    return jnp.where(lax.broadcasted_iota(jnp.int32, tops.shape, 0) < 2, tops, total)


def merge_kernel(stats_ref, out_ref):
    out_ref[...] = jnp.broadcast_to(merged(stats_ref[...]), out_ref.shape)


def merge(stats, copies):
    return pl.pallas_call(
        merge_kernel,
        out_shape=jax.ShapeDtypeStruct((copies,) + stats.shape[1:], jnp.float32),
    )(stats)


def local_stats(info, digits, student, teacher, pair, copies):
    tokens, unit = pair.shape
    first = lambda i, info: (0, 0)
    return pl.pallas_call(
        stats_kernel,
        grid_spec=pltpu.PrefetchScalarGridSpec(
            num_scalar_prefetch=1,
            grid=(1,),
            in_specs=[
                pl.BlockSpec(digits.shape, first),
                pl.BlockSpec(student.shape, lambda i, info: (0, 0, 0)),
                pl.BlockSpec((tokens, unit), first),
                pl.BlockSpec((tokens, unit), first),
            ],
            out_specs=pl.BlockSpec((copies, stat_rows, tokens), lambda i, info: (0, 0, 0)),
        ),
        out_shape=jax.ShapeDtypeStruct((copies, stat_rows, tokens), jnp.float32),
        compiler_params=pltpu.CompilerParams(vmem_limit_bytes=32 * 2**20),
    )(info, digits, student, teacher, pair)


def teacher_regroup_kernel(head_ref, out_ref):
    unit = out_ref.shape[2]
    for j in range(out_ref.shape[0]):
        out_ref[j] = head_ref[:, j * unit : (j + 1) * unit]


def teacher_regroup(head, unit):
    depth, width = head.shape
    units = width // unit
    block = units // 2
    return pl.pallas_call(
        teacher_regroup_kernel,
        grid=(units // block,),
        in_specs=[pl.BlockSpec((depth, block * unit), lambda j: (0, j))],
        out_specs=pl.BlockSpec((block, depth, unit), lambda j: (j, 0, 0)),
        out_shape=jax.ShapeDtypeStruct((units, depth, unit), head.dtype),
        compiler_params=pltpu.CompilerParams(vmem_limit_bytes=big_vmem),
    )(head)


def teacher_kernel(own_ref, other_ref, cols_ref, out_ref):
    unit = out_ref.shape[2]
    count = own_ref.shape[0]
    for j in range(0, out_ref.shape[0], 2):
        cols = jnp.concatenate([cols_ref[j], cols_ref[j + 1]], axis=1)
        for start, rows_ref in ((0, own_ref), (count, other_ref)):
            part = jnp.dot(rows_ref[...], cols, preferred_element_type=jnp.float32)
            out_ref[j, start : start + count] = part[:, :unit]
            out_ref[j + 1, start : start + count] = part[:, unit:]


def teacher_partial(own, other, cols):
    units, depth, unit = cols.shape
    count = own.shape[0]
    block = units // 2
    return pl.pallas_call(
        teacher_kernel,
        grid=(units // block,),
        in_specs=[
            pl.BlockSpec((count, depth), lambda j: (0, 0)),
            pl.BlockSpec((count, depth), lambda j: (0, 0)),
            pl.BlockSpec((block, depth, unit), lambda j: (j, 0, 0)),
        ],
        out_specs=pl.BlockSpec((block, 2 * count, unit), lambda j: (j, 0, 0)),
        out_shape=jax.ShapeDtypeStruct((units, 2 * count, unit), jnp.float32),
        compiler_params=pltpu.CompilerParams(vmem_limit_bytes=big_vmem),
    )(own, other, cols)


def regroup_kernel(odd_ref, low_ref, high_ref, out_ref):
    unit = out_ref.shape[4]
    odd = odd_ref[0]
    for half, head_ref in enumerate((low_ref, high_ref)):
        for j in range(out_ref.shape[0]):
            row = 1 - odd if half != j % 2 else odd
            out_ref[j, row, 0] = head_ref[:, j * unit : (j + 1) * unit]


def regroup(odd, head, units, unit):
    rows, width = head.shape
    return pl.pallas_call(
        regroup_kernel,
        grid_spec=pltpu.PrefetchScalarGridSpec(
            num_scalar_prefetch=1,
            grid=(2,),
            in_specs=[
                pl.BlockSpec((rows, width // 4), lambda core, odd: (0, core)),
                pl.BlockSpec((rows, width // 4), lambda core, odd: (0, 2 + core)),
            ],
            out_specs=pl.BlockSpec(
                (units, 2, 1, rows, unit), lambda core, odd: (0, 0, core, 0, 0)
            ),
        ),
        out_shape=jax.ShapeDtypeStruct((units, 2, 2, rows, unit), head.dtype),
        compiler_params=pltpu.CompilerParams(vmem_limit_bytes=32 * 2**20),
    )(odd, head, head)


def student_kernel(core_ref, rows_ref, own_mine, own_pair, far_mine, far_pair, out_ref, turned_ref):
    core = core_ref[0]
    slices, _, depth = rows_ref.shape
    part, unit = own_mine.shape[2], own_mine.shape[3]
    own_rows, far_rows = [], []
    for k in range(slices):
        for start in range(0, depth, 2 * part):
            near = pl.multiple_of(start + core * part, part)
            away = pl.multiple_of(start + part - core * part, part)
            own_rows.append(rows_ref[k, :, pl.ds(near, part)])
            far_rows.append(rows_ref[k, :, pl.ds(away, part)])
    own_rows = jnp.concatenate(own_rows, axis=1)
    far_rows = jnp.concatenate(far_rows, axis=1)

    @pl.when(pl.program_id(0) == 0)
    def _():
        for h, cols_ref in enumerate((own_mine, own_pair)):
            turned_ref[0, h] = cols_ref[:, 0].reshape(-1, unit).T

    @pl.when(pl.program_id(0) == 1)
    def _():
        for h, cols_ref in enumerate((far_mine, far_pair)):
            turned_ref[0, h] = cols_ref[:, 0].reshape(-1, unit).T

    for h, (own_ref, far_ref) in enumerate(((own_mine, far_mine), (own_pair, far_pair))):
        out_ref[h] = jnp.dot(
            own_rows, own_ref[:, 0].reshape(-1, unit), preferred_element_type=jnp.float32
        ) + jnp.dot(far_rows, far_ref[:, 0].reshape(-1, unit), preferred_element_type=jnp.float32)


def student_full(core, rows, own, far):
    slices, tokens, depth = rows.shape
    groups, _, part, unit = own.shape
    block = tokens // 2
    cols = (groups, 1, part, unit)
    mine = pl.BlockSpec(cols, lambda i, core: (0, core[0], 0, 0))
    pair = pl.BlockSpec(cols, lambda i, core: (0, 1 - core[0], 0, 0))
    return pl.pallas_call(
        student_kernel,
        grid_spec=pltpu.PrefetchScalarGridSpec(
            num_scalar_prefetch=1,
            grid=(tokens // block,),
            in_specs=[
                pl.BlockSpec((slices, block, depth), lambda i, core: (0, i, 0)),
                mine,
                pair,
                mine,
                pair,
            ],
            out_specs=[
                pl.BlockSpec((2, block, unit), lambda i, core: (0, i, 0)),
                pl.BlockSpec((1, 2, unit, groups * part), lambda i, core: (i, 0, 0, 0)),
            ],
        ),
        out_shape=[
            jax.ShapeDtypeStruct((2, tokens, unit), jnp.float32),
            jax.ShapeDtypeStruct((2, 2, unit, groups * part), own.dtype),
        ],
        compiler_params=pltpu.CompilerParams(vmem_limit_bytes=48 * 2**20),
    )(core, rows, own, own, far, far)


def grad_kernel(
    info_ref, stats_ref, digits_ref, student_ref, own_ref, pair_ref,
    turned_ref, out_ref, loss_ref, grad_ref,
):
    core = info_ref[0]
    unit = turned_ref.shape[2]
    tokens = out_ref.shape[0]
    part = lanes
    block = turned_ref.shape[3] // part

    @pl.when(pl.program_id(0) == 0)
    def _():
        stats = merged(stats_ref[...])
        student_norm = stats[0:1] + jnp.log(stats[2:3])
        teacher_norm = stats[1:2] + jnp.log(stats[3:4])
        gap = stats[4:5] / stats[2:3]
        loss = gap - student_norm + teacher_norm + ce_weight * (student_norm - stats[5:6])
        loss_ref[...] = jnp.broadcast_to(loss, loss_ref.shape)
        row = lax.broadcasted_iota(jnp.int32, (lanes, tokens), 0)
        table = jnp.where(row == 0, student_norm, jnp.where(row == 1, gap, 0.0)).T
        for h, teacher_ref in enumerate((own_ref, pair_ref)):
            student = student_ref[h]
            prob = jnp.exp(student - table[:, 0:1])
            found = hits(info_ref, h, digits_ref, (tokens, unit)).astype(jnp.float32)
            grad = prob * ((student - teacher_ref[...]) - table[:, 1:2])
            grad_ref[h] = (grad + ce_weight * (prob - found)).astype(grad_ref.dtype)

    for near, which in ((core, 0), (1 - core, 1)):
        total = jnp.dot(
            grad_ref[0], turned_ref[which, 0], preferred_element_type=jnp.float32
        ) + jnp.dot(grad_ref[1], turned_ref[which, 1], preferred_element_type=jnp.float32)
        total = total.astype(out_ref.dtype)
        for m in range(block):
            start = pl.multiple_of((2 * m + near) * part, part)
            out_ref[:, pl.ds(start, part)] = total[:, m * part : (m + 1) * part]


def grad_partial(info, stats, digits, student, teacher_own, teacher_pair, turned):
    _, tokens, unit = student.shape
    width = turned.shape[3]
    block = width // 4
    whole = [
        pl.BlockSpec(shape, lambda i, info, n=len(shape): (0,) * n)
        for shape in (
            stats.shape, digits.shape, student.shape, (tokens, unit), (tokens, unit)
        )
    ]
    return pl.pallas_call(
        grad_kernel,
        grid_spec=pltpu.PrefetchScalarGridSpec(
            num_scalar_prefetch=1,
            grid=(width // block,),
            in_specs=whole + [pl.BlockSpec((2, 2, unit, block), lambda i, info: (0, 0, 0, i))],
            out_specs=[
                pl.BlockSpec((tokens, 2 * block), lambda i, info: (0, i)),
                pl.BlockSpec((stat_rows, tokens), lambda i, info: (0, 0)),
            ],
            scratch_shapes=[pltpu.VMEM((2, tokens, unit), jnp.bfloat16)],
        ),
        out_shape=[
            jax.ShapeDtypeStruct((tokens, 2 * width), jnp.bfloat16),
            jax.ShapeDtypeStruct((stat_rows, tokens), jnp.float32),
        ],
        compiler_params=pltpu.CompilerParams(vmem_limit_bytes=40 * 2**20),
    )(info, stats, digits, student, teacher_own, teacher_pair, turned)


def local(student_hidden, teacher_hidden, student_head, teacher_head, sampled_ids):
    core = lax.axis_index("c")
    core_id = core.reshape(1).astype(jnp.int32)
    plane = lax.axis_index("z")
    tok, width = student_hidden.shape
    xy_count = lax.axis_size(XY)
    z_count = lax.axis_size("z")
    row_part = student_head.shape[0]
    unit = teacher_head.shape[1] // z_count
    depth = teacher_head.shape[0]
    share = width // z_count

    pay = jnp.concatenate(
        [
            lax.dynamic_slice_in_dim(teacher_hidden, plane * depth, depth, 1),
            lax.dynamic_slice_in_dim(student_hidden, plane * share, share, 1),
        ],
        axis=1,
    )
    teacher_head, student_head, sampled_ids, pay = lax.optimization_barrier(
        (teacher_head, student_head, sampled_ids, pay)
    )
    gathered = spread(pay, XY).reshape(-1, depth + share)
    tokens = gathered.shape[0]

    teacher_parts = teacher_regroup(teacher_head, unit)
    odd_plane = lax.rem(plane, 2)
    parts = regroup(odd_plane.reshape(1).astype(jnp.int32), student_head, z_count, unit)
    parts = parts.reshape(xy_count, 2, row_part, unit)
    digits = jnp.stack(
        [sampled_ids // (digit * digit), sampled_ids // digit % digit, sampled_ids % digit], axis=1
    ).astype(jnp.bfloat16)
    digits = jnp.pad(digits, ((0, 0), (0, lanes - 3)))
    teacher_other = swap_cores(gathered[:, :depth])
    share_rows = gathered[:, depth:]
    teacher_parts, gathered, teacher_other, share_rows, parts, digits = lax.optimization_barrier(
        (teacher_parts, gathered, teacher_other, share_rows, parts, digits)
    )

    student_rows = lax.all_gather(share_rows, "z", axis=0, tiled=False)
    teacher_cols = lax.all_to_all(
        teacher_parts, XY, 0, 0, axis_index_groups=near_groups, tiled=True
    )
    teacher_part = teacher_partial(gathered, teacher_other, teacher_cols)

    parts, student_rows, teacher_part = lax.optimization_barrier(
        (parts, student_rows, teacher_part)
    )
    teacher_sum = lax.psum_scatter(
        teacher_part.reshape(-1, unit), "z", scatter_dimension=0, tiled=True
    )
    own_cols = exchange(parts, XY)
    far_cols = swap_cores(own_cols)
    student_logits, turned = student_full(core_id, student_rows, own_cols, far_cols)
    digits, place, turned = lax.optimization_barrier((digits, lax.axis_index(XY), turned))
    id_digits = spread(digits, XY).reshape(tokens, lanes)
    teacher_sum, id_digits = lax.optimization_barrier((teacher_sum, id_digits))
    teacher_pair = swap_cores(teacher_sum[tokens:])

    row = lax.rem(place, 4)
    xyh = place // 2
    near = lax.rem(row // 2 + row, 2)
    cores = jnp.stack([core, 1 - core]).astype(jnp.int32)
    owner = (plane * 2 + lax.rem(near + plane, 2)) * 2 + cores
    info = jnp.concatenate([core_id, (owner * z_count + xyh) * unit])

    stats = local_stats(info, id_digits, student_logits, teacher_sum, teacher_pair, xy_count)
    stats = exchange(merge(exchange(stats, XY), z_count), "z")
    grad_part, losses = grad_partial(
        info, stats, id_digits, student_logits, teacher_sum, teacher_pair, turned
    )
    token_loss = lax.dynamic_slice_in_dim(losses[0], lax.axis_index(XY) * tok, tok, 0)
    grad_part = grad_part.reshape(xy_count, tok, width)
    plane_sum = jnp.sum(exchange(grad_part, XY).astype(jnp.float32), axis=0)
    plane_part = plane_sum.astype(jnp.bfloat16).reshape(tok, z_count, share).transpose(1, 0, 2)
    total = jnp.sum(exchange(plane_part, "z").astype(jnp.float32), axis=0).astype(jnp.bfloat16)
    final = spread(total, "z")
    grad_hidden = final.transpose(1, 0, 2).reshape(tok, width)
    return (grad_hidden, token_loss)


def solution(mesh):
    fine = Mesh(mesh.devices.reshape(16, 2, 8), ("xy", "c", "z"))
    in_specs = (P(DP, None), P(DP, None), P(DP, "z"), P("z", DP), P(DP))
    out_specs = (P(DP, None), P(DP))
    return jax.shard_map(local, mesh=fine, in_specs=in_specs, out_specs=out_specs, check_vma=False)
```

time: 263 us -> 258 us (0.981)
  blocking collectives: 123 us -> 164 us
  waiting for transfers between devices: 64.8 us -> 25.8 us
  starting transfers between devices: 21 us -> 10.9 us
  other arithmetic: 9.71 us -> 0.51 us
  Pallas kernels: 17 us -> 26.1 us
  local copies, waits for them, and re-layouts: 10.2 us -> 15.9 us
    all_to_all x5 -> x6, blocking collectives: 82.8 us -> 122 us  [exchange(): return lax.all_to_all(value, axes, 0, 0, tiled=True)]
    all_to_all x3 -> x2, waiting for transfers between devices: 49.8 us -> 12.6 us  [exchange(): return lax.all_to_all(value, axes, 0, 0, tiled=True)]
    all_to_all x3 -> x2, starting transfers between devices: 20.4 us -> 10.8 us  [exchange(): return lax.all_to_all(value, axes, 0, 0, tiled=True)]
    pallas_call x1 -> x3, Pallas kernels: 4.08 us -> 11.5 us  [the longest x1 8.66 us: student_full(): pl.pallas_call(student_kernel, grid_spec=pltpu.PrefetchScalarGridSpec(num...]
    reduce_scatter x1, waiting for transfers between devices: 10.3 us -> 4.38 us  [local(): lax.psum_scatter(teacher_part.reshape(-1, unit), 'z', scatter_dimension=0...]
    unnamed x11 -> x25, local copies, waits for them, and re-layouts: 4.21 us -> 9.36 us
    ppermute x6 -> x3, waiting for transfers between devices: 4.63 us -> 8.77 us  [swap_cores(): return lax.ppermute(value, 'c', [(0, 1), (1, 0)])]
    reduce_max x3 -> x0, other arithmetic: 3.69 us -> none  [the longest x1 2.37 us: local(): student_top = jnp.max(student_logits, axis=1)]
  transfers between devices with their start and end apart: 11 -> 7, of which waited for: 8 -> 6; matrix products, arithmetic and copies ran while one was open for 2% -> 0% of each run, Pallas kernels for 5% -> 7%
where the time goes in v6:
time: 258 us
  blocking collectives  164 us (64%)
  Pallas kernels  26.1 us (10%)
  waiting for transfers between devices  25.8 us (10%)
  local copies, waits for them, and re-layouts  15.9 us (6%)
  between operations  14.2 us (6%)
  starting transfers between devices  10.9 us (4%)
    all_to_all x6, blocking collectives, exchange(): return lax.all_to_all(value, axes, 0, 0, tiled=True)  122 us
    all_to_all x1, blocking collectives, local(): lax.all_to_all(teacher_parts, XY, 0, 0, axis_index_groups=near_groups, ti...  41.6 us
    all_to_all x2, waiting for transfers between devices, exchange(): return lax.all_to_all(value, axes, 0, 0, tiled=True)  12.6 us
    all_to_all x2, starting transfers between devices, exchange(): return lax.all_to_all(value, axes, 0, 0, tiled=True)  10.8 us
    unnamed x25, local copies, waits for them, and re-layouts  9.36 us
    ppermute x3, waiting for transfers between devices, swap_cores(): return lax.ppermute(value, 'c', [(0, 1), (1, 0)])  8.77 us
    pallas_call x1, Pallas kernels, student_full(): pl.pallas_call(student_kernel, grid_spec=pltpu.PrefetchScalarGridSpec(num...  8.66 us
    pallas_call x1, Pallas kernels, teacher_partial(): pl.pallas_call(teacher_kernel, grid=(units // block,), in_specs=[pl.Block...  5.17 us
  transfers between devices with their start and end apart: 7, of which 6 were waited for; matrix products, arithmetic and copies ran while one was open for 0% of the time, Pallas kernels for 7%

profile of v6, /device:TPU:8, one launch (start us, length us, event | category | flops | bytes accessed | tf_op | source)
XLA Modules:
  0.0 257.5 jit_solution(9104784037471952936)
XLA Ops:
  7.2 0.8 constant_dynamic-slice_fusion.1
  7.9 0.8 broadcast_in_dim.6
  8.8 7.4 %all-to-all-start = ((bf16[16,16,1024]{2,1,0:T(8,128)(2,1)}), bf16[16,16,1024]{2,1,0:T(8,128)(2,1)}, u32[]{:S(2)}, u32[]{:S(2)}) async-start(bf16[16,16,1024]{2,1,0:T(8,128)(2,1)} %broadcast_in_dim.6), calls=%async_computation | async-start | bytes 1048576 | tf_op jit(solution)/shard_map/all_to_all | solution.py:25
  16.2 0.0 all-gather.3.cloned.1.call-start
  16.2 0.0 copy-start.1
  16.2 3.4 %shard_map.68 = bf16[8,512,384]{2,1,0:T(8,128)(2,1)} custom-call(bf16[512,3072]{1,0:T(8,128)(2,1)} %head_ref), custom_call_target="tpu_custom_call" | custom-call | tf_op jit(solution)/shard_map/pallas_call | solution.py:114
  19.6 0.0 copy-done.1
  19.6 0.0 copy-start.11
  19.6 0.0 copy-start.9
  19.6 0.9 shard_map.69
  20.5 0.0 copy-start
  20.5 1.7 copy-done
  22.2 4.2 %all-to-all-done = bf16[16,16,1024]{2,1,0:T(8,128)(2,1)} async-done(((bf16[16,16,1024]{2,1,0:T(8,128)(2,1)}), bf16[16,16,1024]{2,1,0:T(8,128)(2,1)}, u32[]{:S(2)}, u32[]{:S(2)}) %all-to-all-start) | async-done | bytes 524320 | tf_op jit(solution)/shard_map/all_to_all | solution.py:25
  26.4 1.8 fusion.12
  28.2 0.0 collective-permute-start
  28.2 0.0 copy-done.11
  28.2 1.5 collective-permute-done.other_ref
  29.7 0.0 copy-start.10
  29.7 0.0 all-gather.3.cloned.1.call-update
  29.7 0.0 reduce-scatter.2.cloned.1.call-start
  29.8 0.0 copy-done.9
  29.8 41.6 %all_to_all.45.cols_ref = bf16[8,512,384]{2,1,0:T(8,128)(2,1)} all-to-all(bf16[8,512,384]{2,1,0:T(8,128)(2,1)S(1)} %copy-done.9), channel_id=1, replica_groups={{0,48,64,112,128,176,192,240},{16,32,80,96,144,160,208,224},{1,49,65,11..., dimensions={0} | all-to-all | bytes 6291456 | tf_op jit(solution)/shard_map/all_to_all | solution.py:351
  71.4 0.0 copy-done.10
  71.4 5.2 %shard_map.70 = f32[8,512,384]{2,1,0:T(8,128)} custom-call(bf16[256,1024]{1,0:T(8,128)(2,1)} %bitcast.1.own_ref, bf16[256,512]{1,0:T(8,128)(2,1)} %copy-done.10, bf16[8,512,384]{2,1,0:T(8,128)(2,1)} %all_to_all.45.cols_ref), custom_call_target="tpu_custom_call" | custom-call | tf_op jit(solution)/shard_map/pallas_call | solution.py:139
  76.6 0.0 reduce-scatter.2.cloned.1.call-update
  76.6 44.1 %all_to_all.46.own_mine.own_pair = bf16[16,2,128,384]{3,2,1,0:T(8,128)(2,1)S(1)} all-to-all(bf16[16,2,128,384]{3,2,1,0:T(8,128)(2,1)} %bitcast.24), channel_id=1, replica_groups=mesh['xy'=16,'c'=2,'z'=8] {'xy'}, dimensions={0} | all-to-all | bytes 6291456 | tf_op jit(solution)/shard_map/all_to_all | solution.py:25
  120.8 0.0 collective-permute-start.1
  120.8 5.8 %collective-permute-done.1.far_mine.far_pair = bf16[16,2,128,384]{3,2,1,0:T(8,128)(2,1)} collective-permute-done((bf16[16,2,128,384]{3,2,1,0:T(8,128)(2,1)S(1)}, bf16[16,2,128,384]{3,2,1,0:T(8,128)(2,1)}, u32[]{:S(2)}, u32[]{:S(2)}) %collective-permute-start.1) | collective-permute-done | bytes 3145760 | tf_op jit(solution)/shard_map/ppermute | solution.py:21
  126.5 0.0 copy-start.8
  126.5 1.6 copy-done.8
  128.1 8.7 %shard_map.71 = (f32[2,256,384]{2,1,0:T(8,128)S(1)}, bf16[2,2,384,2048]{3,2,1,0:T(8,128)(2,1)}) custom-call(s32[1]{0:T(128)} %bitcast.core_ref, bf16[8,256,512]{2,1,0:T(8,128)(2,1)S(1)} %bitcast.26, bf16[16,2,128,384]{3,2,1,0:T(8,128)(2,1)S(1)} %all_to_all.46.own_mine.own_pair, bf16[16,2,128,384]{3,2,1,0:T(8,128)(2,1)S(1)} %all_to_all.46.own_mine.own_pair, ...), custom_call_target="tpu_custom_call" | custom-call | tf_op jit(solution)/shard_map/pallas_call | solution.py:219
  136.8 0.0 copy-start.5
  136.8 0.9 copy-done.5
  137.7 0.1 copy.9
  137.8 10.9 %all_to_all.47 = bf16[16,16,128]{2,1,0:T(8,128)(2,1)S(1)} all-to-all(bf16[16,16,128]{2,1,0:T(8,128)(2,1)S(1)} %broadcast_in_dim.7), channel_id=1, replica_groups=mesh['xy'=16,'c'=2,'z'=8] {'xy'}, dimensions={0} | all-to-all | bytes 131072 | tf_op jit(solution)/shard_map/all_to_all | solution.py:25
  148.7 4.4 %reduce-scatter.2.cloned.1.call-done.own_ref = f32[512,384]{1,0:T(8,128)} async-done(((f32[4096,384]{1,0:T(8,128)}), f32[512,384]{1,0:T(8,128)}) %reduce-scatter.2.cloned.1.call-update) | async-done | bytes 786448 | tf_op jit(solution)/shard_map/reduce_scatter | solution.py:359
  153.1 0.0 copy-start.4
  153.1 1.1 slice.14
  154.2 0.1 collective-permute-start.2
  154.4 0.1 add_multiply_fusion
  154.5 0.1 pad_add_fusion.info_ref
  154.5 1.5 collective-permute-done.2.pair_ref
  156.0 0.0 copy-start.3
  156.0 1.1 copy-done.3
  157.2 0.0 copy-start.6
  157.2 1.1 copy-done.6
  158.3 0.0 copy-start.7
  158.3 1.3 shard_map.72
  159.6 13.5 %all_to_all.48.stats_ref = f32[16,8,256]{2,1,0:T(8,128)} all-to-all(f32[16,8,256]{2,1,0:T(8,128)S(1)} %shard_map.72), channel_id=1, replica_groups=mesh['xy'=16,'c'=2,'z'=8] {'xy'}, dimensions={0} | all-to-all | bytes 262144 | tf_op jit(solution)/shard_map/all_to_all | solution.py:25
  173.1 1.6 shard_map.73
  174.7 12.7 %all_to_all.49.stats_ref = f32[8,8,256]{2,1,0:T(8,128)S(1)} all-to-all(f32[8,8,256]{2,1,0:T(8,128)} %shard_map.73), channel_id=1, replica_groups=mesh['xy'=16,'c'=2,'z'=8] {'z'}, dimensions={0} | all-to-all | bytes 131072 | tf_op jit(solution)/shard_map/all_to_all | solution.py:25
  187.5 0.0 copy-done.4
  187.5 0.0 copy-done.7
  187.5 0.0 copy-start.2
  187.5 2.8 %copy-done.2 = bf16[2,2,384,2048]{3,2,1,0:T(8,128)(2,1)S(1)} copy-done((bf16[2,2,384,2048]{3,2,1,0:T(8,128)(2,1)S(1)}, bf16[2,2,384,2048]{3,2,1,0:T(8,128)(2,1)}, u32[]{:S(2)}) %copy-start.2) | copy-done | bytes 6291480
  190.3 5.2 %shard_map.74 = (bf16[256,4096]{1,0:T(8,128)(2,1)S(1)}, f32[8,256]{1,0:T(8,128)S(1)}) custom-call(s32[3]{0:T(128)S(1)} %pad_add_fusion.info_ref, f32[8,8,256]{2,1,0:T(8,128)S(1)} %all_to_all.49.stats_ref, bf16[256,128]{1,0:T(8,128)(2,1)S(1)} %bitcast.28, f32[2,256,384]{2,1,0:T(8,128)S(1)} %copy-done.7, f32[512,384]{1,0:T(8,128)S(1)} %copy-done.4, ...), custom_call_target="tpu_custom_call" | custom-call | tf_op jit(solution)/shard_map/pallas_call | solution.py:291
  195.4 29.7 %all_to_all.50 = bf16[16,16,4096]{2,1,0:T(8,128)(2,1)S(1)} all-to-all(bf16[16,16,4096]{2,1,0:T(8,128)(2,1)S(1)} %bitcast.25), channel_id=1, replica_groups=mesh['xy'=16,'c'=2,'z'=8] {'xy'}, dimensions={0} | all-to-all | bytes 4194304 | tf_op jit(solution)/shard_map/all_to_all | solution.py:25
  225.1 0.3 reduce_sum.24
  225.5 11.5 %all_to_all.51 = bf16[8,16,512]{2,1,0:T(8,128)(2,1)S(1)} all-to-all(bf16[8,16,512]{2,1,0:T(8,128)(2,1)S(1)} %copy.10), channel_id=1, replica_groups=mesh['xy'=16,'c'=2,'z'=8] {'z'}, dimensions={0} | all-to-all | bytes 262144 | tf_op jit(solution)/shard_map/all_to_all | solution.py:25
  237.0 0.7 broadcast_in_dim.8
  237.6 3.4 %all-to-all-start.8 = ((bf16[8,16,512]{2,1,0:T(8,128)(2,1)}), bf16[8,16,512]{2,1,0:T(8,128)(2,1)S(1)}, u32[]{:S(2)}, u32[]{:S(2)}) async-start(bf16[8,16,512]{2,1,0:T(8,128)(2,1)} %broadcast_in_dim.8), calls=%async_computation.9 | async-start | bytes 262144 | tf_op jit(solution)/shard_map/all_to_all | solution.py:25
  241.0 0.6 fusion.5
  241.6 8.4 %all-to-all-done.8 = bf16[8,16,512]{2,1,0:T(8,128)(2,1)S(1)} async-done(((bf16[8,16,512]{2,1,0:T(8,128)(2,1)}), bf16[8,16,512]{2,1,0:T(8,128)(2,1)S(1)}, u32[]{:S(2)}, u32[]{:S(2)}) %all-to-all-start.8) | async-done | bytes 131104 | tf_op jit(solution)/shard_map/all_to_all | solution.py:25
  250.0 0.7 copy.12
  (9 shorter events, 0.2 us)
Async XLA Ops:
  8.8 17.6 %all-to-all-start = ((bf16[16,16,1024]{2,1,0:T(8,128)(2,1)}), bf16[16,16,1024]{2,1,0:T(8,128)(2,1)}, u32[]{:S(2)}, u32[]{:S(2)}) async-start(bf16[16,16,1024]{2,1,0:T(8,128)(2,1)} %broadcast_in_dim.6), calls=%async_computation | async-start | bytes 1048576 | tf_op jit(solution)/shard_map/all_to_all | solution.py:25
  16.2 60.4 %all-gather.3.cloned.1.call-start = ((), (), s32[]{:S(2)}) async-start(), calls=%async_computation.11 | async-start | bytes 2359296 | tf_op jit(solution)/shard_map/all_gather | solution.py:350
  16.2 3.4 %copy-start.1 = (bf16[128,12288]{1,0:T(8,128)(2,1)S(1)}, bf16[128,12288]{1,0:T(8,128)(2,1)}, u32[]{:S(2)}) copy-start(bf16[128,12288]{1,0:T(8,128)(2,1)} %high_ref) | copy-start | bytes 9437188
  19.6 8.6 %copy-start.11 = (s32[16]{0:T(128)S(1)}, s32[16]{0:T(128)}, u32[]{:S(2)}) copy-start(s32[16]{0:T(128)} %param.9) | copy-start | bytes 196
  19.6 10.2 %copy-start.9 = (bf16[8,512,384]{2,1,0:T(8,128)(2,1)S(1)}, bf16[8,512,384]{2,1,0:T(8,128)(2,1)}, u32[]{:S(2)}) copy-start(bf16[8,512,384]{2,1,0:T(8,128)(2,1)} %shard_map.68) | copy-start | bytes 9437188
  20.5 1.7 copy-start
  28.2 1.5 collective-permute-start
  29.7 41.7 %copy-start.10 = (bf16[256,512]{1,0:T(8,128)(2,1)}, bf16[256,512]{1,0:T(8,128)(2,1)S(1)}, u32[]{:S(2)}) copy-start(bf16[256,512]{1,0:T(8,128)(2,1)S(1)} %collective-permute-done.other_ref) | copy-start | bytes 786436
  29.7 123.4 %reduce-scatter.2.cloned.1.call-start = ((), (), s32[]{:S(2)}) async-start(), calls=%async_computation.10 | async-start | bytes 7077888 | tf_op jit(solution)/shard_map/reduce_scatter | solution.py:359
  120.8 5.8 %collective-permute-start.1 = (bf16[16,2,128,384]{3,2,1,0:T(8,128)(2,1)S(1)}, bf16[16,2,128,384]{3,2,1,0:T(8,128)(2,1)}, u32[]{:S(2)}, u32[]{:S(2)}) collective-permute-start(bf16[16,2,128,384]{3,2,1,0:T(8,128)(2,1)S(1)} %all_to_all.46.own_mine.own_pair), channel_id=1, source_target_pairs={{0,8},{8,0},{1,9},{9,1},{2,10},{10,2},{3,11},{11,3},{4,12},{12,4},... | collective-permute-start | bytes 9437192 | tf_op jit(solution)/shard_map/ppermute | solution.py:21
  126.5 1.6 copy-start.8
  136.8 0.9 copy-start.5
  153.1 34.3 %copy-start.4 = (f32[512,384]{1,0:T(8,128)S(1)}, f32[512,384]{1,0:T(8,128)}, u32[]{:S(2)}) copy-start(f32[512,384]{1,0:T(8,128)} %reduce-scatter.2.cloned.1.call-done.own_ref) | copy-start | bytes 2359300
  154.2 1.8 collective-permute-start.2
  156.0 1.1 copy-start.3
  157.2 1.1 copy-start.6
  158.3 29.2 %copy-start.7 = (f32[2,256,384]{2,1,0:T(8,128)S(1)}, f32[2,256,384]{2,1,0:T(8,128)}, u32[]{:S(2)}) copy-start(f32[2,256,384]{2,1,0:T(8,128)} %copy-done.5) | copy-start | bytes 2359300
  187.5 2.8 %copy-start.2 = (bf16[2,2,384,2048]{3,2,1,0:T(8,128)(2,1)S(1)}, bf16[2,2,384,2048]{3,2,1,0:T(8,128)(2,1)}, u32[]{:S(2)}) copy-start(bf16[2,2,384,2048]{3,2,1,0:T(8,128)(2,1)} %get-tuple-element.43.turned_ref) | copy-start | bytes 18874372
  237.6 12.4 %all-to-all-start.8 = ((bf16[8,16,512]{2,1,0:T(8,128)(2,1)}), bf16[8,16,512]{2,1,0:T(8,128)(2,1)S(1)}, u32[]{:S(2)}, u32[]{:S(2)}) async-start(bf16[8,16,512]{2,1,0:T(8,128)(2,1)} %broadcast_in_dim.8), calls=%async_computation.9 | async-start | bytes 262144 | tf_op jit(solution)/shard_map/all_to_all | solution.py:25
Sparse Core Ops, SparseCore 0:
  29.9 41.5 all-gather.2
  76.8 76.3 reduce-scatter.1

commit v7 on v6

--- a/solution.py
+++ b/solution.py
@@ -8,7 +8,7 @@
 ce_weight = 0.5
 digit = 64
 lanes = 128
-stat_rows = 8
+stat_rows = 4
 big_vmem = 56 * 2**20
 XY = "xy"
 DP = ("xy", "c")
@@ -53,31 +53,27 @@
         sums = [a + jnp.sum(b, axis=1, keepdims=True) for a, b in zip(sums, terms)]
     lane = lax.broadcasted_iota(jnp.int32, (tokens, lanes), 1)
     table = jnp.zeros((tokens, lanes), jnp.float32)
-    for k, column in enumerate(tops + sums):
+    for k, column in zip((0, 4, 1, 5, 2, 6), tops + sums):
         table = jnp.where(lane == k, column, table)
-    out_ref[...] = jnp.broadcast_to(table.T[: out_ref.shape[1]], out_ref.shape)
+    table = table.T
+    table = jnp.concatenate([table[:stat_rows], table[stat_rows : 2 * stat_rows]], axis=1)
+    out_ref[...] = jnp.broadcast_to(table, out_ref.shape)
 
 
 def merged(stats):
-    tops = jnp.max(stats, axis=0)
-    scale = jnp.exp(stats - tops[None])
-    row = lax.broadcasted_iota(jnp.int32, stats.shape, 1)
-    weight = jnp.where((row == 2) | (row == 4), scale[:, 0:1], 0.0)
-    weight = jnp.where(row == 3, scale[:, 1:2], weight)
-    weight = jnp.where(row == 5, 1.0, weight)
-    total = jnp.sum(stats * weight, axis=0)
-    return jnp.where(lax.broadcasted_iota(jnp.int32, tops.shape, 0) < 2, tops, total)
-
-
-def merge_kernel(stats_ref, out_ref):
-    out_ref[...] = jnp.broadcast_to(merged(stats_ref[...]), out_ref.shape)
-
-
-def merge(stats, copies):
-    return pl.pallas_call(
-        merge_kernel,
-        out_shape=jax.ShapeDtypeStruct((copies,) + stats.shape[1:], jnp.float32),
-    )(stats)
+    half = stats.shape[2] // 2
+    tops = jnp.max(stats[:, 0], axis=0, keepdims=True)
+    scale = jnp.exp(stats[:, 0] - tops)
+    sums = jnp.sum(stats[:, 1] * scale, axis=0, keepdims=True)
+    cross = jnp.sum(stats[:, 2, :half] * scale[:, :half], axis=0, keepdims=True)
+    picked = jnp.sum(stats[:, 2, half:], axis=0, keepdims=True)
+    return tops, sums, cross, picked
+
+
+def merge(stats):
+    tops, sums, cross, picked = merged(stats)
+    last = jnp.concatenate([cross, picked], axis=1)
+    return jnp.concatenate([tops, sums, last, jnp.zeros_like(last)], axis=0)
 
 
 def local_stats(info, digits, student, teacher, pair, copies):
@@ -94,9 +90,9 @@
                 pl.BlockSpec((tokens, unit), first),
                 pl.BlockSpec((tokens, unit), first),
             ],
-            out_specs=pl.BlockSpec((copies, stat_rows, tokens), lambda i, info: (0, 0, 0)),
+            out_specs=pl.BlockSpec((copies, stat_rows, 2 * tokens), lambda i, info: (0, 0, 0)),
         ),
-        out_shape=jax.ShapeDtypeStruct((copies, stat_rows, tokens), jnp.float32),
+        out_shape=jax.ShapeDtypeStruct((copies, stat_rows, 2 * tokens), jnp.float32),
         compiler_params=pltpu.CompilerParams(vmem_limit_bytes=32 * 2**20),
     )(info, digits, student, teacher, pair)
 
@@ -253,11 +249,11 @@
 
     @pl.when(pl.program_id(0) == 0)
     def _():
-        stats = merged(stats_ref[...])
-        student_norm = stats[0:1] + jnp.log(stats[2:3])
-        teacher_norm = stats[1:2] + jnp.log(stats[3:4])
-        gap = stats[4:5] / stats[2:3]
-        loss = gap - student_norm + teacher_norm + ce_weight * (student_norm - stats[5:6])
+        tops, sums, cross, picked = merged(stats_ref[...])
+        norms = tops + jnp.log(sums)
+        student_norm, teacher_norm = norms[:, :tokens], norms[:, tokens:]
+        gap = cross / sums[:, :tokens]
+        loss = gap - student_norm + teacher_norm + ce_weight * (student_norm - picked)
         loss_ref[...] = jnp.broadcast_to(loss, loss_ref.shape)
         row = lax.broadcasted_iota(jnp.int32, (lanes, tokens), 0)
         table = jnp.where(row == 0, student_norm, jnp.where(row == 1, gap, 0.0)).T
@@ -308,6 +304,25 @@
     )(info, stats, digits, student, teacher_own, teacher_pair, turned)
 
 
+def sum_kernel(parts_ref, out_ref):
+    share = out_ref.shape[2]
+    for k in range(out_ref.shape[0]):
+        part = parts_ref[:, :, k * share : (k + 1) * share].astype(jnp.float32)
+        out_ref[k] = jnp.sum(part, axis=0).astype(out_ref.dtype)
+
+
+def plane_sums(parts, count):
+    _, rows, width = parts.shape
+    whole = pl.BlockSpec(memory_space=pltpu.VMEM)
+    return pl.pallas_call(
+        sum_kernel,
+        in_specs=[whole],
+        out_specs=whole,
+        out_shape=jax.ShapeDtypeStruct((count, rows, width // count), parts.dtype),
+        compiler_params=pltpu.CompilerParams(vmem_limit_bytes=16 * 2**20),
+    )(parts)
+
+
 def local(student_hidden, teacher_hidden, student_head, teacher_head, sampled_ids):
     core = lax.axis_index("c")
     core_id = core.reshape(1).astype(jnp.int32)
@@ -375,14 +390,13 @@
     info = jnp.concatenate([core_id, (owner * z_count + xyh) * unit])
 
     stats = local_stats(info, id_digits, student_logits, teacher_sum, teacher_pair, xy_count)
-    stats = exchange(merge(exchange(stats, XY), z_count), "z")
+    stats = spread(merge(exchange(stats, XY)), "z")
     grad_part, losses = grad_partial(
         info, stats, id_digits, student_logits, teacher_sum, teacher_pair, turned
     )
     token_loss = lax.dynamic_slice_in_dim(losses[0], lax.axis_index(XY) * tok, tok, 0)
     grad_part = grad_part.reshape(xy_count, tok, width)
-    plane_sum = jnp.sum(exchange(grad_part, XY).astype(jnp.float32), axis=0)
-    plane_part = plane_sum.astype(jnp.bfloat16).reshape(tok, z_count, share).transpose(1, 0, 2)
+    plane_part = plane_sums(exchange(grad_part, XY), z_count)
     total = jnp.sum(exchange(plane_part, "z").astype(jnp.float32), axis=0).astype(jnp.bfloat16)
     final = spread(total, "z")
     grad_hidden = final.transpose(1, 0, 2).reshape(tok, width)

time: 258 us -> 257 us (level)
  blocking collectives: 164 us -> 150 us
  starting transfers between devices: 10.9 us -> 18.2 us
  waiting for transfers between devices: 25.8 us -> 32.1 us
    all_to_all x6 -> x5, blocking collectives: 122 us -> 109 us  [exchange(): return lax.all_to_all(value, axes, 0, 0, tiled=True)]
    all_to_all x2 -> x3, starting transfers between devices: 10.8 us -> 18 us  [exchange(): return lax.all_to_all(value, axes, 0, 0, tiled=True)]
    all_to_all x2 -> x3, waiting for transfers between devices: 12.6 us -> 18.9 us  [exchange(): return lax.all_to_all(value, axes, 0, 0, tiled=True)]
    unnamed x25 -> x24, local copies, waits for them, and re-layouts: 9.36 us -> 9.31 us
  transfers between devices with their start and end apart: 7 -> 8, of which waited for: 6 -> 7; matrix products, arithmetic and copies ran while one was open for 0% -> 0% of each run, Pallas kernels for 7% -> 7%
where the time goes in v7:
time: 257 us
  blocking collectives  150 us (58%)
  waiting for transfers between devices  32.1 us (12%)
  Pallas kernels  25.4 us (10%)
  starting transfers between devices  18.2 us (7%)
  local copies, waits for them, and re-layouts  15.9 us (6%)
  between operations  14.2 us (6%)
    all_to_all x5, blocking collectives, exchange(): return lax.all_to_all(value, axes, 0, 0, tiled=True)  109 us
    all_to_all x1, blocking collectives, local(): lax.all_to_all(teacher_parts, XY, 0, 0, axis_index_groups=near_groups, ti...  41.6 us
    all_to_all x3, waiting for transfers between devices, exchange(): return lax.all_to_all(value, axes, 0, 0, tiled=True)  18.9 us
    all_to_all x3, starting transfers between devices, exchange(): return lax.all_to_all(value, axes, 0, 0, tiled=True)  18 us
    unnamed x24, local copies, waits for them, and re-layouts  9.31 us
    ppermute x3, waiting for transfers between devices, swap_cores(): return lax.ppermute(value, 'c', [(0, 1), (1, 0)])  8.77 us
    pallas_call x1, Pallas kernels, student_full(): pl.pallas_call(student_kernel, grid_spec=pltpu.PrefetchScalarGridSpec(num...  8.66 us
    pallas_call x1, Pallas kernels, teacher_partial(): pl.pallas_call(teacher_kernel, grid=(units // block,), in_specs=[pl.Block...  5.17 us
  transfers between devices with their start and end apart: 8, of which 7 were waited for; matrix products, arithmetic and copies ran while one was open for 0% of the time, Pallas kernels for 7%

profile of v7, /device:TPU:8, one launch (start us, length us, event | category | flops | bytes accessed | tf_op | source)
XLA Modules:
  0.0 256.6 jit_solution(6158375196334371759)
XLA Ops:
  7.2 0.7 constant_dynamic-slice_fusion.1
  7.9 0.9 broadcast_in_dim.18
  8.8 7.4 %all-to-all-start = ((bf16[16,16,1024]{2,1,0:T(8,128)(2,1)}), bf16[16,16,1024]{2,1,0:T(8,128)(2,1)}, u32[]{:S(2)}, u32[]{:S(2)}) async-start(bf16[16,16,1024]{2,1,0:T(8,128)(2,1)} %broadcast_in_dim.18), calls=%async_computation | async-start | bytes 1048576 | tf_op jit(solution)/shard_map/all_to_all | solution.py:25
  16.2 0.0 all-gather.3.cloned.1.call-start
  16.2 0.0 copy-start.1
  16.2 3.4 %shard_map.68 = bf16[8,512,384]{2,1,0:T(8,128)(2,1)} custom-call(bf16[512,3072]{1,0:T(8,128)(2,1)} %head_ref), custom_call_target="tpu_custom_call" | custom-call | tf_op jit(solution)/shard_map/pallas_call | solution.py:110
  19.6 0.0 copy-done.1
  19.6 0.0 copy-start.11
  19.6 0.0 copy-start.9
  19.6 0.9 shard_map.69
  20.5 0.0 copy-start
  20.5 1.7 copy-done
  22.2 4.2 %all-to-all-done = bf16[16,16,1024]{2,1,0:T(8,128)(2,1)} async-done(((bf16[16,16,1024]{2,1,0:T(8,128)(2,1)}), bf16[16,16,1024]{2,1,0:T(8,128)(2,1)}, u32[]{:S(2)}, u32[]{:S(2)}) %all-to-all-start) | async-done | bytes 524320 | tf_op jit(solution)/shard_map/all_to_all | solution.py:25
  26.4 1.8 fusion.18
  28.2 0.0 collective-permute-start
  28.2 0.0 copy-done.11
  28.2 1.5 collective-permute-done.other_ref
  29.7 0.0 copy-start.10
  29.7 0.0 all-gather.3.cloned.1.call-update
  29.7 0.0 reduce-scatter.2.cloned.1.call-start
  29.8 0.0 copy-done.9
  29.8 41.6 %all_to_all.45.cols_ref = bf16[8,512,384]{2,1,0:T(8,128)(2,1)} all-to-all(bf16[8,512,384]{2,1,0:T(8,128)(2,1)S(1)} %copy-done.9), channel_id=1, replica_groups={{0,48,64,112,128,176,192,240},{16,32,80,96,144,160,208,224},{1,49,65,11..., dimensions={0} | all-to-all | bytes 6291456 | tf_op jit(solution)/shard_map/all_to_all | solution.py:366
  71.4 0.0 copy-done.10
  71.4 5.2 %shard_map.70 = f32[8,512,384]{2,1,0:T(8,128)} custom-call(bf16[256,1024]{1,0:T(8,128)(2,1)} %bitcast.1.own_ref, bf16[256,512]{1,0:T(8,128)(2,1)} %copy-done.10, bf16[8,512,384]{2,1,0:T(8,128)(2,1)} %all_to_all.45.cols_ref), custom_call_target="tpu_custom_call" | custom-call | tf_op jit(solution)/shard_map/pallas_call | solution.py:135
  76.6 0.0 all-gather.3.cloned.1.call-done
  76.6 0.0 reduce-scatter.2.cloned.1.call-update
  76.6 44.1 %all_to_all.46.own_mine.own_pair = bf16[16,2,128,384]{3,2,1,0:T(8,128)(2,1)S(1)} all-to-all(bf16[16,2,128,384]{3,2,1,0:T(8,128)(2,1)} %bitcast.40), channel_id=1, replica_groups=mesh['xy'=16,'c'=2,'z'=8] {'xy'}, dimensions={0} | all-to-all | bytes 6291456 | tf_op jit(solution)/shard_map/all_to_all | solution.py:25
  120.7 0.0 collective-permute-start.1
  120.7 5.8 %collective-permute-done.1.far_mine.far_pair = bf16[16,2,128,384]{3,2,1,0:T(8,128)(2,1)} collective-permute-done((bf16[16,2,128,384]{3,2,1,0:T(8,128)(2,1)S(1)}, bf16[16,2,128,384]{3,2,1,0:T(8,128)(2,1)}, u32[]{:S(2)}, u32[]{:S(2)}) %collective-permute-start.1) | collective-permute-done | bytes 3145760 | tf_op jit(solution)/shard_map/ppermute | solution.py:21
  126.5 0.0 copy-start.8
  126.5 1.6 copy-done.8
  128.1 8.7 %shard_map.71 = (f32[2,256,384]{2,1,0:T(8,128)S(1)}, bf16[2,2,384,2048]{3,2,1,0:T(8,128)(2,1)}) custom-call(s32[1]{0:T(128)} %bitcast.core_ref, bf16[8,256,512]{2,1,0:T(8,128)(2,1)S(1)} %bitcast.42, bf16[16,2,128,384]{3,2,1,0:T(8,128)(2,1)S(1)} %all_to_all.46.own_mine.own_pair, bf16[16,2,128,384]{3,2,1,0:T(8,128)(2,1)S(1)} %all_to_all.46.own_mine.own_pair, ...), custom_call_target="tpu_custom_call" | custom-call | tf_op jit(solution)/shard_map/pallas_call | solution.py:215
  136.8 0.0 copy-start.5
  136.8 0.9 copy-done.5
  137.7 0.1 copy.13
  137.8 10.9 %all_to_all.47 = bf16[16,16,128]{2,1,0:T(8,128)(2,1)S(1)} all-to-all(bf16[16,16,128]{2,1,0:T(8,128)(2,1)S(1)} %broadcast_in_dim.19), channel_id=1, replica_groups=mesh['xy'=16,'c'=2,'z'=8] {'xy'}, dimensions={0} | all-to-all | bytes 131072 | tf_op jit(solution)/shard_map/all_to_all | solution.py:25
  148.7 4.4 %reduce-scatter.2.cloned.1.call-done.own_ref = f32[512,384]{1,0:T(8,128)} async-done(((f32[4096,384]{1,0:T(8,128)}), f32[512,384]{1,0:T(8,128)}) %reduce-scatter.2.cloned.1.call-update) | async-done | bytes 786448 | tf_op jit(solution)/shard_map/reduce_scatter | solution.py:374
  153.1 1.1 slice.30
  154.2 0.1 collective-permute-start.2
  154.4 0.1 add_multiply_fusion
  154.5 0.1 pad_add_fusion.info_ref
  154.6 1.5 collective-permute-done.2.pair_ref
  156.0 1.1 copy-done.3
  157.2 1.1 copy-done.6
  158.3 1.9 shard_map.72
  160.3 7.2 %all-to-all-start.4 = ((f32[16,4,512]{2,1,0:T(4,128)}), f32[16,4,512]{2,1,0:T(4,128)S(1)}, u32[]{:S(2)}, u32[]{:S(2)}) async-start(f32[16,4,512]{2,1,0:T(4,128)} %shard_map.72), calls=%async_computation.5 | async-start | bytes 262144 | tf_op jit(solution)/shard_map/all_to_all | solution.py:25
  167.5 0.1 pad.9.clone
  167.6 6.3 %all-to-all-done.4 = f32[16,4,512]{2,1,0:T(4,128)S(1)} async-done(((f32[16,4,512]{2,1,0:T(4,128)}), f32[16,4,512]{2,1,0:T(4,128)S(1)}, u32[]{:S(2)}, u32[]{:S(2)}) %all-to-all-start.4) | async-done | bytes 131104 | tf_op jit(solution)/shard_map/all_to_all | solution.py:25
  173.9 0.1 fusion.20
  174.0 0.1 fusion.19
  174.1 0.1 maximum_maximum_fusion
  174.2 12.5 %all_to_all.48.stats_ref = f32[8,4,512]{2,1,0:T(4,128)S(1)} all-to-all(f32[8,4,512]{2,1,0:T(4,128)S(1)} %broadcast_in_dim.46), channel_id=1, replica_groups=mesh['xy'=16,'c'=2,'z'=8] {'z'}, dimensions={0} | all-to-all | bytes 131072 | tf_op jit(solution)/shard_map/all_to_all | solution.py:25
  186.7 0.0 copy-done.4
  186.7 0.0 copy-done.7
  186.7 2.8 %copy-done.2 = bf16[2,2,384,2048]{3,2,1,0:T(8,128)(2,1)S(1)} copy-done((bf16[2,2,384,2048]{3,2,1,0:T(8,128)(2,1)S(1)}, bf16[2,2,384,2048]{3,2,1,0:T(8,128)(2,1)}, u32[]{:S(2)}) %copy-start.2) | copy-done | bytes 6291480
  189.5 5.1 %shard_map.73 = (bf16[256,4096]{1,0:T(8,128)(2,1)S(1)}, f32[4,256]{1,0:T(4,128)S(1)}) custom-call(s32[3]{0:T(128)S(1)} %pad_add_fusion.info_ref, f32[8,4,512]{2,1,0:T(4,128)S(1)} %all_to_all.48.stats_ref, bf16[256,128]{1,0:T(8,128)(2,1)S(1)} %bitcast.44, f32[2,256,384]{2,1,0:T(8,128)S(1)} %copy-done.7, f32[512,384]{1,0:T(8,128)S(1)} %copy-done.4, ...), custom_call_target="tpu_custom_call" | custom-call | tf_op jit(solution)/shard_map/pallas_call | solution.py:287
  194.6 29.7 %all_to_all.49.parts_ref = bf16[16,16,4096]{2,1,0:T(8,128)(2,1)S(1)} all-to-all(bf16[16,16,4096]{2,1,0:T(8,128)(2,1)S(1)} %bitcast.41), channel_id=1, replica_groups=mesh['xy'=16,'c'=2,'z'=8] {'xy'}, dimensions={0} | all-to-all | bytes 4194304 | tf_op jit(solution)/shard_map/all_to_all | solution.py:25
  224.3 0.3 shard_map.74
  224.6 11.5 %all_to_all.50 = bf16[8,16,512]{2,1,0:T(8,128)(2,1)S(1)} all-to-all(bf16[8,16,512]{2,1,0:T(8,128)(2,1)S(1)} %shard_map.74), channel_id=1, replica_groups=mesh['xy'=16,'c'=2,'z'=8] {'z'}, dimensions={0} | all-to-all | bytes 262144 | tf_op jit(solution)/shard_map/all_to_all | solution.py:25
  236.1 0.7 broadcast_in_dim.47
  236.7 3.4 %all-to-all-start.8 = ((bf16[8,16,512]{2,1,0:T(8,128)(2,1)}), bf16[8,16,512]{2,1,0:T(8,128)(2,1)S(1)}, u32[]{:S(2)}, u32[]{:S(2)}) async-start(bf16[8,16,512]{2,1,0:T(8,128)(2,1)} %broadcast_in_dim.47), calls=%async_computation.9 | async-start | bytes 262144 | tf_op jit(solution)/shard_map/all_to_all | solution.py:25
  240.1 0.6 fusion.10
  240.7 8.4 %all-to-all-done.8 = bf16[8,16,512]{2,1,0:T(8,128)(2,1)S(1)} async-done(((bf16[8,16,512]{2,1,0:T(8,128)(2,1)}), bf16[8,16,512]{2,1,0:T(8,128)(2,1)S(1)}, u32[]{:S(2)}, u32[]{:S(2)}) %all-to-all-start.8) | async-done | bytes 131104 | tf_op jit(solution)/shard_map/all_to_all | solution.py:25
  249.1 0.7 copy.21
  (14 shorter events, 0.2 us)
Async XLA Ops:
  8.8 17.6 %all-to-all-start = ((bf16[16,16,1024]{2,1,0:T(8,128)(2,1)}), bf16[16,16,1024]{2,1,0:T(8,128)(2,1)}, u32[]{:S(2)}, u32[]{:S(2)}) async-start(bf16[16,16,1024]{2,1,0:T(8,128)(2,1)} %broadcast_in_dim.18), calls=%async_computation | async-start | bytes 1048576 | tf_op jit(solution)/shard_map/all_to_all | solution.py:25
  16.2 60.4 %all-gather.3.cloned.1.call-start = ((), (), s32[]{:S(2)}) async-start(), calls=%async_computation.11 | async-start | bytes 2359296 | tf_op jit(solution)/shard_map/all_gather | solution.py:365
  16.2 3.4 %copy-start.1 = (bf16[128,12288]{1,0:T(8,128)(2,1)S(1)}, bf16[128,12288]{1,0:T(8,128)(2,1)}, u32[]{:S(2)}) copy-start(bf16[128,12288]{1,0:T(8,128)(2,1)} %high_ref) | copy-start | bytes 9437188
  19.6 8.6 %copy-start.11 = (s32[16]{0:T(128)S(1)}, s32[16]{0:T(128)}, u32[]{:S(2)}) copy-start(s32[16]{0:T(128)} %param.9) | copy-start | bytes 196
  19.6 10.2 %copy-start.9 = (bf16[8,512,384]{2,1,0:T(8,128)(2,1)S(1)}, bf16[8,512,384]{2,1,0:T(8,128)(2,1)}, u32[]{:S(2)}) copy-start(bf16[8,512,384]{2,1,0:T(8,128)(2,1)} %shard_map.68) | copy-start | bytes 9437188
  20.5 1.7 copy-start
  28.2 1.5 collective-permute-start
  29.7 41.7 %copy-start.10 = (bf16[256,512]{1,0:T(8,128)(2,1)}, bf16[256,512]{1,0:T(8,128)(2,1)S(1)}, u32[]{:S(2)}) copy-start(bf16[256,512]{1,0:T(8,128)(2,1)S(1)} %collective-permute-done.other_ref) | copy-start | bytes 786436
  29.7 123.4 %reduce-scatter.2.cloned.1.call-start = ((), (), s32[]{:S(2)}) async-start(), calls=%async_computation.10 | async-start | bytes 7077888 | tf_op jit(solution)/shard_map/reduce_scatter | solution.py:374
  120.7 5.8 %collective-permute-start.1 = (bf16[16,2,128,384]{3,2,1,0:T(8,128)(2,1)S(1)}, bf16[16,2,128,384]{3,2,1,0:T(8,128)(2,1)}, u32[]{:S(2)}, u32[]{:S(2)}) collective-permute-start(bf16[16,2,128,384]{3,2,1,0:T(8,128)(2,1)S(1)} %all_to_all.46.own_mine.own_pair), channel_id=1, source_target_pairs={{0,8},{8,0},{1,9},{9,1},{2,10},{10,2},{3,11},{11,3},{4,12},{12,4},... | collective-permute-start | bytes 9437192 | tf_op jit(solution)/shard_map/ppermute | solution.py:21
  126.5 1.6 copy-start.8
  136.8 0.9 copy-start.5
  153.1 33.6 %copy-start.4 = (f32[512,384]{1,0:T(8,128)S(1)}, f32[512,384]{1,0:T(8,128)}, u32[]{:S(2)}) copy-start(f32[512,384]{1,0:T(8,128)} %reduce-scatter.2.cloned.1.call-done.own_ref) | copy-start | bytes 2359300
  154.2 1.8 collective-permute-start.2
  156.0 1.1 copy-start.3
  157.2 1.1 copy-start.6
  158.3 28.4 %copy-start.7 = (f32[2,256,384]{2,1,0:T(8,128)S(1)}, f32[2,256,384]{2,1,0:T(8,128)}, u32[]{:S(2)}) copy-start(f32[2,256,384]{2,1,0:T(8,128)} %copy-done.5) | copy-start | bytes 2359300
  160.3 13.6 %all-to-all-start.4 = ((f32[16,4,512]{2,1,0:T(4,128)}), f32[16,4,512]{2,1,0:T(4,128)S(1)}, u32[]{:S(2)}, u32[]{:S(2)}) async-start(f32[16,4,512]{2,1,0:T(4,128)} %shard_map.72), calls=%async_computation.5 | async-start | bytes 262144 | tf_op jit(solution)/shard_map/all_to_all | solution.py:25
  186.7 2.8 %copy-start.2 = (bf16[2,2,384,2048]{3,2,1,0:T(8,128)(2,1)S(1)}, bf16[2,2,384,2048]{3,2,1,0:T(8,128)(2,1)}, u32[]{:S(2)}) copy-start(bf16[2,2,384,2048]{3,2,1,0:T(8,128)(2,1)} %get-tuple-element.43.turned_ref) | copy-start | bytes 18874372
  236.7 12.4 %all-to-all-start.8 = ((bf16[8,16,512]{2,1,0:T(8,128)(2,1)}), bf16[8,16,512]{2,1,0:T(8,128)(2,1)S(1)}, u32[]{:S(2)}, u32[]{:S(2)}) async-start(bf16[8,16,512]{2,1,0:T(8,128)(2,1)} %broadcast_in_dim.47), calls=%async_computation.9 | async-start | bytes 262144 | tf_op jit(solution)/shard_map/all_to_all | solution.py:25
Sparse Core Ops, SparseCore 0:
  29.9 41.5 all-gather.2
  76.7 76.3 reduce-scatter.1

commit v8 on v7

--- a/solution.py
+++ b/solution.py
@@ -77,7 +77,7 @@
 
 
 def local_stats(info, digits, student, teacher, pair, copies):
-    tokens, unit = pair.shape
+    tokens, unit = pair.shape[0] // 2, pair.shape[1]
     first = lambda i, info: (0, 0)
     return pl.pallas_call(
         stats_kernel,
@@ -88,7 +88,7 @@
                 pl.BlockSpec(digits.shape, first),
                 pl.BlockSpec(student.shape, lambda i, info: (0, 0, 0)),
                 pl.BlockSpec((tokens, unit), first),
-                pl.BlockSpec((tokens, unit), first),
+                pl.BlockSpec((tokens, unit), lambda i, info: (1, 0)),
             ],
             out_specs=pl.BlockSpec((copies, stat_rows, 2 * tokens), lambda i, info: (0, 0, 0)),
         ),
@@ -281,9 +281,10 @@
     whole = [
         pl.BlockSpec(shape, lambda i, info, n=len(shape): (0,) * n)
         for shape in (
-            stats.shape, digits.shape, student.shape, (tokens, unit), (tokens, unit)
+            stats.shape, digits.shape, student.shape, (tokens, unit)
         )
     ]
+    whole.append(pl.BlockSpec((tokens, unit), lambda i, info: (1, 0)))
     return pl.pallas_call(
         grad_kernel,
         grid_spec=pltpu.PrefetchScalarGridSpec(
@@ -380,7 +381,7 @@
     digits, place, turned = lax.optimization_barrier((digits, lax.axis_index(XY), turned))
     id_digits = spread(digits, XY).reshape(tokens, lanes)
     teacher_sum, id_digits = lax.optimization_barrier((teacher_sum, id_digits))
-    teacher_pair = swap_cores(teacher_sum[tokens:])
+    teacher_pair = swap_cores(teacher_sum)
 
     row = lax.rem(place, 4)
     xyh = place // 2

time: 257 us -> 257 us (level)
  no operation moved by 1% of the time
where the time goes in v8:
time: 257 us; the launch traced here: 256 us
  blocking collectives  150 us (58%)
  waiting for transfers between devices  33 us (13%)
  Pallas kernels  25.4 us (10%)
  starting transfers between devices  18.1 us (7%)
  local copies, waits for them, and re-layouts  14.8 us (6%)
  between operations  14.2 us (6%)
    all_to_all x5, blocking collectives, exchange(): return lax.all_to_all(value, axes, 0, 0, tiled=True)  109 us
    all_to_all x1, blocking collectives, local(): lax.all_to_all(teacher_parts, XY, 0, 0, axis_index_groups=near_groups, ti...  41.6 us
    all_to_all x3, waiting for transfers between devices, exchange(): return lax.all_to_all(value, axes, 0, 0, tiled=True)  18.9 us
    all_to_all x3, starting transfers between devices, exchange(): return lax.all_to_all(value, axes, 0, 0, tiled=True)  18 us
    ppermute x3, waiting for transfers between devices, swap_cores(): return lax.ppermute(value, 'c', [(0, 1), (1, 0)])  9.61 us
    unnamed x24, local copies, waits for them, and re-layouts  9.31 us
    pallas_call x1, Pallas kernels, student_full(): pl.pallas_call(student_kernel, grid_spec=pltpu.PrefetchScalarGridSpec(num...  8.66 us
    pallas_call x1, Pallas kernels, teacher_partial(): pl.pallas_call(teacher_kernel, grid=(units // block,), in_specs=[pl.Block...  5.17 us
  transfers between devices with their start and end apart: 8, of which 7 were waited for; matrix products, arithmetic and copies ran while one was open for 0% of the time, Pallas kernels for 7%

profile of v8, /device:TPU:8, one launch (start us, length us, event | category | flops | bytes accessed | tf_op | source)
XLA Modules:
  0.0 256.2 jit_solution(17418167976875653630)
XLA Ops:
  7.2 0.7 constant_dynamic-slice_fusion.1
  7.9 0.9 broadcast_in_dim.18
  8.8 7.4 %all-to-all-start = ((bf16[16,16,1024]{2,1,0:T(8,128)(2,1)}), bf16[16,16,1024]{2,1,0:T(8,128)(2,1)}, u32[]{:S(2)}, u32[]{:S(2)}) async-start(bf16[16,16,1024]{2,1,0:T(8,128)(2,1)} %broadcast_in_dim.18), calls=%async_computation | async-start | bytes 1048576 | tf_op jit(solution)/shard_map/all_to_all | solution.py:25
  16.2 0.0 all-gather.3.cloned.1.call-start
  16.2 0.0 copy-start.1
  16.2 3.4 %shard_map.68 = bf16[8,512,384]{2,1,0:T(8,128)(2,1)} custom-call(bf16[512,3072]{1,0:T(8,128)(2,1)} %head_ref), custom_call_target="tpu_custom_call" | custom-call | tf_op jit(solution)/shard_map/pallas_call | solution.py:110
  19.6 0.0 copy-done.1
  19.6 0.0 copy-start.11
  19.6 0.0 copy-start.9
  19.6 0.9 shard_map.69
  20.5 0.0 copy-start
  20.5 1.7 copy-done
  22.2 4.2 %all-to-all-done = bf16[16,16,1024]{2,1,0:T(8,128)(2,1)} async-done(((bf16[16,16,1024]{2,1,0:T(8,128)(2,1)}), bf16[16,16,1024]{2,1,0:T(8,128)(2,1)}, u32[]{:S(2)}, u32[]{:S(2)}) %all-to-all-start) | async-done | bytes 524320 | tf_op jit(solution)/shard_map/all_to_all | solution.py:25
  26.4 1.8 fusion.18
  28.2 0.0 collective-permute-start
  28.2 0.0 copy-done.11
  28.2 1.5 collective-permute-done.other_ref
  29.7 0.0 copy-start.10
  29.7 0.0 all-gather.3.cloned.1.call-update
  29.7 0.0 reduce-scatter.2.cloned.1.call-start
  29.8 0.0 copy-done.9
  29.8 41.6 %all_to_all.45.cols_ref = bf16[8,512,384]{2,1,0:T(8,128)(2,1)} all-to-all(bf16[8,512,384]{2,1,0:T(8,128)(2,1)S(1)} %copy-done.9), channel_id=1, replica_groups={{0,48,64,112,128,176,192,240},{16,32,80,96,144,160,208,224},{1,49,65,11..., dimensions={0} | all-to-all | bytes 6291456 | tf_op jit(solution)/shard_map/all_to_all | solution.py:367
  71.4 0.0 copy-done.10
  71.4 5.2 %shard_map.70 = f32[8,512,384]{2,1,0:T(8,128)} custom-call(bf16[256,1024]{1,0:T(8,128)(2,1)} %bitcast.1.own_ref, bf16[256,512]{1,0:T(8,128)(2,1)} %copy-done.10, bf16[8,512,384]{2,1,0:T(8,128)(2,1)} %all_to_all.45.cols_ref), custom_call_target="tpu_custom_call" | custom-call | tf_op jit(solution)/shard_map/pallas_call | solution.py:135
  76.6 0.0 all-gather.3.cloned.1.call-done
  76.6 0.0 reduce-scatter.2.cloned.1.call-update
  76.6 44.1 %all_to_all.46.own_mine.own_pair = bf16[16,2,128,384]{3,2,1,0:T(8,128)(2,1)S(1)} all-to-all(bf16[16,2,128,384]{3,2,1,0:T(8,128)(2,1)} %bitcast.40), channel_id=1, replica_groups=mesh['xy'=16,'c'=2,'z'=8] {'xy'}, dimensions={0} | all-to-all | bytes 6291456 | tf_op jit(solution)/shard_map/all_to_all | solution.py:25
  120.7 0.0 collective-permute-start.1
  120.7 5.8 %collective-permute-done.1.far_mine.far_pair = bf16[16,2,128,384]{3,2,1,0:T(8,128)(2,1)} collective-permute-done((bf16[16,2,128,384]{3,2,1,0:T(8,128)(2,1)S(1)}, bf16[16,2,128,384]{3,2,1,0:T(8,128)(2,1)}, u32[]{:S(2)}, u32[]{:S(2)}) %collective-permute-start.1) | collective-permute-done | bytes 3145760 | tf_op jit(solution)/shard_map/ppermute | solution.py:21
  126.5 0.0 copy-start.8
  126.5 1.6 copy-done.8
  128.1 8.7 %shard_map.71 = (f32[2,256,384]{2,1,0:T(8,128)S(1)}, bf16[2,2,384,2048]{3,2,1,0:T(8,128)(2,1)}) custom-call(s32[1]{0:T(128)} %bitcast.core_ref, bf16[8,256,512]{2,1,0:T(8,128)(2,1)S(1)} %bitcast.42, bf16[16,2,128,384]{3,2,1,0:T(8,128)(2,1)S(1)} %all_to_all.46.own_mine.own_pair, bf16[16,2,128,384]{3,2,1,0:T(8,128)(2,1)S(1)} %all_to_all.46.own_mine.own_pair, ...), custom_call_target="tpu_custom_call" | custom-call | tf_op jit(solution)/shard_map/pallas_call | solution.py:215
  136.8 0.0 copy-start.5
  136.8 0.9 copy-done.5
  137.7 0.1 copy.13
  137.8 10.9 %all_to_all.47 = bf16[16,16,128]{2,1,0:T(8,128)(2,1)S(1)} all-to-all(bf16[16,16,128]{2,1,0:T(8,128)(2,1)S(1)} %broadcast_in_dim.19), channel_id=1, replica_groups=mesh['xy'=16,'c'=2,'z'=8] {'xy'}, dimensions={0} | all-to-all | bytes 131072 | tf_op jit(solution)/shard_map/all_to_all | solution.py:25
  148.7 4.4 %reduce-scatter.2.cloned.1.call-done.own_ref = f32[512,384]{1,0:T(8,128)} async-done(((f32[4096,384]{1,0:T(8,128)}), f32[512,384]{1,0:T(8,128)}) %reduce-scatter.2.cloned.1.call-update) | async-done | bytes 786448 | tf_op jit(solution)/shard_map/reduce_scatter | solution.py:375
  153.1 0.0 collective-permute-start.2
  153.1 0.1 add_multiply_fusion
  153.2 0.1 pad_add_fusion.info_ref
  153.3 2.3 collective-permute-done.2.pair_ref
  155.6 0.0 copy-start.3
  155.6 1.1 copy-done.3
  156.8 1.1 copy-done.6
  157.9 1.9 shard_map.72
  159.8 7.2 %all-to-all-start.4 = ((f32[16,4,512]{2,1,0:T(4,128)}), f32[16,4,512]{2,1,0:T(4,128)S(1)}, u32[]{:S(2)}, u32[]{:S(2)}) async-start(f32[16,4,512]{2,1,0:T(4,128)} %shard_map.72), calls=%async_computation.5 | async-start | bytes 262144 | tf_op jit(solution)/shard_map/all_to_all | solution.py:25
  167.1 0.1 pad.9.clone
  167.2 6.3 %all-to-all-done.4 = f32[16,4,512]{2,1,0:T(4,128)S(1)} async-done(((f32[16,4,512]{2,1,0:T(4,128)}), f32[16,4,512]{2,1,0:T(4,128)S(1)}, u32[]{:S(2)}, u32[]{:S(2)}) %all-to-all-start.4) | async-done | bytes 131104 | tf_op jit(solution)/shard_map/all_to_all | solution.py:25
  173.5 0.1 fusion.20
  173.6 0.1 fusion.19
  173.7 0.1 maximum_maximum_fusion
  173.7 12.5 %all_to_all.48.stats_ref = f32[8,4,512]{2,1,0:T(4,128)S(1)} all-to-all(f32[8,4,512]{2,1,0:T(4,128)S(1)} %broadcast_in_dim.46), channel_id=1, replica_groups=mesh['xy'=16,'c'=2,'z'=8] {'z'}, dimensions={0} | all-to-all | bytes 131072 | tf_op jit(solution)/shard_map/all_to_all | solution.py:25
  186.3 0.0 copy-done.4
  186.3 0.0 copy-done.7
  186.3 2.8 %copy-done.2 = bf16[2,2,384,2048]{3,2,1,0:T(8,128)(2,1)S(1)} copy-done((bf16[2,2,384,2048]{3,2,1,0:T(8,128)(2,1)S(1)}, bf16[2,2,384,2048]{3,2,1,0:T(8,128)(2,1)}, u32[]{:S(2)}) %copy-start.2) | copy-done | bytes 6291480
  189.1 5.1 %shard_map.73 = (bf16[256,4096]{1,0:T(8,128)(2,1)S(1)}, f32[4,256]{1,0:T(4,128)S(1)}) custom-call(s32[3]{0:T(128)S(1)} %pad_add_fusion.info_ref, f32[8,4,512]{2,1,0:T(4,128)S(1)} %all_to_all.48.stats_ref, bf16[256,128]{1,0:T(8,128)(2,1)S(1)} %bitcast.44, f32[2,256,384]{2,1,0:T(8,128)S(1)} %copy-done.7, f32[512,384]{1,0:T(8,128)S(1)} %copy-done.4, ...), custom_call_target="tpu_custom_call" | custom-call | tf_op jit(solution)/shard_map/pallas_call | solution.py:288
  194.2 29.7 %all_to_all.49.parts_ref = bf16[16,16,4096]{2,1,0:T(8,128)(2,1)S(1)} all-to-all(bf16[16,16,4096]{2,1,0:T(8,128)(2,1)S(1)} %bitcast.41), channel_id=1, replica_groups=mesh['xy'=16,'c'=2,'z'=8] {'xy'}, dimensions={0} | all-to-all | bytes 4194304 | tf_op jit(solution)/shard_map/all_to_all | solution.py:25
  223.9 0.3 shard_map.74
  224.2 11.5 %all_to_all.50 = bf16[8,16,512]{2,1,0:T(8,128)(2,1)S(1)} all-to-all(bf16[8,16,512]{2,1,0:T(8,128)(2,1)S(1)} %shard_map.74), channel_id=1, replica_groups=mesh['xy'=16,'c'=2,'z'=8] {'z'}, dimensions={0} | all-to-all | bytes 262144 | tf_op jit(solution)/shard_map/all_to_all | solution.py:25
  235.6 0.7 broadcast_in_dim.47
  236.3 3.4 %all-to-all-start.8 = ((bf16[8,16,512]{2,1,0:T(8,128)(2,1)}), bf16[8,16,512]{2,1,0:T(8,128)(2,1)S(1)}, u32[]{:S(2)}, u32[]{:S(2)}) async-start(bf16[8,16,512]{2,1,0:T(8,128)(2,1)} %broadcast_in_dim.47), calls=%async_computation.9 | async-start | bytes 262144 | tf_op jit(solution)/shard_map/all_to_all | solution.py:25
  239.7 0.6 fusion.10
  240.3 8.4 %all-to-all-done.8 = bf16[8,16,512]{2,1,0:T(8,128)(2,1)S(1)} async-done(((bf16[8,16,512]{2,1,0:T(8,128)(2,1)}), bf16[8,16,512]{2,1,0:T(8,128)(2,1)S(1)}, u32[]{:S(2)}, u32[]{:S(2)}) %all-to-all-start.8) | async-done | bytes 131104 | tf_op jit(solution)/shard_map/all_to_all | solution.py:25
  248.7 0.7 copy.21
  (13 shorter events, 0.2 us)
Async XLA Ops:
  8.8 17.6 %all-to-all-start = ((bf16[16,16,1024]{2,1,0:T(8,128)(2,1)}), bf16[16,16,1024]{2,1,0:T(8,128)(2,1)}, u32[]{:S(2)}, u32[]{:S(2)}) async-start(bf16[16,16,1024]{2,1,0:T(8,128)(2,1)} %broadcast_in_dim.18), calls=%async_computation | async-start | bytes 1048576 | tf_op jit(solution)/shard_map/all_to_all | solution.py:25
  16.2 60.4 %all-gather.3.cloned.1.call-start = ((), (), s32[]{:S(2)}) async-start(), calls=%async_computation.11 | async-start | bytes 2359296 | tf_op jit(solution)/shard_map/all_gather | solution.py:366
  16.2 3.4 %copy-start.1 = (bf16[128,12288]{1,0:T(8,128)(2,1)S(1)}, bf16[128,12288]{1,0:T(8,128)(2,1)}, u32[]{:S(2)}) copy-start(bf16[128,12288]{1,0:T(8,128)(2,1)} %high_ref) | copy-start | bytes 9437188
  19.6 8.6 %copy-start.11 = (s32[16]{0:T(128)S(1)}, s32[16]{0:T(128)}, u32[]{:S(2)}) copy-start(s32[16]{0:T(128)} %param.9) | copy-start | bytes 196
  19.6 10.2 %copy-start.9 = (bf16[8,512,384]{2,1,0:T(8,128)(2,1)S(1)}, bf16[8,512,384]{2,1,0:T(8,128)(2,1)}, u32[]{:S(2)}) copy-start(bf16[8,512,384]{2,1,0:T(8,128)(2,1)} %shard_map.68) | copy-start | bytes 9437188
  20.5 1.7 copy-start
  28.2 1.5 collective-permute-start
  29.7 41.7 %copy-start.10 = (bf16[256,512]{1,0:T(8,128)(2,1)}, bf16[256,512]{1,0:T(8,128)(2,1)S(1)}, u32[]{:S(2)}) copy-start(bf16[256,512]{1,0:T(8,128)(2,1)S(1)} %collective-permute-done.other_ref) | copy-start | bytes 786436
  29.7 123.4 %reduce-scatter.2.cloned.1.call-start = ((), (), s32[]{:S(2)}) async-start(), calls=%async_computation.10 | async-start | bytes 7077888 | tf_op jit(solution)/shard_map/reduce_scatter | solution.py:375
  120.7 5.8 %collective-permute-start.1 = (bf16[16,2,128,384]{3,2,1,0:T(8,128)(2,1)S(1)}, bf16[16,2,128,384]{3,2,1,0:T(8,128)(2,1)}, u32[]{:S(2)}, u32[]{:S(2)}) collective-permute-start(bf16[16,2,128,384]{3,2,1,0:T(8,128)(2,1)S(1)} %all_to_all.46.own_mine.own_pair), channel_id=1, source_target_pairs={{0,8},{8,0},{1,9},{9,1},{2,10},{10,2},{3,11},{11,3},{4,12},{12,4},... | collective-permute-start | bytes 9437192 | tf_op jit(solution)/shard_map/ppermute | solution.py:21
  126.5 1.6 copy-start.8
  136.8 0.9 copy-start.5
  153.1 2.5 collective-permute-start.2
  155.6 1.1 copy-start.3
  156.8 1.1 copy-start.6
  157.9 28.4 %copy-start.4 = (f32[512,384]{1,0:T(8,128)S(1)}, f32[512,384]{1,0:T(8,128)}, u32[]{:S(2)}) copy-start(f32[512,384]{1,0:T(8,128)} %reduce-scatter.2.cloned.1.call-done.own_ref) | copy-start | bytes 2359300
  157.9 28.4 %copy-start.7 = (f32[2,256,384]{2,1,0:T(8,128)S(1)}, f32[2,256,384]{2,1,0:T(8,128)}, u32[]{:S(2)}) copy-start(f32[2,256,384]{2,1,0:T(8,128)} %copy-done.5) | copy-start | bytes 2359300
  159.8 13.6 %all-to-all-start.4 = ((f32[16,4,512]{2,1,0:T(4,128)}), f32[16,4,512]{2,1,0:T(4,128)S(1)}, u32[]{:S(2)}, u32[]{:S(2)}) async-start(f32[16,4,512]{2,1,0:T(4,128)} %shard_map.72), calls=%async_computation.5 | async-start | bytes 262144 | tf_op jit(solution)/shard_map/all_to_all | solution.py:25
  186.3 2.8 %copy-start.2 = (bf16[2,2,384,2048]{3,2,1,0:T(8,128)(2,1)S(1)}, bf16[2,2,384,2048]{3,2,1,0:T(8,128)(2,1)}, u32[]{:S(2)}) copy-start(bf16[2,2,384,2048]{3,2,1,0:T(8,128)(2,1)} %get-tuple-element.43.turned_ref) | copy-start | bytes 18874372
  236.3 12.4 %all-to-all-start.8 = ((bf16[8,16,512]{2,1,0:T(8,128)(2,1)}), bf16[8,16,512]{2,1,0:T(8,128)(2,1)S(1)}, u32[]{:S(2)}, u32[]{:S(2)}) async-start(bf16[8,16,512]{2,1,0:T(8,128)(2,1)} %broadcast_in_dim.47), calls=%async_computation.9 | async-start | bytes 262144 | tf_op jit(solution)/shard_map/all_to_all | solution.py:25
Sparse Core Ops, SparseCore 0:
  29.9 41.5 all-gather.2
  76.7 76.3 reduce-scatter.1

commit v9 on v8

--- a/solution.py
+++ b/solution.py
@@ -324,6 +324,22 @@
     )(parts)
 
 
+def copies_kernel(parts_ref, out_ref):
+    total = jnp.sum(parts_ref[...].astype(jnp.float32), axis=0).astype(out_ref.dtype)
+    out_ref[...] = jnp.broadcast_to(total, out_ref.shape)
+
+
+def summed_copies(parts):
+    whole = pl.BlockSpec(memory_space=pltpu.VMEM)
+    return pl.pallas_call(
+        copies_kernel,
+        in_specs=[whole],
+        out_specs=whole,
+        out_shape=jax.ShapeDtypeStruct(parts.shape, parts.dtype),
+        compiler_params=pltpu.CompilerParams(vmem_limit_bytes=16 * 2**20),
+    )(parts)
+
+
 def local(student_hidden, teacher_hidden, student_head, teacher_head, sampled_ids):
     core = lax.axis_index("c")
     core_id = core.reshape(1).astype(jnp.int32)
@@ -398,8 +414,7 @@
     token_loss = lax.dynamic_slice_in_dim(losses[0], lax.axis_index(XY) * tok, tok, 0)
     grad_part = grad_part.reshape(xy_count, tok, width)
     plane_part = plane_sums(exchange(grad_part, XY), z_count)
-    total = jnp.sum(exchange(plane_part, "z").astype(jnp.float32), axis=0).astype(jnp.bfloat16)
-    final = spread(total, "z")
+    final = exchange(summed_copies(exchange(plane_part, "z")), "z")
     grad_hidden = final.transpose(1, 0, 2).reshape(tok, width)
     return (grad_hidden, token_loss)
 

time: 257 us -> 257 us (level)
  no operation moved by 1% of the time
where the time goes in v9:
time: 257 us; the launch traced here: 256 us
  blocking collectives  150 us (58%)
  waiting for transfers between devices  32.9 us (13%)
  Pallas kernels  26.1 us (10%)
  starting transfers between devices  18.1 us (7%)
  local copies, waits for them, and re-layouts  14.2 us (6%)
  between operations  14.1 us (5%)
    all_to_all x5, blocking collectives, exchange(): return lax.all_to_all(value, axes, 0, 0, tiled=True)  109 us
    all_to_all x1, blocking collectives, local(): lax.all_to_all(teacher_parts, XY, 0, 0, axis_index_groups=near_groups, ti...  41.6 us
    all_to_all x3, waiting for transfers between devices, exchange(): return lax.all_to_all(value, axes, 0, 0, tiled=True)  18.9 us
    all_to_all x3, starting transfers between devices, exchange(): return lax.all_to_all(value, axes, 0, 0, tiled=True)  18 us
    ppermute x3, waiting for transfers between devices, swap_cores(): return lax.ppermute(value, 'c', [(0, 1), (1, 0)])  9.61 us
    unnamed x24, local copies, waits for them, and re-layouts  9.33 us
    pallas_call x1, Pallas kernels, student_full(): pl.pallas_call(student_kernel, grid_spec=pltpu.PrefetchScalarGridSpec(num...  8.66 us
    pallas_call x1, Pallas kernels, teacher_partial(): pl.pallas_call(teacher_kernel, grid=(units // block,), in_specs=[pl.Block...  5.18 us
  transfers between devices with their start and end apart: 8, of which 7 were waited for; matrix products, arithmetic and copies ran while one was open for 0% of the time, Pallas kernels for 7%

profile of v9, /device:TPU:8, one launch (start us, length us, event | category | flops | bytes accessed | tf_op | source)
XLA Modules:
  0.0 256.2 jit_solution(43313508247817549)
XLA Ops:
  7.2 0.7 constant_dynamic-slice_fusion.1
  7.9 0.9 broadcast_in_dim.16
  8.8 7.4 %all-to-all-start = ((bf16[16,16,1024]{2,1,0:T(8,128)(2,1)}), bf16[16,16,1024]{2,1,0:T(8,128)(2,1)}, u32[]{:S(2)}, u32[]{:S(2)}) async-start(bf16[16,16,1024]{2,1,0:T(8,128)(2,1)} %broadcast_in_dim.16), calls=%async_computation | async-start | bytes 1048576 | tf_op jit(solution)/shard_map/all_to_all | solution.py:25
  16.2 0.0 all-gather.3.cloned.1.call-start
  16.2 0.0 copy-start.1
  16.2 3.4 %shard_map.68 = bf16[8,512,384]{2,1,0:T(8,128)(2,1)} custom-call(bf16[512,3072]{1,0:T(8,128)(2,1)} %head_ref), custom_call_target="tpu_custom_call" | custom-call | tf_op jit(solution)/shard_map/pallas_call | solution.py:110
  19.6 0.0 copy-done.1
  19.6 0.0 copy-start.11
  19.6 0.0 copy-start.9
  19.6 0.9 shard_map.69
  20.5 0.0 copy-start
  20.5 1.7 copy-done
  22.2 4.2 %all-to-all-done = bf16[16,16,1024]{2,1,0:T(8,128)(2,1)} async-done(((bf16[16,16,1024]{2,1,0:T(8,128)(2,1)}), bf16[16,16,1024]{2,1,0:T(8,128)(2,1)}, u32[]{:S(2)}, u32[]{:S(2)}) %all-to-all-start) | async-done | bytes 524320 | tf_op jit(solution)/shard_map/all_to_all | solution.py:25
  26.4 1.8 fusion.18
  28.2 0.0 collective-permute-start
  28.2 0.0 copy-done.11
  28.2 1.5 collective-permute-done.other_ref
  29.7 0.0 copy-start.10
  29.7 0.0 all-gather.3.cloned.1.call-update
  29.8 0.0 reduce-scatter.2.cloned.1.call-start
  29.8 0.0 copy-done.9
  29.8 41.6 %all_to_all.45.cols_ref = bf16[8,512,384]{2,1,0:T(8,128)(2,1)} all-to-all(bf16[8,512,384]{2,1,0:T(8,128)(2,1)S(1)} %copy-done.9), channel_id=1, replica_groups={{0,48,64,112,128,176,192,240},{16,32,80,96,144,160,208,224},{1,49,65,11..., dimensions={0} | all-to-all | bytes 6291456 | tf_op jit(solution)/shard_map/all_to_all | solution.py:383
  71.5 0.0 copy-done.10
  71.5 5.2 %shard_map.70 = f32[8,512,384]{2,1,0:T(8,128)} custom-call(bf16[256,1024]{1,0:T(8,128)(2,1)} %bitcast.1.own_ref, bf16[256,512]{1,0:T(8,128)(2,1)} %copy-done.10, bf16[8,512,384]{2,1,0:T(8,128)(2,1)} %all_to_all.45.cols_ref), custom_call_target="tpu_custom_call" | custom-call | tf_op jit(solution)/shard_map/pallas_call | solution.py:135
  76.6 0.0 all-gather.3.cloned.1.call-done
  76.6 0.0 reduce-scatter.2.cloned.1.call-update
  76.7 44.1 %all_to_all.46.own_mine.own_pair = bf16[16,2,128,384]{3,2,1,0:T(8,128)(2,1)S(1)} all-to-all(bf16[16,2,128,384]{3,2,1,0:T(8,128)(2,1)} %bitcast.40), channel_id=1, replica_groups=mesh['xy'=16,'c'=2,'z'=8] {'xy'}, dimensions={0} | all-to-all | bytes 6291456 | tf_op jit(solution)/shard_map/all_to_all | solution.py:25
  120.8 0.0 collective-permute-start.1
  120.8 5.8 %collective-permute-done.1.far_mine.far_pair = bf16[16,2,128,384]{3,2,1,0:T(8,128)(2,1)} collective-permute-done((bf16[16,2,128,384]{3,2,1,0:T(8,128)(2,1)S(1)}, bf16[16,2,128,384]{3,2,1,0:T(8,128)(2,1)}, u32[]{:S(2)}, u32[]{:S(2)}) %collective-permute-start.1) | collective-permute-done | bytes 3145760 | tf_op jit(solution)/shard_map/ppermute | solution.py:21
  126.6 0.0 copy-start.8
  126.6 1.6 copy-done.8
  128.2 8.7 %shard_map.71 = (f32[2,256,384]{2,1,0:T(8,128)S(1)}, bf16[2,2,384,2048]{3,2,1,0:T(8,128)(2,1)}) custom-call(s32[1]{0:T(128)} %bitcast.core_ref, bf16[8,256,512]{2,1,0:T(8,128)(2,1)S(1)} %bitcast.42, bf16[16,2,128,384]{3,2,1,0:T(8,128)(2,1)S(1)} %all_to_all.46.own_mine.own_pair, bf16[16,2,128,384]{3,2,1,0:T(8,128)(2,1)S(1)} %all_to_all.46.own_mine.own_pair, ...), custom_call_target="tpu_custom_call" | custom-call | tf_op jit(solution)/shard_map/pallas_call | solution.py:215
  136.8 0.0 copy-start.5
  136.8 0.9 copy-done.5
  137.8 0.1 copy.10
  137.9 10.9 %all_to_all.47 = bf16[16,16,128]{2,1,0:T(8,128)(2,1)S(1)} all-to-all(bf16[16,16,128]{2,1,0:T(8,128)(2,1)S(1)} %broadcast_in_dim.34), channel_id=1, replica_groups=mesh['xy'=16,'c'=2,'z'=8] {'xy'}, dimensions={0} | all-to-all | bytes 131072 | tf_op jit(solution)/shard_map/all_to_all | solution.py:25
  148.8 4.4 %reduce-scatter.2.cloned.1.call-done.own_ref = f32[512,384]{1,0:T(8,128)} async-done(((f32[4096,384]{1,0:T(8,128)}), f32[512,384]{1,0:T(8,128)}) %reduce-scatter.2.cloned.1.call-update) | async-done | bytes 786448 | tf_op jit(solution)/shard_map/reduce_scatter | solution.py:391
  153.2 0.0 collective-permute-start.2
  153.2 0.1 add_multiply_fusion
  153.3 0.1 pad_add_fusion.info_ref
  153.3 2.3 collective-permute-done.2.pair_ref
  155.7 0.0 copy-start.3
  155.7 1.1 copy-done.3
  156.8 1.1 copy-done.6
  157.9 1.9 shard_map.72
  159.9 7.2 %all-to-all-start.4 = ((f32[16,4,512]{2,1,0:T(4,128)}), f32[16,4,512]{2,1,0:T(4,128)S(1)}, u32[]{:S(2)}, u32[]{:S(2)}) async-start(f32[16,4,512]{2,1,0:T(4,128)} %shard_map.72), calls=%async_computation.5 | async-start | bytes 262144 | tf_op jit(solution)/shard_map/all_to_all | solution.py:25
  167.1 0.1 pad.9.clone
  167.2 6.3 %all-to-all-done.4 = f32[16,4,512]{2,1,0:T(4,128)S(1)} async-done(((f32[16,4,512]{2,1,0:T(4,128)}), f32[16,4,512]{2,1,0:T(4,128)S(1)}, u32[]{:S(2)}, u32[]{:S(2)}) %all-to-all-start.4) | async-done | bytes 131104 | tf_op jit(solution)/shard_map/all_to_all | solution.py:25
  173.5 0.1 fusion.20
  173.6 0.1 fusion.19
  173.7 0.1 maximum_maximum_fusion
  173.8 12.5 %all_to_all.48.stats_ref = f32[8,4,512]{2,1,0:T(4,128)S(1)} all-to-all(f32[8,4,512]{2,1,0:T(4,128)S(1)} %broadcast_in_dim.40), channel_id=1, replica_groups=mesh['xy'=16,'c'=2,'z'=8] {'z'}, dimensions={0} | all-to-all | bytes 131072 | tf_op jit(solution)/shard_map/all_to_all | solution.py:25
  186.3 0.0 copy-done.4
  186.3 0.0 copy-done.7
  186.3 2.8 %copy-done.2 = bf16[2,2,384,2048]{3,2,1,0:T(8,128)(2,1)S(1)} copy-done((bf16[2,2,384,2048]{3,2,1,0:T(8,128)(2,1)S(1)}, bf16[2,2,384,2048]{3,2,1,0:T(8,128)(2,1)}, u32[]{:S(2)}) %copy-start.2) | copy-done | bytes 6291480
  189.1 5.1 %shard_map.73 = (bf16[256,4096]{1,0:T(8,128)(2,1)S(1)}, f32[4,256]{1,0:T(4,128)S(1)}) custom-call(s32[3]{0:T(128)S(1)} %pad_add_fusion.info_ref, f32[8,4,512]{2,1,0:T(4,128)S(1)} %all_to_all.48.stats_ref, bf16[256,128]{1,0:T(8,128)(2,1)S(1)} %bitcast.44, f32[2,256,384]{2,1,0:T(8,128)S(1)} %copy-done.7, f32[512,384]{1,0:T(8,128)S(1)} %copy-done.4, ...), custom_call_target="tpu_custom_call" | custom-call | tf_op jit(solution)/shard_map/pallas_call | solution.py:288
  194.3 29.7 %all_to_all.49.parts_ref = bf16[16,16,4096]{2,1,0:T(8,128)(2,1)S(1)} all-to-all(bf16[16,16,4096]{2,1,0:T(8,128)(2,1)S(1)} %bitcast.41), channel_id=1, replica_groups=mesh['xy'=16,'c'=2,'z'=8] {'xy'}, dimensions={0} | all-to-all | bytes 4194304 | tf_op jit(solution)/shard_map/all_to_all | solution.py:25
  223.9 0.3 shard_map.74
  224.2 11.5 %all_to_all.50.parts_ref = bf16[8,16,512]{2,1,0:T(8,128)(2,1)S(1)} all-to-all(bf16[8,16,512]{2,1,0:T(8,128)(2,1)S(1)} %shard_map.74), channel_id=1, replica_groups=mesh['xy'=16,'c'=2,'z'=8] {'z'}, dimensions={0} | all-to-all | bytes 262144 | tf_op jit(solution)/shard_map/all_to_all | solution.py:25
  235.7 0.7 shard_map.75
  236.3 3.4 %all-to-all-start.8 = ((bf16[8,16,512]{2,1,0:T(8,128)(2,1)}), bf16[8,16,512]{2,1,0:T(8,128)(2,1)S(1)}, u32[]{:S(2)}, u32[]{:S(2)}) async-start(bf16[8,16,512]{2,1,0:T(8,128)(2,1)} %shard_map.75), calls=%async_computation.9 | async-start | bytes 262144 | tf_op jit(solution)/shard_map/all_to_all | solution.py:25
  239.7 0.6 fusion.10
  240.3 8.4 %all-to-all-done.8 = bf16[8,16,512]{2,1,0:T(8,128)(2,1)S(1)} async-done(((bf16[8,16,512]{2,1,0:T(8,128)(2,1)}), bf16[8,16,512]{2,1,0:T(8,128)(2,1)S(1)}, u32[]{:S(2)}, u32[]{:S(2)}) %all-to-all-start.8) | async-done | bytes 131104 | tf_op jit(solution)/shard_map/all_to_all | solution.py:25
  248.7 0.7 copy.18
  (12 shorter events, 0.1 us)
Async XLA Ops:
  8.8 17.6 %all-to-all-start = ((bf16[16,16,1024]{2,1,0:T(8,128)(2,1)}), bf16[16,16,1024]{2,1,0:T(8,128)(2,1)}, u32[]{:S(2)}, u32[]{:S(2)}) async-start(bf16[16,16,1024]{2,1,0:T(8,128)(2,1)} %broadcast_in_dim.16), calls=%async_computation | async-start | bytes 1048576 | tf_op jit(solution)/shard_map/all_to_all | solution.py:25
  16.2 60.5 %all-gather.3.cloned.1.call-start = ((), (), s32[]{:S(2)}) async-start(), calls=%async_computation.11 | async-start | bytes 2359296 | tf_op jit(solution)/shard_map/all_gather | solution.py:382
  16.2 3.4 %copy-start.1 = (bf16[128,12288]{1,0:T(8,128)(2,1)S(1)}, bf16[128,12288]{1,0:T(8,128)(2,1)}, u32[]{:S(2)}) copy-start(bf16[128,12288]{1,0:T(8,128)(2,1)} %high_ref) | copy-start | bytes 9437188
  19.6 8.6 %copy-start.11 = (s32[16]{0:T(128)S(1)}, s32[16]{0:T(128)}, u32[]{:S(2)}) copy-start(s32[16]{0:T(128)} %param.9) | copy-start | bytes 196
  19.6 10.2 %copy-start.9 = (bf16[8,512,384]{2,1,0:T(8,128)(2,1)S(1)}, bf16[8,512,384]{2,1,0:T(8,128)(2,1)}, u32[]{:S(2)}) copy-start(bf16[8,512,384]{2,1,0:T(8,128)(2,1)} %shard_map.68) | copy-start | bytes 9437188
  20.5 1.7 copy-start
  28.2 1.5 collective-permute-start
  29.7 41.7 %copy-start.10 = (bf16[256,512]{1,0:T(8,128)(2,1)}, bf16[256,512]{1,0:T(8,128)(2,1)S(1)}, u32[]{:S(2)}) copy-start(bf16[256,512]{1,0:T(8,128)(2,1)S(1)} %collective-permute-done.other_ref) | copy-start | bytes 786436
  29.8 123.4 %reduce-scatter.2.cloned.1.call-start = ((), (), s32[]{:S(2)}) async-start(), calls=%async_computation.10 | async-start | bytes 7077888 | tf_op jit(solution)/shard_map/reduce_scatter | solution.py:391
  120.8 5.8 %collective-permute-start.1 = (bf16[16,2,128,384]{3,2,1,0:T(8,128)(2,1)S(1)}, bf16[16,2,128,384]{3,2,1,0:T(8,128)(2,1)}, u32[]{:S(2)}, u32[]{:S(2)}) collective-permute-start(bf16[16,2,128,384]{3,2,1,0:T(8,128)(2,1)S(1)} %all_to_all.46.own_mine.own_pair), channel_id=1, source_target_pairs={{0,8},{8,0},{1,9},{9,1},{2,10},{10,2},{3,11},{11,3},{4,12},{12,4},... | collective-permute-start | bytes 9437192 | tf_op jit(solution)/shard_map/ppermute | solution.py:21
  126.6 1.6 copy-start.8
  136.8 0.9 copy-start.5
  153.2 2.5 collective-permute-start.2
  155.7 1.1 copy-start.3
  156.8 1.1 copy-start.6
  157.9 28.4 %copy-start.4 = (f32[512,384]{1,0:T(8,128)S(1)}, f32[512,384]{1,0:T(8,128)}, u32[]{:S(2)}) copy-start(f32[512,384]{1,0:T(8,128)} %reduce-scatter.2.cloned.1.call-done.own_ref) | copy-start | bytes 2359300
  157.9 28.4 %copy-start.7 = (f32[2,256,384]{2,1,0:T(8,128)S(1)}, f32[2,256,384]{2,1,0:T(8,128)}, u32[]{:S(2)}) copy-start(f32[2,256,384]{2,1,0:T(8,128)} %copy-done.5) | copy-start | bytes 2359300
  159.9 13.6 %all-to-all-start.4 = ((f32[16,4,512]{2,1,0:T(4,128)}), f32[16,4,512]{2,1,0:T(4,128)S(1)}, u32[]{:S(2)}, u32[]{:S(2)}) async-start(f32[16,4,512]{2,1,0:T(4,128)} %shard_map.72), calls=%async_computation.5 | async-start | bytes 262144 | tf_op jit(solution)/shard_map/all_to_all | solution.py:25
  186.3 2.8 %copy-start.2 = (bf16[2,2,384,2048]{3,2,1,0:T(8,128)(2,1)S(1)}, bf16[2,2,384,2048]{3,2,1,0:T(8,128)(2,1)}, u32[]{:S(2)}) copy-start(bf16[2,2,384,2048]{3,2,1,0:T(8,128)(2,1)} %get-tuple-element.43.turned_ref) | copy-start | bytes 18874372
  236.3 12.4 %all-to-all-start.8 = ((bf16[8,16,512]{2,1,0:T(8,128)(2,1)}), bf16[8,16,512]{2,1,0:T(8,128)(2,1)S(1)}, u32[]{:S(2)}, u32[]{:S(2)}) async-start(bf16[8,16,512]{2,1,0:T(8,128)(2,1)} %shard_map.75), calls=%async_computation.9 | async-start | bytes 262144 | tf_op jit(solution)/shard_map/all_to_all | solution.py:25
Sparse Core Ops, SparseCore 0:
  29.9 41.5 all-gather.2
  76.8 76.3 reduce-scatter.1
